TPU v7x, 32 devices: a whole 2x2x4 slice. The times are simulated.
32 devices in a mesh: narrow: 2 (over x), wide: 16 (over z, y, core).
Axes of the slice: x: 2, y: 2, z: 4, core: 2. Of those that a mesh axis runs over, the one named last changes fastest.
Arguments:
- momentum: float32 [4096, 28672], P('narrow', 'wide'), may hold values from -6 to 6
- gradient: bfloat16 [4096, 28672], P('narrow', 'wide'), may hold values from -6 to 6
- right_basis: float32 [28672, 256], P('wide'), may hold values from -0.03125 to 0.03125
- signs: int32 [4096], replicated, may hold values from -1 to 1, as said below
- select: int32 [384], replicated, may hold values from 0 to 4095, as said below
Outputs:
- momentum_out: float32 [4096, 28672], P('narrow', 'wide')
- basis_out: float32 [28672, 256], P('wide')
- update: bfloat16 [4096, 28672], P('narrow', 'wide')
Inputs may be any that keep to these rules, and one draw needn't show every extreme that they name: `signs`: each entry is -1 or 1. `select`: 384 distinct row numbers.
All inputs are finite; a program needn't handle non-finite values.
Results may differ from a plain program's by a relative error of at most 0.001.
Values sent between devices are 32-bit elements; how exact they have to be, the bound alone decides.
No kernel may reach another device: no remote copies, remote signals or barrier semaphores. Data moves between devices by JAX's collectives and lax.ppermute only.
A program may use at most 128 MiB of HBM per device.

v0:
```python
import math

import jax
import jax.numpy as jnp
from jax import lax
from jax.sharding import PartitionSpec as P

ROWS = 4096
COLS = 28672
RANK = 256
SKETCH = 384


decay_mu = 0.95
norm_epsilon = 1e-06


def hadamard_rows(select, sign_part, first_row, row_count):
    columns = first_row + jnp.arange(row_count, dtype=jnp.int32)
    shared_bits = jnp.bitwise_and(select[:, None], columns[None, :])
    parity = jnp.zeros(shared_bits.shape, jnp.int32)
    for bit_index in range(ROWS.bit_length()):
        parity = jnp.bitwise_xor(
            parity, jnp.bitwise_and(jnp.right_shift(shared_bits, bit_index), 1)
        )
    entries = (1 - 2 * parity).astype(jnp.float32) * sign_part.astype(jnp.float32)[None, :]
    return entries / math.sqrt(SKETCH)


def sketch_term(select, signs, first_row, row_values):
    row_count = row_values.shape[0]
    sign_part = lax.dynamic_slice_in_dim(signs, first_row, row_count)
    hadamard = hadamard_rows(select, sign_part, first_row, row_count)
    return jnp.dot(
        hadamard, row_values, precision=lax.Precision.HIGHEST, preferred_element_type=jnp.float32
    )


def orthonormal(sketch, row_values):
    gram = jnp.dot(
        sketch.T, sketch, precision=lax.Precision.HIGHEST, preferred_element_type=jnp.float32
    )
    lower_factor = jnp.linalg.cholesky(gram)
    return jax.scipy.linalg.solve_triangular(lower_factor, row_values.T, lower=True).T


def per_device(momentum, gradient, right_basis, signs, select):
    high = lax.Precision.HIGHEST
    summed = momentum + gradient.astype(jnp.float32)
    block_rows = summed.shape[0]
    narrow_index = lax.axis_index("narrow")
    block_start = narrow_index * block_rows
    partial_left = jnp.dot(summed, right_basis, precision=high, preferred_element_type=jnp.float32)
    row_block = lax.psum(partial_left, "wide")
    sketch = lax.psum(sketch_term(select, signs, block_start, row_block), "narrow")
    left_full = orthonormal(sketch, row_block)
    right_share = lax.psum_scatter(
        lax.dot_general(
            summed,
            left_full,
            (((0,), (0,)), ((), ())),
            precision=high,
            preferred_element_type=jnp.float32,
        ),
        "narrow",
        scatter_dimension=0,
        tiled=True,
    )
    squares = jnp.sum(right_share * right_share, axis=0)
    norms = jnp.sqrt(lax.psum(squares, ("narrow", "wide")) + norm_epsilon)
    normalized = right_share / norms[None, :]
    basis_out = lax.all_gather(normalized, "narrow", axis=0, tiled=True)
    right_full = basis_out * norms[None, :]
    momentum_out = summed - (1.0 - decay_mu) * jnp.dot(
        left_full, right_full.T, precision=high, preferred_element_type=jnp.float32
    )
    scale_factor = math.sqrt(ROWS * COLS / RANK)
    update = (
        scale_factor
        * jnp.dot(left_full, basis_out.T, precision=high, preferred_element_type=jnp.float32)
    ).astype(jnp.bfloat16)
    return (momentum_out, basis_out, update)


def solution(mesh):
    in_specs = (P("narrow", "wide"), P("narrow", "wide"), P("wide", None), P(), P())
    out_specs = (P("narrow", "wide"), P("wide", None), P("narrow", "wide"))
    return jax.shard_map(
        per_device, mesh=mesh, in_specs=in_specs, out_specs=out_specs, check_vma=False
    )
```

profile of v0, /device:TPU:0, one launch (start us, length us, event | category | flops | bytes accessed | tf_op | source)
XLA Modules:
  0.0 426.5 jit_solution(3474336650434042202)
XLA Ops:
  7.2 0.0 copy-start
  7.2 0.0 copy-start.4
  7.2 0.0 copy-start.5
  7.2 0.0 all-reduce.4.cloned.1.call-start
  7.2 1.4 copy-done
  8.7 17.0 %fusion.1 = f32[2048,256]{1,0:T(8,128)} fusion(f32[1792,256]{1,0:T(8,128)S(1)} %copy-done, f32[2048,1792]{1,0:T(8,128)} %param.5, bf16[2048,1792]{1,0:T(8,128)(2,1)} %param.6), kind=kOutput, calls=%fused_computation.19 | convolution fusion | flops 11281629184 | bytes 25952256 | tf_op jit(solution)/shard_map/dot_general | solution.py:53
  25.6 0.0 all-reduce.4.cloned.1.call-update
  25.7 0.3 all-reduce.6.cloned.1.call-start
  26.0 0.0 copy-done.4
  26.1 100.3 %all-reduce.4.cloned.1.call-done = f32[2048,256]{1,0:T(8,128)} async-done(((f32[2048,256]{1,0:T(8,128)}), f32[2048,256]{1,0:T(8,128)}) %all-reduce.4.cloned.1.call-update) | async-done | bytes 2097168 | tf_op jit(solution)/shard_map/psum | solution.py:54
  126.3 0.0 copy-done.5
  126.3 9.3 %fusion.32 = f32[384,256]{1,0:T(8,128)} fusion(f32[2048,256]{1,0:T(8,128)} %all-reduce.4.cloned.1.call-done, f32[2048]{0:T(1024)S(1)} %get-tuple-element.27, s32[2048]{0:T(1024)S(1)} %get-tuple-element.28, s32[384]{0:T(512)S(1)} %copy-done.5), kind=kOutput, calls=%fused_computation.50 | convolution fusion | flops 2450522112 | bytes 2508288 | tf_op jit(solution)/shard_map/dot_general | solution.py:34
  135.7 0.0 all-reduce.6.cloned.1.call-update
  135.7 0.6 reduce-scatter.2.cloned.1.call-start
  136.3 24.5 %all-reduce.6.cloned.1.call-done = f32[384,256]{1,0:T(8,128)} async-done(((f32[384,256]{1,0:T(8,128)}), f32[384,256]{1,0:T(8,128)}) %all-reduce.6.cloned.1.call-update) | async-done | bytes 393232 | tf_op jit(solution)/shard_map/psum | solution.py:55
  160.8 1.9 fusion.79
  162.8 0.1 copy.8
  163.0 11.7 %cholesky.50 = f32[128,128]{1,0:T(8,128)S(1)} custom-call(f32[128,128]{1,0:T(8,128)S(1)} %cholesky.118), custom_call_target="Cholesky" | custom-call | tf_op jit(solution)/shard_map/jit(cholesky)/cholesky | solution.py:43
  174.7 9.8 %custom-call.15 = f32[1,128,128]{1,2,0:T(8,128)S(1)} custom-call(f32[1,128,128]{2,1,0:T(8,128)S(1)} %get-tuple-element.24), custom_call_target="InvertDiagBlocksLowerTriangular" | custom-call | tf_op jit(solution)/shard_map/jit(cholesky)/cholesky | solution.py:43
  184.5 0.2 constant_dynamic-update-slice_fusion.1
  184.8 0.3 convolution_subtract_fusion.1
  185.0 11.7 %cholesky.105 = f32[128,128]{1,0:T(8,128)S(1)} custom-call(f32[128,128]{1,0:T(8,128)S(1)} %convolution_subtract_fusion.1), custom_call_target="Cholesky" | custom-call | tf_op jit(solution)/shard_map/jit(cholesky)/cholesky | solution.py:43
  196.8 0.6 compare_reduce_fusion
  197.4 0.6 compare_reduce_fusion.1
  199.4 0.1 triangular_solve.57
  199.5 4.2 while.1
  199.6 0.6 fusion.90
  200.2 1.4 bitcast_dynamic-update-slice_fusion.2
  201.6 0.6 fusion.90
  202.2 1.4 bitcast_dynamic-update-slice_fusion.2
  203.6 19.7 %custom-call.16 = f32[2,128,128]{1,2,0:T(8,128)S(1)} custom-call(f32[2,128,128]{2,1,0:T(8,128)S(1)} %get-tuple-element.10), custom_call_target="InvertDiagBlocksLowerTriangular" | custom-call | tf_op jit(solution)/shard_map/jit(_solve_triangular)/triangular_solve | solution.py:44
  223.3 2.3 fusion.52
  225.6 3.0 convolution_subtract_fusion
  228.6 1.1 fusion.57
  229.7 0.0 copy-start.1
  229.7 1.0 copy-done.1
  230.7 28.2 %fusion = f32[1792,256]{1,0:T(8,128)} fusion(f32[2048,1792]{1,0:T(8,128)} %param.5, bf16[2048,1792]{1,0:T(8,128)(2,1)} %param.6, f32[128,2048]{1,0:T(8,128)S(1)} %fusion.57, f32[128,2048]{1,0:T(8,128)S(1)} %fusion.52), kind=kOutput, calls=%fused_computation.18 | convolution fusion | flops 11282153472 | bytes 25952256 | tf_op jit(solution)/shard_map/dot_general | solution.py:58
  258.9 0.0 reduce-scatter.2.cloned.1.call-update
  258.9 0.0 all-gather.2.cloned.1.call-start
  259.0 29.1 %reduce-scatter.2.cloned.1.call-done = f32[896,256]{1,0:T(8,128)} async-done(((f32[1792,256]{1,0:T(8,128)}), f32[896,256]{1,0:T(8,128)}) %reduce-scatter.2.cloned.1.call-update) | async-done | bytes 917520 | tf_op jit(solution)/shard_map/reduce_scatter | solution.py:57
  288.1 1.3 multiply_reduce_fusion
  289.4 39.3 %psum.23 = f32[256]{0:T(256)S(1)} all-reduce(f32[256]{0:T(256)S(1)} %multiply_reduce_fusion), channel_id=1, replica_groups=mesh['narrow'=2,'wide'=16] {'narrow','wide'}, use_global_device_ids=true, to_apply=%region_8.9 | all-reduce | flops 256 | bytes 2048 | tf_op jit(solution)/shard_map/psum | solution.py:70
  328.7 2.2 broadcast_divide_fusion
  330.9 0.0 all-gather.2.cloned.1.call-update
  330.9 31.1 %all-gather.2.cloned.1.call-done = f32[1792,256]{1,0:T(8,128)} async-done(((f32[896,256]{1,0:T(8,128)}), f32[1792,256]{1,0:T(8,128)}) %all-gather.2.cloned.1.call-update) | async-done | bytes 1835024 | tf_op jit(solution)/shard_map/all_gather | solution.py:72
  362.0 0.0 copy-start.2
  362.0 0.0 copy-start.3
  362.0 27.3 %multiply_convert_fusion = bf16[2048,1792]{1,0:T(8,128)(2,1)} fusion(f32[1792,256]{1,0:T(8,128)} %all-gather.2.cloned.1.call-done, f32[128,2048]{1,0:T(8,128)} %copy-done.1, f32[128,2048]{1,0:T(8,128)S(1)} %fusion.52), kind=kOutput, calls=%fused_computation.15 | convolution fusion | flops 11282153472 | bytes 11272192 | tf_op jit(solution)/shard_map/dot_general | solution.py:80
  389.3 0.0 copy-done.2
  389.3 0.0 copy-done.3
  389.3 29.2 %multiply_subtract_fusion = f32[2048,1792]{1,0:T(8,128)} fusion(f32[2048,1792]{1,0:T(8,128)} %param.5, bf16[2048,1792]{1,0:T(8,128)(2,1)} %param.6, f32[1792,256]{1,0:T(8,128)S(1)} %copy-done.3, f32[128,2048]{1,0:T(8,128)S(1)} %copy-done.2, f32[128,2048]{1,0:T(8,128)S(1)} %fusion.52, f32[256]{0:T(256)S(1)} %add_sqrt_fusion), kind=kOutput, calls=%fused_computation.16 | convolution fusion | flops 11289952256 | bytes 40633344 | tf_op jit(solution)/shard_map/dot_general | solution.py:74
  418.5 1.2 copy.23
  (12 shorter events, 0.2 us)
Async XLA Ops:
  7.2 1.5 copy-start
  7.2 18.8 %copy-start.4 = (s32[4096]{0:T(1024)S(1)}, s32[4096]{0:T(1024)}, u32[]{:S(2)}) copy-start(s32[4096]{0:T(1024)} %param.8) | copy-start | bytes 49156
  7.2 119.1 %copy-start.5 = (s32[384]{0:T(512)S(1)}, s32[384]{0:T(512)}, u32[]{:S(2)}) copy-start(s32[384]{0:T(512)} %param.9) | copy-start | bytes 4612
  7.2 119.1 %all-reduce.4.cloned.1.call-start = ((), (), s32[]{:S(2)}) async-start(), calls=%async_computation.1 | async-start | bytes 4194304 | tf_op jit(solution)/shard_map/psum | solution.py:54
  25.7 135.1 %all-reduce.6.cloned.1.call-start = ((), (), s32[]{:S(2)}) async-start(), calls=%async_computation.2 | async-start | bytes 786432 | tf_op jit(solution)/shard_map/psum | solution.py:55
  135.7 152.4 %reduce-scatter.2.cloned.1.call-start = ((), (), s32[]{:S(2)}) async-start(), calls=%async_computation.3 | async-start | bytes 2752512 | tf_op jit(solution)/shard_map/reduce_scatter | solution.py:57
  229.7 1.0 copy-start.1
  258.9 103.0 %all-gather.2.cloned.1.call-start = ((), (), s32[]{:S(2)}) async-start(), calls=%async_computation.4 | async-start | bytes 2752512 | tf_op jit(solution)/shard_map/all_gather | solution.py:72
  362.0 27.3 %copy-start.2 = (f32[128,2048]{1,0:T(8,128)S(1)}, f32[128,2048]{1,0:T(8,128)}, u32[]{:S(2)}) copy-start(f32[128,2048]{1,0:T(8,128)} %copy-done.1) | copy-start | bytes 3145732
  362.0 27.3 %copy-start.3 = (f32[1792,256]{1,0:T(8,128)S(1)}, f32[1792,256]{1,0:T(8,128)}, u32[]{:S(2)}) copy-start(f32[1792,256]{1,0:T(8,128)} %all-gather.2.cloned.1.call-done) | copy-start | bytes 5505028
Sparse Core Ops, SparseCore 0:
  25.8 100.4 all-reduce.3
  135.8 24.9 all-reduce.5
  259.1 28.9 reduce-scatter.1
  331.0 30.8 all-gather.1
where the time goes:
time: 432 us; the launch traced here: 426 us
  waiting for transfers between devices  185 us (43%)
  matrix products  120 us (28%)
  other arithmetic  57.8 us (13%)
  blocking collectives  39.3 us (9%)
  between operations  15.4 us (4%)
  local copies, waits for them, and re-layouts  7.82 us (2%)
    psum x1, waiting for transfers between devices, per_device(): row_block = lax.psum(partial_left, 'wide')  100 us
    psum x1, blocking collectives, per_device(): norms = jnp.sqrt(lax.psum(squares, ('narrow', 'wide')) + norm_epsilon)  39.3 us
    another operation x7, other arithmetic, orthonormal(): lower_factor = jnp.linalg.cholesky(gram)  34.6 us
    all_gather x1, waiting for transfers between devices, per_device(): basis_out = lax.all_gather(normalized, 'narrow', axis=0, tiled=True)  31.1 us
    dot_general x1, matrix products, per_device(): jnp.dot(left_full, right_full.T, precision=high, preferred_element_type=j...  29.2 us
    reduce_scatter x1, waiting for transfers between devices, per_device(): lax.psum_scatter(lax.dot_general(summed, left_full, (((0,), (0,)), ((), (...  29.1 us
    dot_general x1, matrix products, per_device(): lax.dot_general(summed, left_full, (((0,), (0,)), ((), ())), precision=hi...  28.2 us
    dot_general x1, matrix products, per_device(): jnp.dot(left_full, basis_out.T, precision=high, preferred_element_type=jn...  27.3 us
  transfers between devices with their start and end apart: 4, of which 4 were waited for; matrix products, arithmetic and copies ran while one was open for 0% of the time, Pallas kernels for 0%

commit v1 on v0

v1 whole, which is shorter than its diff:
```python
import functools
import math

import jax
import jax.numpy as jnp
from jax import lax
from jax.experimental import pallas as pl
from jax.experimental.pallas import tpu as pltpu
from jax.sharding import PartitionSpec as P

decay_mu = 0.95
norm_epsilon = 1e-06

F32 = jnp.float32
BF16 = jnp.bfloat16
HIGH = lax.Precision.HIGHEST
MIB = 1024 * 1024


def split2(x):
    hi = x.astype(BF16)
    return hi, (x - hi.astype(F32)).astype(BF16)


def dot(a, b):
    return jnp.dot(a, b, preferred_element_type=F32)


def params(mib):
    return pltpu.CompilerParams(
        vmem_limit_bytes=mib * MIB, dimension_semantics=("arbitrary",)
    )


def cost(flops, bytes_accessed):
    return pl.CostEstimate(
        flops=int(flops), bytes_accessed=int(bytes_accessed), transcendentals=0
    )


def left_kernel(
    blocks,
    info,
    m_ref,
    g_ref,
    b_ref,
    signs_ref,
    select_ref,
    shi_ref,
    slo_ref,
    send1_ref,
    keep1_ref,
    send2_ref,
    keep2_ref,
    skend_ref,
    skkeep_ref,
    bhi,
    blo,
    lt,
    sketch,
):
    step = pl.program_id(0)
    beta = info[0]
    tile = m_ref.shape[0]
    rank = b_ref.shape[1]
    chunk = rank // 2
    groups = chunk // 8

    @pl.when(step == 0)
    def _():
        hi, lo = split2(b_ref[...])
        bhi[...] = hi
        blo[...] = lo
        sketch[...] = jnp.zeros_like(sketch)

    hi, lo = split2(m_ref[...] + g_ref[...].astype(F32))
    shi_ref[...] = hi
    slo_ref[...] = lo
    left = dot(hi, bhi[...]) + (dot(lo, bhi[...]) + dot(hi, blo[...]))
    lt[...] = left.T
    for c, (keep, send) in enumerate(((keep1_ref, send1_ref), (keep2_ref, send2_ref))):
        for p in range(groups):
            start = pl.multiple_of(c * chunk + 8 * (beta ^ p), 8)
            rows = lt[pl.ds(start, 8), :]
            if p < groups // 2:
                keep[8 * p : 8 * p + 8, :] = rows
            else:
                q = p - groups // 2
                send[8 * q : 8 * q + 8, :] = rows

    sketch_rows = select_ref.shape[0]
    column = info[1] + step * tile + lax.broadcasted_iota(jnp.int32, (1, tile), 1)
    bits = jnp.bitwise_and(select_ref[...], column)
    for shift in (8, 4, 2, 1):
        bits = jnp.bitwise_xor(bits, jnp.right_shift(bits, shift))
    bits = jnp.bitwise_and(bits, 1)
    hadamard = ((1 - 2 * bits) * signs_ref[...]).astype(F32).astype(BF16)
    l0, rest = left.astype(BF16), None
    rest = left - l0.astype(F32)
    l1 = rest.astype(BF16)
    l2 = (rest - l1.astype(F32)).astype(BF16)
    sketch[...] += dot(hadamard, l0) + (dot(hadamard, l1) + dot(hadamard, l2))

    @pl.when(step == blocks - 1)
    def _():
        scale = 1.0 / math.sqrt(sketch_rows)
        share = sketch_rows // groups
        for p in range(groups):
            for i in range(share // 8):
                start = pl.multiple_of(share * (beta ^ p) + 8 * i, 8)
                rows = sketch[pl.ds(start, 8), :] * scale
                if p < groups // 2:
                    skkeep_ref[8 * p : 8 * p + 8, rank * i : rank * i + rank] = rows
                else:
                    q = p - groups // 2
                    skend_ref[8 * q : 8 * q + 8, rank * i : rank * i + rank] = rows


def left_call(info, momentum, gradient, right_basis, signs, select):
    rows, cols = momentum.shape
    rank = right_basis.shape[1]
    sketch_rows = select.shape[0]
    tile = 256
    blocks = rows // tile
    quarter = rank // 4
    wide_sketch = sketch_rows // (rank // 16) // 8 * rank
    part = jax.ShapeDtypeStruct((quarter, rows), F32)
    part_spec = pl.BlockSpec((quarter, tile), lambda i, s: (0, i))
    sk = jax.ShapeDtypeStruct((quarter, wide_sketch), F32)
    sk_spec = pl.BlockSpec((quarter, wide_sketch), lambda i, s: (0, 0))
    row_spec = pl.BlockSpec((tile, cols), lambda i, s: (i, 0))
    return pl.pallas_call(
        functools.partial(left_kernel, blocks),
        grid_spec=pltpu.PrefetchScalarGridSpec(
            num_scalar_prefetch=1,
            grid=(blocks,),
            in_specs=[
                row_spec,
                row_spec,
                pl.BlockSpec((cols, rank), lambda i, s: (0, 0)),
                pl.BlockSpec((1, tile), lambda i, s: (0, s[1] // tile + i)),
                pl.BlockSpec((sketch_rows, 1), lambda i, s: (0, 0)),
            ],
            out_specs=[row_spec, row_spec] + [part_spec] * 4 + [sk_spec] * 2,
            scratch_shapes=[
                pltpu.VMEM((cols, rank), BF16),
                pltpu.VMEM((cols, rank), BF16),
                pltpu.VMEM((rank, tile), F32),
                pltpu.VMEM((sketch_rows, rank), F32),
            ],
        ),
        out_shape=[
            jax.ShapeDtypeStruct((rows, cols), BF16),
            jax.ShapeDtypeStruct((rows, cols), BF16),
            part,
            part,
            part,
            part,
            sk,
            sk,
        ],
        compiler_params=params(40),
        cost_estimate=cost(6 * rows * cols * rank, rows * cols * 10),
        name="left_factor",
    )(info, momentum, gradient, right_basis, signs[None, :], select[:, None])


def right_kernel(a_ref, b_ref, shi_ref, slo_ref, w_ref):
    step = pl.program_id(0)
    left = jnp.concatenate([a_ref[...], b_ref[...]], axis=0)
    hi, lo = split2(left)
    half = left.shape[0]
    both = dot(jnp.concatenate([hi, lo], axis=0), shi_ref[...])
    term = (both[:half] + both[half:]) + dot(hi, slo_ref[...])

    @pl.when(step == 0)
    def _():
        w_ref[...] = term

    @pl.when(step > 0)
    def _():
        w_ref[...] += term


def right_call(first, second, shi, slo):
    rows, cols = shi.shape
    quarter = first.shape[0]
    tile = 256
    part_spec = pl.BlockSpec((quarter, tile), lambda i: (0, i))
    row_spec = pl.BlockSpec((tile, cols), lambda i: (i, 0))
    return pl.pallas_call(
        right_kernel,
        grid=(rows // tile,),
        in_specs=[part_spec, part_spec, row_spec, row_spec],
        out_specs=pl.BlockSpec((2 * quarter, cols), lambda i: (0, 0)),
        out_shape=jax.ShapeDtypeStruct((2 * quarter, cols), F32),
        compiler_params=params(30),
        cost_estimate=cost(12 * rows * cols * quarter, rows * cols * 4),
        name="right_factor",
    )(first, second, shi, slo)


def eliminate(block):
    n = block.shape[0]
    row_id = lax.broadcasted_iota(jnp.int32, (n, n), 0)
    lane_id = lax.broadcasted_iota(jnp.int32, (n, n), 1)
    groups = [block[8 * g : 8 * g + 8, :] for g in range(n // 8)]
    lane = lane_id[:8, :]
    sub = row_id[:8, :]
    for k in range(n):
        g0 = k // 8
        row = groups[g0][k % 8 : k % 8 + 1, :]
        inverse = 1.0 / row[:, k : k + 1]
        scaled = row * inverse
        scaled = jnp.broadcast_to(scaled, (8, n))
        is_pivot = lane == k
        inverse = jnp.broadcast_to(inverse, (8, n))
        for g in range(g0, n // 8):
            x = groups[g]
            col = x[:, k : k + 1]
            if g == g0:
                col = jnp.where(sub[:, :1] > k % 8, col, 0.0)
                keep = jnp.logical_and(is_pivot, sub > k % 8)
            else:
                keep = is_pivot
            groups[g] = jnp.where(keep, -(col * inverse), x - col * scaled)
    full = jnp.concatenate(groups, axis=0)
    diagonal = jnp.sum(jnp.where(row_id == lane_id, full, 0.0), axis=1, keepdims=True)
    unit = jnp.where(row_id > lane_id, full, jnp.where(row_id == lane_id, 1.0, 0.0))
    return unit * lax.rsqrt(diagonal)


def dot_high(a, b, dims=((1,), (0,))):
    return lax.dot_general(
        a, b, (dims, ((), ())), precision=HIGH, preferred_element_type=F32
    )


def factor_kernel(info, *refs):
    parts, (hi_ref, lo_ref) = refs[:-2], refs[-2:]
    gram = None
    for ref in parts:
        term = dot_high(ref[...], ref[...], ((0,), (0,)))
        gram = term if gram is None else gram + term
    rank = gram.shape[0]
    half = rank // 2
    a21 = gram[half:, :half]
    inv11 = eliminate(gram[:half, :half])
    l21 = dot_high(a21, inv11, ((1,), (1,)))
    inv22 = eliminate(gram[half:, half:] - dot_high(l21, l21, ((1,), (1,))))
    inv21 = -dot_high(inv22, dot_high(l21, inv11))
    top = jnp.concatenate([inv11, jnp.zeros_like(inv11)], axis=1)
    inverse = jnp.concatenate([top, jnp.concatenate([inv21, inv22], axis=1)], axis=0)
    source = lax.broadcasted_iota(jnp.int32, (rank, rank), 0)
    target = lax.broadcasted_iota(jnp.int32, (rank, rank), 1)
    order = jnp.where(source == jnp.bitwise_xor(target, 8 * info[0]), 1.0, 0.0)
    hi, lo = split2(dot_high(inverse, order.astype(F32)))
    hi_ref[...] = hi
    lo_ref[...] = lo


def factor_call(info, sk_first, sk_second, rank):
    quarter, lanes = sk_first.shape
    specs = [
        pl.BlockSpec((quarter, rank), functools.partial(lambda j, i, s: (0, j), j))
        for j in range(lanes // rank)
    ]
    out = jax.ShapeDtypeStruct((rank, rank), BF16)
    out_spec = pl.BlockSpec((rank, rank), lambda i, s: (0, 0))
    return pl.pallas_call(
        factor_kernel,
        grid_spec=pltpu.PrefetchScalarGridSpec(
            num_scalar_prefetch=1,
            grid=(1,),
            in_specs=specs + specs,
            out_specs=[out_spec, out_spec],
        ),
        out_shape=[out, out],
        compiler_params=params(30),
        cost_estimate=cost(2e10, 1e6),
        name="factor_inverse",
    )(info, *([sk_first] * len(specs) + [sk_second] * len(specs)))


def basis_kernel(hi_ref, lo_ref, a_ref, b_ref, c_ref, d_ref, lhi_ref, llo_ref):
    raw = jnp.concatenate([a_ref[...], b_ref[...], c_ref[...], d_ref[...]], axis=0)
    hi, lo = split2(raw)
    basis = dot(hi_ref[...], hi) + (dot(hi_ref[...], lo) + dot(lo_ref[...], hi))
    hi, lo = split2(basis.T)
    lhi_ref[...] = hi
    llo_ref[...] = lo


def basis_call(inv, parts):
    quarter, rows = parts[0].shape
    rank = inv[0].shape[0]
    tile = 256
    inv_spec = pl.BlockSpec((rank, rank), lambda i: (0, 0))
    part_spec = pl.BlockSpec((quarter, tile), lambda i: (0, i))
    out_spec = pl.BlockSpec((tile, rank), lambda i: (i, 0))
    out = jax.ShapeDtypeStruct((rows, rank), BF16)
    return pl.pallas_call(
        basis_kernel,
        grid=(rows // tile,),
        in_specs=[inv_spec] * 2 + [part_spec] * 4,
        out_specs=[out_spec] * 2,
        out_shape=[out, out],
        compiler_params=params(20),
        cost_estimate=cost(6 * rows * rank * rank, rows * rank * 8),
        name="left_basis",
    )(*inv, *parts)


def rotate_kernel(hi_ref, lo_ref, *refs):
    parts, (r_ref, rhi_ref, rlo_ref, squares_ref) = refs[:-4], refs[-4:]
    per = len(parts) // 2
    halves = []
    for c in range(2):
        total = parts[c * per][...]
        for ref in parts[c * per + 1 : (c + 1) * per]:
            total = total + ref[...]
        halves.append(total)
    hi, lo = split2(jnp.concatenate(halves, axis=0))
    right = dot(hi_ref[...], hi) + (dot(hi_ref[...], lo) + dot(lo_ref[...], hi))
    r_ref[...] = right
    hi, lo = split2((1.0 - decay_mu) * right)
    rhi_ref[...] = hi
    rlo_ref[...] = lo
    squares = jnp.sum(right * right, axis=1, keepdims=True)
    squares_ref[...] = jnp.broadcast_to(squares, (right.shape[0], 128)).T[:8, :]


def rotate_call(inv, parts):
    half, cols = parts[0].shape
    rank = 2 * half
    return pl.pallas_call(
        rotate_kernel,
        out_shape=[
            jax.ShapeDtypeStruct((rank, cols), F32),
            jax.ShapeDtypeStruct((rank, cols), BF16),
            jax.ShapeDtypeStruct((rank, cols), BF16),
            jax.ShapeDtypeStruct((8, rank), F32),
        ],
        compiler_params=pltpu.CompilerParams(vmem_limit_bytes=40 * MIB),
        cost_estimate=cost(6 * cols * rank * rank, cols * rank * 16),
        name="right_rotate",
    )(*inv, *parts)


def momentum_kernel(shi_ref, slo_ref, lhi_ref, llo_ref, rhi_ref, rlo_ref, out_ref):
    lhi = lhi_ref[...]
    term = dot(lhi, rhi_ref[...]) + (dot(lhi, rlo_ref[...]) + dot(llo_ref[...], rhi_ref[...]))
    out_ref[...] = (shi_ref[...].astype(F32) + slo_ref[...].astype(F32)) - term


def momentum_call(shi, slo, left, right):
    rows, cols = shi.shape
    rank = right[0].shape[0]
    tile = 256
    row_spec = pl.BlockSpec((tile, cols), lambda i: (i, 0))
    left_spec = pl.BlockSpec((tile, rank), lambda i: (i, 0))
    right_spec = pl.BlockSpec((rank, cols), lambda i: (0, 0))
    return pl.pallas_call(
        momentum_kernel,
        grid=(rows // tile,),
        in_specs=[row_spec] * 2 + [left_spec] * 2 + [right_spec] * 2,
        out_specs=row_spec,
        out_shape=jax.ShapeDtypeStruct((rows, cols), F32),
        compiler_params=params(40),
        cost_estimate=cost(6 * rows * cols * rank, rows * cols * 8),
        name="momentum_update",
    )(shi, slo, *left, *right)


def update_kernel(factor, r_ref, squares_ref, lhi_ref, llo_ref, update_ref, basis_ref, bhi, blo):
    @pl.when(pl.program_id(0) == 0)
    def _():
        rank = r_ref.shape[0]
        squares = jnp.broadcast_to(squares_ref[:1, :], (128, rank)).T[:, :1]
        basis = r_ref[...] / jnp.sqrt(squares + norm_epsilon)
        basis_ref[...] = basis.T
        hi, lo = split2(factor * basis)
        bhi[...] = hi
        blo[...] = lo

    lhi = lhi_ref[...]
    term = dot(lhi, bhi[...]) + (dot(lhi, blo[...]) + dot(llo_ref[...], bhi[...]))
    update_ref[...] = term.astype(BF16)


def update_call(factor, right, squares, left):
    rank, cols = right.shape
    rows = left[0].shape[0]
    tile = 256
    left_spec = pl.BlockSpec((tile, rank), lambda i: (i, 0))
    return pl.pallas_call(
        functools.partial(update_kernel, factor),
        grid=(rows // tile,),
        in_specs=[
            pl.BlockSpec((rank, cols), lambda i: (0, 0)),
            pl.BlockSpec((8, rank), lambda i: (0, 0)),
            left_spec,
            left_spec,
        ],
        out_specs=[
            pl.BlockSpec((tile, cols), lambda i: (i, 0)),
            pl.BlockSpec((cols, rank), lambda i: (0, 0)),
        ],
        out_shape=[
            jax.ShapeDtypeStruct((rows, cols), BF16),
            jax.ShapeDtypeStruct((cols, rank), F32),
        ],
        scratch_shapes=[pltpu.VMEM((rank, cols), BF16), pltpu.VMEM((rank, cols), BF16)],
        compiler_params=params(40),
        cost_estimate=cost(6 * rows * cols * rank, rows * cols * 2),
        name="update_basis",
    )(right, squares, *left)


def swap(x, axis, size, bit):
    return lax.ppermute(x, axis, [(i, i ^ bit) for i in range(size)])


def scatter_sum(wide, keep, send):
    got = swap(send, "wide", wide, 1)
    h = keep.shape[0] // 2
    send = keep[h:] + got[h:]
    keep = keep[:h] + got[:h]
    got = swap(send, "wide", wide, 2)
    total = keep + got
    q = h // 4
    mine = total[:q]
    got = [swap(total[q * d : q * d + q], "wide", wide, 4 * d) for d in (1, 2, 3)]
    return mine + (got[0] + got[1] + got[2])


def gather_parts(wide, mine):
    got = [swap(mine, "wide", wide, 4 * d) for d in (1, 2, 3)]
    quad = jnp.concatenate([mine] + got, axis=0)
    half = jnp.concatenate([quad, swap(quad, "wide", wide, 2)], axis=0)
    return half, swap(half, "wide", wide, 1)


def per_device(narrow, wide, whole_rows, whole_cols, momentum, gradient, right_basis, signs, select):
    rows, cols = momentum.shape
    rank = right_basis.shape[1]
    fast = narrow == 2 and wide == 16
    narrow_index = lax.axis_index("narrow")
    index = lax.axis_index("wide")
    if fast:
        core, y, z = index % 2, (index // 2) % 2, index // 4
        beta = 8 * core + 4 * y + z
    else:
        beta = index * 0
    info = jnp.stack([beta, narrow_index * rows]).astype(jnp.int32)
    shi, slo, send1, keep1, send2, keep2, sk_send, sk_keep = left_call(
        info, momentum, gradient, right_basis, signs, select
    )
    if fast:
        mine1 = scatter_sum(wide, keep1, send1)
        first1, second1 = gather_parts(wide, mine1)
        mine_sk = scatter_sum(wide, sk_keep, sk_send)
        mine_sk = mine_sk + swap(mine_sk, "narrow", narrow, 1)
        sk_first, sk_second = gather_parts(wide, mine_sk)
        mine2 = scatter_sum(wide, keep2, send2)
        first2, second2 = gather_parts(wide, mine2)
    else:
        first1, second1, first2, second2 = lax.psum((keep1, send1, keep2, send2), "wide")
        sk_first, sk_second = lax.psum((sk_keep, sk_send), ("narrow", "wide"))
    w1 = right_call(first1, second1, shi, slo)
    w2 = right_call(first2, second2, shi, slo)
    if fast:
        parts = [w1, swap(w1, "narrow", narrow, 1), w2, swap(w2, "narrow", narrow, 1)]
    else:
        parts = list(lax.psum((w1, w2), "narrow"))
    inv = factor_call(info, sk_first, sk_second, rank)
    left = basis_call(inv, [first1, second1, first2, second2])
    right, rhi, rlo, squares = rotate_call(inv, parts)
    if fast:
        for bit in (1, 2, 4, 8):
            squares = squares + swap(squares, "wide", wide, bit)
    else:
        squares = lax.psum(squares, "wide")
    momentum_out = momentum_call(shi, slo, left, (rhi, rlo))
    factor = math.sqrt(whole_rows * whole_cols / rank)
    update, basis_out = update_call(factor, right, squares, left)
    return momentum_out, basis_out, update


def solution(mesh):
    in_specs = (P("narrow", "wide"), P("narrow", "wide"), P("wide", None), P(), P())
    out_specs = (P("narrow", "wide"), P("wide", None), P("narrow", "wide"))
    narrow, wide = mesh.shape["narrow"], mesh.shape["wide"]

    def whole(momentum, *rest):
        body = functools.partial(per_device, narrow, wide, *momentum.shape)
        return jax.shard_map(
            body, mesh=mesh, in_specs=in_specs, out_specs=out_specs, check_vma=False
        )(momentum, *rest)

    return whole
```

time: 432 us -> 177 us (0.41); the launches traced: 426 us -> 176 us
  waiting for transfers between devices: 185 us -> 39.8 us
  matrix products: 120 us -> 0 us
  Pallas kernels: 0 us -> 92.2 us
  other arithmetic: 57.8 us -> 0.42 us
  blocking collectives: 39.3 us -> 0 us
  starting transfers between devices: 1.05 us -> 39.7 us
  between operations: 15.4 us -> 0.94 us
  local copies, waits for them, and re-layouts: 7.82 us -> 3.14 us
    psum x2 -> x0, waiting for transfers between devices: 125 us -> none  [the longest x1 100 us: per_device(): row_block = lax.psum(partial_left, 'wide')]
    dot_general x6 -> x0, matrix products: 113 us -> none  [the longest x1 29.2 us: per_device(): jnp.dot(left_full, right_full.T, precision=high, preferred_element_type=j...]
    pallas_call x0 -> x8, Pallas kernels: none -> 92.2 us  [the longest x1 37.3 us: factor_call(): pl.pallas_call(factor_kernel, grid_spec=pltpu.PrefetchScalarGridSpec(num_...]
    another operation x10 -> x1, other arithmetic: 54.3 us -> 0.08 us  [per_device(): info = jnp.stack([beta, narrow_index * rows]).astype(jnp.int32)]
    ppermute x0 -> x37, waiting for transfers between devices: none -> 39.8 us  [swap(): return lax.ppermute(x, axis, [(i, i ^ bit) for i in range(size)])]
    ppermute x0 -> x37, starting transfers between devices: none -> 39.7 us  [swap(): return lax.ppermute(x, axis, [(i, i ^ bit) for i in range(size)])]
    psum x1 -> x0, blocking collectives: 39.3 us -> none  [per_device(): norms = jnp.sqrt(lax.psum(squares, ('narrow', 'wide')) + norm_epsilon)]
    all_gather x1 -> x0, waiting for transfers between devices: 31.1 us -> none  [per_device(): basis_out = lax.all_gather(normalized, 'narrow', axis=0, tiled=True)]
  transfers between devices with their start and end apart: 4 -> 37, of which waited for: 4 -> 20; matrix products, arithmetic and copies ran while one was open for 0% -> 0% of each run, Pallas kernels for 0% -> 36%
where the time goes in v1:
time: 177 us; the launch traced here: 176 us
  Pallas kernels  92.2 us (52%)
  waiting for transfers between devices  39.8 us (22%)
  starting transfers between devices  39.7 us (22%)
  local copies, waits for them, and re-layouts  3.14 us (2%)
    ppermute x37, waiting for transfers between devices, swap(): return lax.ppermute(x, axis, [(i, i ^ bit) for i in range(size)])  39.8 us
    ppermute x37, starting transfers between devices, swap(): return lax.ppermute(x, axis, [(i, i ^ bit) for i in range(size)])  39.7 us
    pallas_call x1, Pallas kernels, factor_call(): pl.pallas_call(factor_kernel, grid_spec=pltpu.PrefetchScalarGridSpec(num_...  37.3 us
    pallas_call x1, Pallas kernels, left_call(): pl.pallas_call(functools.partial(left_kernel, blocks), grid_spec=pltpu.Pr...  17.9 us
    pallas_call x1, Pallas kernels, momentum_call(): pl.pallas_call(momentum_kernel, grid=(rows // tile,), in_specs=[row_spec]...  12.8 us
    pallas_call x2, Pallas kernels, right_call(): pl.pallas_call(right_kernel, grid=(rows // tile,), in_specs=[part_spec, p...  10.7 us
    pallas_call x1, Pallas kernels, update_call(): pl.pallas_call(functools.partial(update_kernel, factor), grid=(rows // ti...  9.31 us
  transfers between devices with their start and end apart: 37, of which 20 were waited for; matrix products, arithmetic and copies ran while one was open for 0% of the time, Pallas kernels for 36%

profile of v1, /device:TPU:0, one launch (start us, length us, event | category | flops | bytes accessed | tf_op | source)
XLA Modules:
  0.0 176.2 jit_solution(14333444042630704642)
XLA Ops:
  0.7 0.8 broadcast_in_dim.8.select_ref
  1.5 0.1 pad_add_fusion.info
  1.6 1.5 copy-done.1
  3.1 0.7 copy-done.2
  3.8 17.9 %left_factor.1 = (bf16[2048,1792]{1,0:T(8,128)(2,1)S(1)}, bf16[2048,1792]{1,0:T(8,128)(2,1)}, f32[64,2048]{1,0:T(8,128)S(1)}, f32[64,2048]{1,0:T(8,128)S(1)}, f3...) custom-call(s32[2]{0:T(128)S(1)} %pad_add_fusion.info, ...), custom_call_target="tpu_custom_call" | custom-call | flops 5637144576 | bytes 36700160 | tf_op jit(solution)/shard_map/left_factor/pallas_call | solution.py:132
  21.6 0.5 collective-permute-start
  22.1 1.1 collective-permute-done
  23.2 3.0 %collective-permute-start.1 = (f32[32,768]{1,0:T(8,128)S(1)}, f32[32,768]{1,0:T(8,128)S(1)}, u32[]{:S(2)}, u32[]{:S(2)}) collective-permute-start(f32[32,768]{1,0:T(8,128)S(1)} %slice_add_fusion.4), channel_id=1, source_target_pairs={{0,2},{1,3},{2,0},{3,1},{4,6},{5,7},{6,4},{7,5},{8,10},{9,11},{10,... | collective-permute-start | bytes 294920 | tf_op jit(solution)/shard_map/ppermute | solution.py:421
  26.1 3.1 %collective-permute-done.1 = f32[32,768]{1,0:T(8,128)S(1)} collective-permute-done((f32[32,768]{1,0:T(8,128)S(1)}, f32[32,768]{1,0:T(8,128)S(1)}, u32[]{:S(2)}, u32[]{:S(2)}) %collective-permute-start.1) | collective-permute-done | bytes 98336 | tf_op jit(solution)/shard_map/ppermute | solution.py:421
  29.3 2.9 %collective-permute-start.3 = (f32[8,768]{1,0:T(8,128)S(1)}, f32[8,768]{1,0:T(8,128)S(1)}, u32[]{:S(2)}, u32[]{:S(2)}) collective-permute-start(f32[8,768]{1,0:T(8,128)S(1)} %get-tuple-element.51), channel_id=1, source_target_pairs={{0,8},{1,9},{2,10},{3,11},{4,12},{5,13},{6,14},{7,15},{8,0},{9,1},... | collective-permute-start | bytes 73736 | tf_op jit(solution)/shard_map/ppermute | solution.py:421
  32.1 1.3 collective-permute-start.4
  33.5 0.2 collective-permute-start.2
  33.7 0.3 collective-permute-done.3
  34.1 3.7 %collective-permute-done.4 = f32[8,768]{1,0:T(8,128)S(1)} collective-permute-done((f32[8,768]{1,0:T(8,128)S(1)}, f32[8,768]{1,0:T(8,128)S(1)}, u32[]{:S(2)}, u32[]{:S(2)}) %collective-permute-start.4) | collective-permute-done | bytes 24608 | tf_op jit(solution)/shard_map/ppermute | solution.py:421
  37.8 1.6 collective-permute-start.5
  39.3 2.3 %collective-permute-done.5 = f32[8,768]{1,0:T(8,128)S(1)} collective-permute-done((f32[8,768]{1,0:T(8,128)S(1)}, f32[8,768]{1,0:T(8,128)S(1)}, u32[]{:S(2)}, u32[]{:S(2)}) %collective-permute-start.5) | collective-permute-done | bytes 24608 | tf_op jit(solution)/shard_map/ppermute | solution.py:421
  41.7 2.0 %collective-permute-start.8 = (f32[8,768]{1,0:T(8,128)S(1)}, f32[8,768]{1,0:T(8,128)S(1)}, u32[]{:S(2)}, u32[]{:S(2)}) collective-permute-start(f32[8,768]{1,0:T(8,128)S(1)} %get-tuple-element.44), channel_id=1, source_target_pairs={{0,12},{1,13},{2,14},{3,15},{4,8},{5,9},{6,10},{7,11},{8,4},{9,5},... | collective-permute-start | bytes 73736 | tf_op jit(solution)/shard_map/ppermute | solution.py:421
  43.7 2.4 %collective-permute-start.6 = (f32[8,768]{1,0:T(8,128)S(1)}, f32[8,768]{1,0:T(8,128)S(1)}, u32[]{:S(2)}, u32[]{:S(2)}) collective-permute-start(f32[8,768]{1,0:T(8,128)S(1)} %get-tuple-element.44), channel_id=1, source_target_pairs={{0,4},{1,5},{2,6},{3,7},{4,0},{5,1},{6,2},{7,3},{8,12},{9,13},{10,... | collective-permute-start | bytes 73736 | tf_op jit(solution)/shard_map/ppermute | solution.py:421
  46.1 1.2 collective-permute-done.8
  47.3 1.1 collective-permute-done.7
  48.5 1.6 collective-permute-start.9
  50.1 0.6 collective-permute-start.12
  50.7 1.6 collective-permute-start.22
  52.3 7.6 %collective-permute-done.12 = f32[32,2048]{1,0:T(8,128)S(1)} collective-permute-done((f32[32,2048]{1,0:T(8,128)S(1)}, f32[32,2048]{1,0:T(8,128)S(1)}, u32[]{:S(2)}, u32[]{:S(2)}) %collective-permute-start.12) | collective-permute-done | bytes 262176 | tf_op jit(solution)/shard_map/ppermute | solution.py:421
  59.9 0.9 collective-permute-start.14
  60.8 1.8 %collective-permute-start.15 = (f32[8,2048]{1,0:T(8,128)S(1)}, f32[8,2048]{1,0:T(8,128)S(1)}, u32[]{:S(2)}, u32[]{:S(2)}) collective-permute-start(f32[8,2048]{1,0:T(8,128)S(1)} %get-tuple-element.49), channel_id=1, source_target_pairs={{0,12},{1,13},{2,14},{3,15},{4,8},{5,9},{6,10},{7,11},{8,4},{9,5},... | collective-permute-start | bytes 196616 | tf_op jit(solution)/shard_map/ppermute | solution.py:421
  62.6 0.9 collective-permute-start.13
  63.6 1.8 %collective-permute-start.24 = (f32[8,2048]{1,0:T(8,128)S(1)}, f32[8,2048]{1,0:T(8,128)S(1)}, u32[]{:S(2)}, u32[]{:S(2)}) collective-permute-start(f32[8,2048]{1,0:T(8,128)S(1)} %get-tuple-element.45), channel_id=1, source_target_pairs={{0,8},{1,9},{2,10},{3,11},{4,12},{5,13},{6,14},{7,15},{8,0},{9,1},... | collective-permute-start | bytes 196616 | tf_op jit(solution)/shard_map/ppermute | solution.py:421
  65.4 2.9 %collective-permute-done.14 = f32[8,2048]{1,0:T(8,128)S(1)} collective-permute-done((f32[8,2048]{1,0:T(8,128)S(1)}, f32[8,2048]{1,0:T(8,128)S(1)}, u32[]{:S(2)}, u32[]{:S(2)}) %collective-permute-start.14) | collective-permute-done | bytes 65568 | tf_op jit(solution)/shard_map/ppermute | solution.py:421
  68.3 1.5 collective-permute-start.25
  69.8 2.3 %collective-permute-start.23 = (f32[8,2048]{1,0:T(8,128)S(1)}, f32[8,2048]{1,0:T(8,128)S(1)}, u32[]{:S(2)}, u32[]{:S(2)}) collective-permute-start(f32[8,2048]{1,0:T(8,128)S(1)} %get-tuple-element.47), channel_id=1, source_target_pairs={{0,4},{1,5},{2,6},{3,7},{4,0},{5,1},{6,2},{7,3},{8,12},{9,13},{10,... | collective-permute-start | bytes 196616 | tf_op jit(solution)/shard_map/ppermute | solution.py:421
  72.1 1.1 collective-permute-start.18
  73.2 0.5 collective-permute-start.17
  73.7 1.3 collective-permute-done.25
  74.9 1.6 collective-permute-start.16
  76.6 1.1 collective-permute-start.28
  77.7 1.2 collective-permute-done.18
  78.9 1.1 collective-permute-start.27
  80.0 0.8 collective-permute-done.17
  80.7 0.3 collective-permute-start.26
  81.1 1.4 collective-permute-start.19
  82.5 0.2 collective-permute-done.28
  82.7 1.7 collective-permute-done.27
  84.5 0.7 collective-permute-done.26
  85.2 1.1 collective-permute-start.29
  86.4 2.9 %collective-permute-done.19 = f32[32,2048]{1,0:T(8,128)S(1)} collective-permute-done((f32[32,2048]{1,0:T(8,128)S(1)}, f32[32,2048]{1,0:T(8,128)S(1)}, u32[]{:S(2)}, u32[]{:S(2)}) %collective-permute-start.19) | collective-permute-done | bytes 262176 | tf_op jit(solution)/shard_map/ppermute | solution.py:421
  89.3 0.1 collective-permute-start.20
  89.4 2.7 %collective-permute-done.29 = f32[32,2048]{1,0:T(8,128)S(1)} collective-permute-done((f32[32,2048]{1,0:T(8,128)S(1)}, f32[32,2048]{1,0:T(8,128)S(1)}, u32[]{:S(2)}, u32[]{:S(2)}) %collective-permute-start.29) | collective-permute-done | bytes 262176 | tf_op jit(solution)/shard_map/ppermute | solution.py:421
  92.1 0.1 collective-permute-start.30
  92.3 0.5 collective-permute-start.10
  92.8 5.3 %right_factor.2.refs_0_ = f32[128,1792]{1,0:T(8,128)S(1)} custom-call(f32[64,2048]{1,0:T(8,128)S(1)} %constant_dynamic-update-slice_fusion.5.a_ref, f32[64,2048]{1,0:T(8,128)S(1)} %collective-permute-done.20.b_ref, bf16[2048,1792]{1,0:T(8,128)(2,1)S(1)} %get-tuple-element.21.shi_ref, bf16[2048,1792]{1,0:T(8,128)(2,1)S(1)} %copy-done), custom_call_target="tpu_custom_call" | custom-call | flops 2818572288 | bytes 14680064 | tf_op jit(solution)/shard_map/right_factor/pallas_call | solution.py:191
  98.1 1.6 collective-permute-start.31
  99.7 5.4 %right_factor.3.refs_2_ = f32[128,1792]{1,0:T(8,128)S(1)} custom-call(f32[64,2048]{1,0:T(8,128)S(1)} %constant_dynamic-update-slice_fusion.10.c_ref.a_ref, f32[64,2048]{1,0:T(8,128)S(1)} %collective-permute-done.30.d_ref.b_ref, bf16[2048,1792]{1,0:T(8,128)(2,1)S(1)} %get-tuple-element.21.shi_ref, bf16[2048,1792]{1,0:T(8,128)(2,1)S(1)} %copy-done), custom_call_target="tpu_custom_call" | custom-call | flops 2818572288 | bytes 14680064 | tf_op jit(solution)/shard_map/right_factor/pallas_call | solution.py:191
  105.1 0.6 collective-permute-start.32
  105.7 37.3 %factor_inverse.1 = (bf16[256,256]{1,0:T(8,128)(2,1)S(1)}, bf16[256,256]{1,0:T(8,128)(2,1)S(1)}) custom-call(s32[2]{0:T(128)S(1)} %pad_add_fusion.info, f32[64,768]{1,0:T(8,128)S(1)} %constant_dynamic-update-slice_fusion.refs_0_.refs_1_.refs_2_, f32[64,768]{1,0:T(8,128)S(1)} %constant_dynamic-update-slice_fusion.refs_0_.refs_1_.refs_2_, ...), custom_call_target="tpu_custom_call" | custom-call | flops 20000000000 | bytes 1000000 | tf_op jit(solution)/shard_map/factor_inverse/pallas_call | solution.py:270
  143.0 1.2 right_rotate.1
  144.3 1.2 collective-permute-done.33
  145.4 0.6 collective-permute-start.34
  146.0 3.1 %collective-permute-done.34 = f32[8,256]{1,0:T(8,128)S(1)} collective-permute-done((f32[8,256]{1,0:T(8,128)S(1)}, f32[8,256]{1,0:T(8,128)S(1)}, u32[]{:S(2)}, u32[]{:S(2)}) %collective-permute-start.34) | collective-permute-done | bytes 8224 | tf_op jit(solution)/shard_map/ppermute | solution.py:421
  149.1 3.0 %left_basis.1 = (bf16[2048,256]{1,0:T(8,128)(2,1)S(1)}, bf16[2048,256]{1,0:T(8,128)(2,1)S(1)}) custom-call(bf16[256,256]{1,0:T(8,128)(2,1)S(1)} %get-tuple-element.25.hi_ref, bf16[256,256]{1,0:T(8,128)(2,1)S(1)} %get-tuple-element.26.lo_ref, f32[64,2048]{1,0:T(8,128)S(1)} %constant_dynamic-update-slice_fusion.5.a_ref, ...), custom_call_target="tpu_custom_call" | custom-call | flops 805306368 | bytes 4194304 | tf_op jit(solution)/shard_map/left_basis/pallas_call | solution.py:302
  152.2 0.6 collective-permute-done.35
  152.8 1.3 collective-permute-start.36
  154.1 12.8 %momentum_update.1 = f32[2048,1792]{1,0:T(8,128)} custom-call(bf16[2048,1792]{1,0:T(8,128)(2,1)S(1)} %get-tuple-element.21.shi_ref, bf16[2048,1792]{1,0:T(8,128)(2,1)} %get-tuple-element.22.slo_ref, bf16[2048,256]{1,0:T(8,128)(2,1)S(1)} %get-tuple-element.31.lhi_ref, bf16[2048,256]{1,0:T(8,128)(2,1)S(1)} %get-tuple-element.32.llo_ref, ...), custom_call_target="tpu_custom_call" | custom-call | flops 5637144576 | bytes 29360128 | tf_op jit(solution)/shard_map/momentum_update/pallas_call | solution.py:363
  166.9 9.3 %update_basis.1 = (bf16[2048,1792]{1,0:T(8,128)(2,1)}, f32[1792,256]{1,0:T(8,128)}) custom-call(f32[256,1792]{1,0:T(8,128)S(1)} %get-tuple-element.35.r_ref, f32[8,256]{1,0:T(8,128)S(1)} %add.110.squares_ref, bf16[2048,256]{1,0:T(8,128)(2,1)S(1)} %get-tuple-element.31.lhi_ref, bf16[2048,256]{1,0:T(8,128)(2,1)S(1)} %get-tuple-element.32.llo_ref), custom_call_target="tpu_custom_call" | custom-call | flops 5637144576 | bytes 7340032 | tf_op jit(solution)/shard_map/update_basis/pallas_call | solution.py:396
  (58 shorter events, 0.6 us)
Async XLA Ops:
  1.6 1.5 copy-start.1
  3.1 0.7 copy-start.2
  21.6 71.2 %copy-start = (bf16[2048,1792]{1,0:T(8,128)(2,1)S(1)}, bf16[2048,1792]{1,0:T(8,128)(2,1)}, u32[]{:S(2)}) copy-start(bf16[2048,1792]{1,0:T(8,128)(2,1)} %get-tuple-element.22.slo_ref) | copy-start | bytes 22020100
  21.6 1.5 collective-permute-start
  23.2 6.0 %collective-permute-start.1 = (f32[32,768]{1,0:T(8,128)S(1)}, f32[32,768]{1,0:T(8,128)S(1)}, u32[]{:S(2)}, u32[]{:S(2)}) collective-permute-start(f32[32,768]{1,0:T(8,128)S(1)} %slice_add_fusion.4), channel_id=1, source_target_pairs={{0,2},{1,3},{2,0},{3,1},{4,6},{5,7},{6,4},{7,5},{8,10},{9,11},{10,... | collective-permute-start | bytes 294920 | tf_op jit(solution)/shard_map/ppermute | solution.py:421
  29.3 4.8 %collective-permute-start.3 = (f32[8,768]{1,0:T(8,128)S(1)}, f32[8,768]{1,0:T(8,128)S(1)}, u32[]{:S(2)}, u32[]{:S(2)}) collective-permute-start(f32[8,768]{1,0:T(8,128)S(1)} %get-tuple-element.51), channel_id=1, source_target_pairs={{0,8},{1,9},{2,10},{3,11},{4,12},{5,13},{6,14},{7,15},{8,0},{9,1},... | collective-permute-start | bytes 73736 | tf_op jit(solution)/shard_map/ppermute | solution.py:421
  32.1 5.6 %collective-permute-start.4 = (f32[8,768]{1,0:T(8,128)S(1)}, f32[8,768]{1,0:T(8,128)S(1)}, u32[]{:S(2)}, u32[]{:S(2)}) collective-permute-start(f32[8,768]{1,0:T(8,128)S(1)} %get-tuple-element.52), channel_id=1, source_target_pairs={{0,12},{1,13},{2,14},{3,15},{4,8},{5,9},{6,10},{7,11},{8,4},{9,5},... | collective-permute-start | bytes 73736 | tf_op jit(solution)/shard_map/ppermute | solution.py:421
  33.5 4.3 %collective-permute-start.2 = (f32[8,768]{1,0:T(8,128)S(1)}, f32[8,768]{1,0:T(8,128)S(1)}, u32[]{:S(2)}, u32[]{:S(2)}) collective-permute-start(f32[8,768]{1,0:T(8,128)S(1)} %get-tuple-element.53), channel_id=1, source_target_pairs={{0,4},{1,5},{2,6},{3,7},{4,0},{5,1},{6,2},{7,3},{8,12},{9,13},{10,... | collective-permute-start | bytes 73736 | tf_op jit(solution)/shard_map/ppermute | solution.py:421
  33.7 16.3 %collective-permute-start.11 = (f32[64,2048]{1,0:T(8,128)S(1)}, f32[64,2048]{1,0:T(8,128)S(1)}, u32[]{:S(2)}, u32[]{:S(2)}) collective-permute-start(f32[64,2048]{1,0:T(8,128)S(1)} %get-tuple-element.28), channel_id=1, source_target_pairs={{0,1},{1,0},{2,3},{3,2},{4,5},{5,4},{6,7},{7,6},{8,9},{9,8},{10,11... | collective-permute-start | bytes 1572872 | tf_op jit(solution)/shard_map/ppermute | solution.py:421
  37.8 3.9 %collective-permute-start.5 = (f32[8,768]{1,0:T(8,128)S(1)}, f32[8,768]{1,0:T(8,128)S(1)}, u32[]{:S(2)}, u32[]{:S(2)}) collective-permute-start(f32[8,768]{1,0:T(8,128)S(1)} %slice_add_fusion.8), channel_id=1, source_target_pairs={{0,16},{16,0},{1,17},{17,1},{2,18},{18,2},{3,19},{19,3},{4,20},{20... | collective-permute-start | bytes 73736 | tf_op jit(solution)/shard_map/ppermute | solution.py:421
  41.7 5.6 %collective-permute-start.8 = (f32[8,768]{1,0:T(8,128)S(1)}, f32[8,768]{1,0:T(8,128)S(1)}, u32[]{:S(2)}, u32[]{:S(2)}) collective-permute-start(f32[8,768]{1,0:T(8,128)S(1)} %get-tuple-element.44), channel_id=1, source_target_pairs={{0,12},{1,13},{2,14},{3,15},{4,8},{5,9},{6,10},{7,11},{8,4},{9,5},... | collective-permute-start | bytes 73736 | tf_op jit(solution)/shard_map/ppermute | solution.py:421
  43.7 4.7 %collective-permute-start.7 = (f32[8,768]{1,0:T(8,128)S(1)}, f32[8,768]{1,0:T(8,128)S(1)}, u32[]{:S(2)}, u32[]{:S(2)}) collective-permute-start(f32[8,768]{1,0:T(8,128)S(1)} %get-tuple-element.44), channel_id=1, source_target_pairs={{0,8},{1,9},{2,10},{3,11},{4,12},{5,13},{6,14},{7,15},{8,0},{9,1},... | collective-permute-start | bytes 73736 | tf_op jit(solution)/shard_map/ppermute | solution.py:421
  43.7 4.7 %collective-permute-start.6 = (f32[8,768]{1,0:T(8,128)S(1)}, f32[8,768]{1,0:T(8,128)S(1)}, u32[]{:S(2)}, u32[]{:S(2)}) collective-permute-start(f32[8,768]{1,0:T(8,128)S(1)} %get-tuple-element.44), channel_id=1, source_target_pairs={{0,4},{1,5},{2,6},{3,7},{4,0},{5,1},{6,2},{7,3},{8,12},{9,13},{10,... | collective-permute-start | bytes 73736 | tf_op jit(solution)/shard_map/ppermute | solution.py:421
  46.1 4.6 %collective-permute-start.21 = (f32[64,2048]{1,0:T(8,128)S(1)}, f32[64,2048]{1,0:T(8,128)S(1)}, u32[]{:S(2)}, u32[]{:S(2)}) collective-permute-start(f32[64,2048]{1,0:T(8,128)S(1)} %get-tuple-element.30), channel_id=1, source_target_pairs={{0,1},{1,0},{2,3},{3,2},{4,5},{5,4},{6,7},{7,6},{8,9},{9,8},{10,11... | collective-permute-start | bytes 1572872 | tf_op jit(solution)/shard_map/ppermute | solution.py:421
  48.5 43.8 %collective-permute-start.9 = (f32[32,768]{1,0:T(8,128)S(1)}, f32[32,768]{1,0:T(8,128)S(1)}, u32[]{:S(2)}, u32[]{:S(2)}) collective-permute-start(f32[32,768]{1,0:T(8,128)S(1)} %pad_maximum_fusion.2), channel_id=1, source_target_pairs={{0,2},{1,3},{2,0},{3,1},{4,6},{5,7},{6,4},{7,5},{8,10},{9,11},{10,... | collective-permute-start | bytes 294920 | tf_op jit(solution)/shard_map/ppermute | solution.py:421
  50.1 9.8 %collective-permute-start.12 = (f32[32,2048]{1,0:T(8,128)S(1)}, f32[32,2048]{1,0:T(8,128)S(1)}, u32[]{:S(2)}, u32[]{:S(2)}) collective-permute-start(f32[32,2048]{1,0:T(8,128)S(1)} %slice_add_fusion.2), channel_id=1, source_target_pairs={{0,2},{1,3},{2,0},{3,1},{4,6},{5,7},{6,4},{7,5},{8,10},{9,11},{10,... | collective-permute-start | bytes 786440 | tf_op jit(solution)/shard_map/ppermute | solution.py:421
  50.7 12.8 %collective-permute-start.22 = (f32[32,2048]{1,0:T(8,128)S(1)}, f32[32,2048]{1,0:T(8,128)S(1)}, u32[]{:S(2)}, u32[]{:S(2)}) collective-permute-start(f32[32,2048]{1,0:T(8,128)S(1)} %slice_add_fusion), channel_id=1, source_target_pairs={{0,2},{1,3},{2,0},{3,1},{4,6},{5,7},{6,4},{7,5},{8,10},{9,11},{10,... | collective-permute-start | bytes 786440 | tf_op jit(solution)/shard_map/ppermute | solution.py:421
  59.9 8.4 %collective-permute-start.14 = (f32[8,2048]{1,0:T(8,128)S(1)}, f32[8,2048]{1,0:T(8,128)S(1)}, u32[]{:S(2)}, u32[]{:S(2)}) collective-permute-start(f32[8,2048]{1,0:T(8,128)S(1)} %get-tuple-element.48), channel_id=1, source_target_pairs={{0,8},{1,9},{2,10},{3,11},{4,12},{5,13},{6,14},{7,15},{8,0},{9,1},... | collective-permute-start | bytes 196616 | tf_op jit(solution)/shard_map/ppermute | solution.py:421
  60.8 9.0 %collective-permute-start.15 = (f32[8,2048]{1,0:T(8,128)S(1)}, f32[8,2048]{1,0:T(8,128)S(1)}, u32[]{:S(2)}, u32[]{:S(2)}) collective-permute-start(f32[8,2048]{1,0:T(8,128)S(1)} %get-tuple-element.49), channel_id=1, source_target_pairs={{0,12},{1,13},{2,14},{3,15},{4,8},{5,9},{6,10},{7,11},{8,4},{9,5},... | collective-permute-start | bytes 196616 | tf_op jit(solution)/shard_map/ppermute | solution.py:421
  62.6 9.5 %collective-permute-start.13 = (f32[8,2048]{1,0:T(8,128)S(1)}, f32[8,2048]{1,0:T(8,128)S(1)}, u32[]{:S(2)}, u32[]{:S(2)}) collective-permute-start(f32[8,2048]{1,0:T(8,128)S(1)} %get-tuple-element.50), channel_id=1, source_target_pairs={{0,4},{1,5},{2,6},{3,7},{4,0},{5,1},{6,2},{7,3},{8,12},{9,13},{10,... | collective-permute-start | bytes 196616 | tf_op jit(solution)/shard_map/ppermute | solution.py:421
  63.6 9.6 %collective-permute-start.24 = (f32[8,2048]{1,0:T(8,128)S(1)}, f32[8,2048]{1,0:T(8,128)S(1)}, u32[]{:S(2)}, u32[]{:S(2)}) collective-permute-start(f32[8,2048]{1,0:T(8,128)S(1)} %get-tuple-element.45), channel_id=1, source_target_pairs={{0,8},{1,9},{2,10},{3,11},{4,12},{5,13},{6,14},{7,15},{8,0},{9,1},... | collective-permute-start | bytes 196616 | tf_op jit(solution)/shard_map/ppermute | solution.py:421
  68.3 6.6 %collective-permute-start.25 = (f32[8,2048]{1,0:T(8,128)S(1)}, f32[8,2048]{1,0:T(8,128)S(1)}, u32[]{:S(2)}, u32[]{:S(2)}) collective-permute-start(f32[8,2048]{1,0:T(8,128)S(1)} %get-tuple-element.46), channel_id=1, source_target_pairs={{0,12},{1,13},{2,14},{3,15},{4,8},{5,9},{6,10},{7,11},{8,4},{9,5},... | collective-permute-start | bytes 196616 | tf_op jit(solution)/shard_map/ppermute | solution.py:421
  69.8 6.8 %collective-permute-start.23 = (f32[8,2048]{1,0:T(8,128)S(1)}, f32[8,2048]{1,0:T(8,128)S(1)}, u32[]{:S(2)}, u32[]{:S(2)}) collective-permute-start(f32[8,2048]{1,0:T(8,128)S(1)} %get-tuple-element.47), channel_id=1, source_target_pairs={{0,4},{1,5},{2,6},{3,7},{4,0},{5,1},{6,2},{7,3},{8,12},{9,13},{10,... | collective-permute-start | bytes 196616 | tf_op jit(solution)/shard_map/ppermute | solution.py:421
  72.1 6.7 %collective-permute-start.18 = (f32[8,2048]{1,0:T(8,128)S(1)}, f32[8,2048]{1,0:T(8,128)S(1)}, u32[]{:S(2)}, u32[]{:S(2)}) collective-permute-start(f32[8,2048]{1,0:T(8,128)S(1)} %get-tuple-element.42), channel_id=1, source_target_pairs={{0,12},{1,13},{2,14},{3,15},{4,8},{5,9},{6,10},{7,11},{8,4},{9,5},... | collective-permute-start | bytes 196616 | tf_op jit(solution)/shard_map/ppermute | solution.py:421
  73.2 7.6 %collective-permute-start.17 = (f32[8,2048]{1,0:T(8,128)S(1)}, f32[8,2048]{1,0:T(8,128)S(1)}, u32[]{:S(2)}, u32[]{:S(2)}) collective-permute-start(f32[8,2048]{1,0:T(8,128)S(1)} %get-tuple-element.42), channel_id=1, source_target_pairs={{0,8},{1,9},{2,10},{3,11},{4,12},{5,13},{6,14},{7,15},{8,0},{9,1},... | collective-permute-start | bytes 196616 | tf_op jit(solution)/shard_map/ppermute | solution.py:421
  74.9 6.2 %collective-permute-start.16 = (f32[8,2048]{1,0:T(8,128)S(1)}, f32[8,2048]{1,0:T(8,128)S(1)}, u32[]{:S(2)}, u32[]{:S(2)}) collective-permute-start(f32[8,2048]{1,0:T(8,128)S(1)} %get-tuple-element.42), channel_id=1, source_target_pairs={{0,4},{1,5},{2,6},{3,7},{4,0},{5,1},{6,2},{7,3},{8,12},{9,13},{10,... | collective-permute-start | bytes 196616 | tf_op jit(solution)/shard_map/ppermute | solution.py:421
  76.6 6.1 %collective-permute-start.28 = (f32[8,2048]{1,0:T(8,128)S(1)}, f32[8,2048]{1,0:T(8,128)S(1)}, u32[]{:S(2)}, u32[]{:S(2)}) collective-permute-start(f32[8,2048]{1,0:T(8,128)S(1)} %get-tuple-element.40), channel_id=1, source_target_pairs={{0,12},{1,13},{2,14},{3,15},{4,8},{5,9},{6,10},{7,11},{8,4},{9,5},... | collective-permute-start | bytes 196616 | tf_op jit(solution)/shard_map/ppermute | solution.py:421
  78.9 5.6 %collective-permute-start.27 = (f32[8,2048]{1,0:T(8,128)S(1)}, f32[8,2048]{1,0:T(8,128)S(1)}, u32[]{:S(2)}, u32[]{:S(2)}) collective-permute-start(f32[8,2048]{1,0:T(8,128)S(1)} %get-tuple-element.40), channel_id=1, source_target_pairs={{0,8},{1,9},{2,10},{3,11},{4,12},{5,13},{6,14},{7,15},{8,0},{9,1},... | collective-permute-start | bytes 196616 | tf_op jit(solution)/shard_map/ppermute | solution.py:421
  80.7 4.4 %collective-permute-start.26 = (f32[8,2048]{1,0:T(8,128)S(1)}, f32[8,2048]{1,0:T(8,128)S(1)}, u32[]{:S(2)}, u32[]{:S(2)}) collective-permute-start(f32[8,2048]{1,0:T(8,128)S(1)} %get-tuple-element.40), channel_id=1, source_target_pairs={{0,4},{1,5},{2,6},{3,7},{4,0},{5,1},{6,2},{7,3},{8,12},{9,13},{10,... | collective-permute-start | bytes 196616 | tf_op jit(solution)/shard_map/ppermute | solution.py:421
  81.1 8.2 %collective-permute-start.19 = (f32[32,2048]{1,0:T(8,128)S(1)}, f32[32,2048]{1,0:T(8,128)S(1)}, u32[]{:S(2)}, u32[]{:S(2)}) collective-permute-start(f32[32,2048]{1,0:T(8,128)S(1)} %pad_maximum_fusion), channel_id=1, source_target_pairs={{0,2},{1,3},{2,0},{3,1},{4,6},{5,7},{6,4},{7,5},{8,10},{9,11},{10,... | collective-permute-start | bytes 786440 | tf_op jit(solution)/shard_map/ppermute | solution.py:421
  85.2 6.9 %collective-permute-start.29 = (f32[32,2048]{1,0:T(8,128)S(1)}, f32[32,2048]{1,0:T(8,128)S(1)}, u32[]{:S(2)}, u32[]{:S(2)}) collective-permute-start(f32[32,2048]{1,0:T(8,128)S(1)} %pad_maximum_fusion.1), channel_id=1, source_target_pairs={{0,2},{1,3},{2,0},{3,1},{4,6},{5,7},{6,4},{7,5},{8,10},{9,11},{10,... | collective-permute-start | bytes 786440 | tf_op jit(solution)/shard_map/ppermute | solution.py:421
  89.3 3.5 %collective-permute-start.20 = (f32[64,2048]{1,0:T(8,128)S(1)}, f32[64,2048]{1,0:T(8,128)S(1)}, u32[]{:S(2)}, u32[]{:S(2)}) collective-permute-start(f32[64,2048]{1,0:T(8,128)S(1)} %constant_dynamic-update-slice_fusion.5.a_ref), channel_id=1, source_target_pairs={{0,1},{1,0},{2,3},{3,2},{4,5},{5,4},{6,7},{7,6},{8,9},{9,8},{10,11... | collective-permute-start | bytes 1572872 | tf_op jit(solution)/shard_map/ppermute | solution.py:421
  92.1 7.6 %collective-permute-start.30 = (f32[64,2048]{1,0:T(8,128)S(1)}, f32[64,2048]{1,0:T(8,128)S(1)}, u32[]{:S(2)}, u32[]{:S(2)}) collective-permute-start(f32[64,2048]{1,0:T(8,128)S(1)} %constant_dynamic-update-slice_fusion.10.c_ref.a_ref), channel_id=1, source_target_pairs={{0,1},{1,0},{2,3},{3,2},{4,5},{5,4},{6,7},{7,6},{8,9},{9,8},{10,11... | collective-permute-start | bytes 1572872 | tf_op jit(solution)/shard_map/ppermute | solution.py:421
  92.3 13.4 %collective-permute-start.10 = (f32[64,768]{1,0:T(8,128)S(1)}, f32[64,768]{1,0:T(8,128)S(1)}, u32[]{:S(2)}, u32[]{:S(2)}) collective-permute-start(f32[64,768]{1,0:T(8,128)S(1)} %constant_dynamic-update-slice_fusion.refs_0_.refs_1_.refs_2_), channel_id=1, source_target_pairs={{0,1},{1,0},{2,3},{3,2},{4,5},{5,4},{6,7},{7,6},{8,9},{9,8},{10,11... | collective-permute-start | bytes 589832 | tf_op jit(solution)/shard_map/ppermute | solution.py:421
  98.1 44.8 %collective-permute-start.31 = (f32[128,1792]{1,0:T(8,128)S(1)}, f32[128,1792]{1,0:T(8,128)S(1)}, u32[]{:S(2)}, u32[]{:S(2)}) collective-permute-start(f32[128,1792]{1,0:T(8,128)S(1)} %right_factor.2.refs_0_), channel_id=1, source_target_pairs={{0,16},{16,0},{1,17},{17,1},{2,18},{18,2},{3,19},{19,3},{4,20},{20... | collective-permute-start | bytes 2752520 | tf_op jit(solution)/shard_map/ppermute | solution.py:421
  105.1 37.9 %collective-permute-start.32 = (f32[128,1792]{1,0:T(8,128)S(1)}, f32[128,1792]{1,0:T(8,128)S(1)}, u32[]{:S(2)}, u32[]{:S(2)}) collective-permute-start(f32[128,1792]{1,0:T(8,128)S(1)} %right_factor.3.refs_2_), channel_id=1, source_target_pairs={{0,16},{16,0},{1,17},{17,1},{2,18},{18,2},{3,19},{19,3},{4,20},{20... | collective-permute-start | bytes 2752520 | tf_op jit(solution)/shard_map/ppermute | solution.py:421
  144.2 1.2 collective-permute-start.33
  145.4 3.7 %collective-permute-start.34 = (f32[8,256]{1,0:T(8,128)S(1)}, f32[8,256]{1,0:T(8,128)S(1)}, u32[]{:S(2)}, u32[]{:S(2)}) collective-permute-start(f32[8,256]{1,0:T(8,128)S(1)} %add.107), channel_id=1, source_target_pairs={{0,2},{1,3},{2,0},{3,1},{4,6},{5,7},{6,4},{7,5},{8,10},{9,11},{10,... | collective-permute-start | bytes 24584 | tf_op jit(solution)/shard_map/ppermute | solution.py:421
  149.1 3.7 %collective-permute-start.35 = (f32[8,256]{1,0:T(8,128)S(1)}, f32[8,256]{1,0:T(8,128)S(1)}, u32[]{:S(2)}, u32[]{:S(2)}) collective-permute-start(f32[8,256]{1,0:T(8,128)S(1)} %add.108), channel_id=1, source_target_pairs={{0,4},{1,5},{2,6},{3,7},{4,0},{5,1},{6,2},{7,3},{8,12},{9,13},{10,... | collective-permute-start | bytes 24584 | tf_op jit(solution)/shard_map/ppermute | solution.py:421
  152.8 14.1 %collective-permute-start.36 = (f32[8,256]{1,0:T(8,128)S(1)}, f32[8,256]{1,0:T(8,128)S(1)}, u32[]{:S(2)}, u32[]{:S(2)}) collective-permute-start(f32[8,256]{1,0:T(8,128)S(1)} %add.109), channel_id=1, source_target_pairs={{0,8},{1,9},{2,10},{3,11},{4,12},{5,13},{6,14},{7,15},{8,0},{9,1},... | collective-permute-start | bytes 24584 | tf_op jit(solution)/shard_map/ppermute | solution.py:421

commit v2 on v0

v2 whole, which is shorter than its diff:
```python
import functools
import math

import jax
import jax.numpy as jnp
from jax import lax
from jax.experimental import pallas as pl
from jax.experimental.pallas import tpu as pltpu
from jax.sharding import PartitionSpec as P

decay_mu = 0.95
norm_epsilon = 1e-06

F32 = jnp.float32
BF16 = jnp.bfloat16
HIGH = lax.Precision.HIGHEST
MIB = 1024 * 1024
WHOLE = pl.BlockSpec(memory_space=pltpu.VMEM)


def split2(x):
    hi = x.astype(BF16)
    return hi, (x - hi.astype(F32)).astype(BF16)


def dot(a, b):
    return jnp.dot(a, b, preferred_element_type=F32)


in_space = pltpu.with_memory_space_constraint


def params(mib):
    return pltpu.CompilerParams(
        vmem_limit_bytes=mib * MIB, dimension_semantics=("arbitrary",)
    )


def cost(flops, bytes_accessed):
    return pl.CostEstimate(
        flops=int(flops), bytes_accessed=int(bytes_accessed), transcendentals=0
    )


TILE = 512
SLOTS = 2


def is_fast(narrow, wide):
    return narrow == 2 and wide == 16


def labels_of(fast):
    if not fast:
        return 0, 4
    index = lax.axis_index("wide")
    core, y, z = index & 1, (index >> 1) & 1, index >> 2
    za = (z >> 1) ^ (z & 1)
    even, odd = 2 * y + za, 4 + 2 * za + y
    return even + core * (odd - even), odd + core * (even - odd)


def left_kernel(
    fast,
    m_hbm,
    g_hbm,
    b_hbm,
    shi_ref,
    slo_ref,
    send_ref,
    keep_ref,
    m_ref,
    g_ref,
    b_ref,
    bhi,
    blo,
    lt,
    sems,
    b_sem,
):
    rows, cols = m_hbm.shape
    rank = b_ref.shape[1]
    block = rank // 8
    tiles = rows // TILE
    labels = labels_of(fast)

    def copies(t):
        source, slot = pl.ds(t * TILE, TILE), pl.ds(t % SLOTS * TILE, TILE)
        return (
            pltpu.make_async_copy(m_hbm.at[source], m_ref.at[slot], sems.at[0, t % SLOTS]),
            pltpu.make_async_copy(g_hbm.at[source], g_ref.at[slot], sems.at[1, t % SLOTS]),
        )

    b_copy = pltpu.make_async_copy(b_hbm, b_ref, b_sem)
    b_copy.start()
    for t in range(min(SLOTS - 1, tiles)):
        for copy in copies(t):
            copy.start()
    b_copy.wait()
    bhi[...], blo[...] = split2(b_ref[...])

    for t in range(tiles):
        for copy in copies(t):
            copy.wait()
        if t + SLOTS - 1 < tiles:
            for copy in copies(t + SLOTS - 1):
                copy.start()
        part, slot = slice(t * TILE, t * TILE + TILE), t % SLOTS * TILE
        slot = slice(slot, slot + TILE)
        hi, lo = split2(m_ref[slot, :] + g_ref[slot, :].astype(F32))
        shi_ref[part, :] = hi
        slo_ref[part, :] = lo
        left = dot(hi, bhi[...]) + (dot(lo, bhi[...]) + dot(hi, blo[...]))
        lt[...] = left.T
        for side, ref in enumerate((keep_ref, send_ref)):
            for q in range(4):
                start = pl.multiple_of(block * (labels[side] ^ q), block)
                ref[block * q : block * q + block, part] = lt[pl.ds(start, block), :]


def left_call(fast, momentum, gradient, right_basis):
    rows, cols = momentum.shape
    rank = right_basis.shape[1]
    part = jax.ShapeDtypeStruct((rank // 2, rows), F32)
    hbm = pl.BlockSpec(memory_space=pltpu.HBM)
    return pl.pallas_call(
        functools.partial(left_kernel, fast),
        in_specs=[hbm] * 3,
        out_specs=[WHOLE] * 4,
        out_shape=[
            pltpu.VMEM((rows, cols), BF16),
            pltpu.VMEM((rows, cols), BF16),
            part,
            part,
        ],
        scratch_shapes=[
            pltpu.VMEM((SLOTS * TILE, cols), F32),
            pltpu.VMEM((SLOTS * TILE, cols), BF16),
            pltpu.VMEM((cols, rank), F32),
            pltpu.VMEM((cols, rank), BF16),
            pltpu.VMEM((cols, rank), BF16),
            pltpu.VMEM((rank, TILE), F32),
            pltpu.SemaphoreType.DMA((2, SLOTS)),
            pltpu.SemaphoreType.DMA,
        ],
        compiler_params=pltpu.CompilerParams(vmem_limit_bytes=24 * MIB),
        cost_estimate=cost(6 * rows * cols * rank, rows * cols * 6),
        name="left_factor",
    )(*(in_space(x, pltpu.HBM) for x in (momentum, gradient, right_basis)))


def sketch_kernel(fast, scale, a_ref, b_ref, select_ref, signs_ref, *refs):
    left_ref, sketch_ref = refs[-2:]
    half, rows = a_ref.shape
    rank = 2 * half
    block = rank // 8
    labels = labels_of(fast)
    for side, ref in enumerate((a_ref, b_ref)):
        for q in range(4):
            start = pl.multiple_of(block * (labels[side] ^ q), block)
            hi, lo = split2(ref[block * q : block * q + block, :])
            left_ref[pl.ds(start, block), :] = hi
            left_ref[pl.ds(pl.multiple_of(rank + start, block), block), :] = lo
    first = pl.multiple_of(lax.axis_index("narrow") * rows, rows)
    column = first + lax.broadcasted_iota(jnp.int32, (1, rows), 1)
    bits = jnp.bitwise_and(select_ref[...], column)
    for shift in (8, 4, 2, 1):
        bits = jnp.bitwise_xor(bits, jnp.right_shift(bits, shift))
    entries = (1 - 2 * jnp.bitwise_and(bits, 1)) * signs_ref[:, pl.ds(first, rows)]
    both = lax.dot_general(
        entries.astype(F32).astype(BF16),
        left_ref[...],
        (((1,), (1,)), ((), ())),
        preferred_element_type=F32,
    )
    sketch_ref[...] = (both[:, :rank] + both[:, rank:]) * scale


def sketch_call(fast, first, second, select, signs, scale, held):
    half, rows = first.shape
    rank = 2 * half
    return pl.pallas_call(
        functools.partial(sketch_kernel, fast, scale),
        in_specs=[WHOLE] * (4 + len(held)),
        out_specs=[WHOLE] * 2,
        out_shape=[
            jax.ShapeDtypeStruct((2 * rank, rows), BF16),
            jax.ShapeDtypeStruct((select.shape[0], rank), F32),
        ],
        compiler_params=pltpu.CompilerParams(vmem_limit_bytes=24 * MIB),
        cost_estimate=cost(4 * select.shape[0] * rank * rows, rows * rank * 8),
        name="sketch_rows",
    )(
        first,
        second,
        select[:, None],
        signs[None, :],
        *(in_space(x, pltpu.VMEM) for x in held),
    )


def right_kernel(first, left_ref, shi_ref, slo_ref, *refs):
    if len(refs) > 1:
        mine_ref, other_ref, w_ref, sketch_ref = refs
        sketch_ref[...] = mine_ref[...] + other_ref[...]
    else:
        (w_ref,) = refs
    rank, cols = w_ref.shape
    for start in range(0, cols, 256):
        stop = min(start + 256, cols)
        source = slice(first + start, first + stop)
        both = dot(left_ref[...], shi_ref[:, source])
        last = dot(left_ref[:rank, :], slo_ref[:, source])
        w_ref[:, start:stop] = (both[:rank] + both[rank:]) + last


def right_call(left, shi, slo, first, stop, *sketches):
    rows = shi.shape[0]
    rank = left.shape[0] // 2
    cols = stop - first
    outs = [jax.ShapeDtypeStruct((rank, cols), F32)]
    if sketches:
        outs.append(jax.ShapeDtypeStruct(sketches[0].shape, F32))
    return pl.pallas_call(
        functools.partial(right_kernel, first),
        in_specs=[WHOLE] * (3 + len(sketches)),
        out_specs=[WHOLE] * len(outs),
        out_shape=outs,
        compiler_params=pltpu.CompilerParams(vmem_limit_bytes=24 * MIB),
        cost_estimate=cost(6 * rows * cols * rank, rows * cols * 4),
        name="right_factor",
    )(left, in_space(shi, pltpu.VMEM), in_space(slo, pltpu.VMEM), *sketches)


def eliminate(block):
    n = block.shape[0]
    groups = [block[8 * g : 8 * g + 8, :] for g in range(n // 8)]
    lane = lax.broadcasted_iota(jnp.int32, (8, n), 1)
    out = []
    for k in range(0, n, 4):
        g0, o = k // 8, k % 8
        rows = [groups[g0][o + j : o + j + 1, :] for j in range(4)]

        def entry(i, j):
            return jnp.broadcast_to(rows[i][:, k + j : k + j + 1], (8, n))

        u = [[entry(i, j) if j >= i else None for j in range(4)] for i in range(4)]
        inv = []
        low = [[None] * 4 for _ in range(4)]
        for i in range(4):
            inv.append(1.0 / u[i][i])
            for r in range(i + 1, 4):
                low[r][i] = u[i][r] * inv[i]
                for j in range(r, 4):
                    u[r][j] = u[r][j] - low[r][i] * u[i][j]
        inside = jnp.logical_and(lane >= k, lane < k + 4)
        q = []
        for i in range(4):
            base = jnp.where(inside, 0.0, jnp.broadcast_to(rows[i], (8, n)))
            base = jnp.where(lane == k + i, 1.0, base)
            for j in range(i):
                base = base - low[i][j] * q[j]
            q.append(base)
            out.append(jnp.where(lane <= k + i, base * lax.rsqrt(u[i][i]), 0.0)[:1])
        for g in range(g0 if o == 0 else g0 + 1, n // 8):
            x = groups[g]
            new = jnp.where(inside, 0.0, x)
            h = []
            for i in range(4):
                c = jnp.broadcast_to(x[:, k + i : k + i + 1], (8, n))
                for j in range(i):
                    c = c - h[j] * u[j][i]
                h.append(c * inv[i])
                new = new - h[i] * q[i]
            groups[g] = new
    return jnp.concatenate(out, axis=0)


def dot_high(a, b, dims=((1,), (0,))):
    return lax.dot_general(
        a, b, (dims, ((), ())), precision=HIGH, preferred_element_type=F32
    )


def factor_kernel(a_ref, b_ref, hi_ref, lo_ref):
    sketch = jnp.concatenate([a_ref[...], b_ref[...]], axis=0)
    gram = dot_high(sketch, sketch, ((0,), (0,)))
    half = gram.shape[0] // 2
    inv11 = eliminate(gram[:half, :half])
    l21 = dot_high(gram[half:, :half], inv11, ((1,), (1,)))
    inv22 = eliminate(gram[half:, half:] - dot_high(l21, l21, ((1,), (1,))))
    inv21 = -dot_high(inv22, dot_high(l21, inv11))
    top = jnp.concatenate([inv11, jnp.zeros_like(inv11)], axis=1)
    inverse = jnp.concatenate([top, jnp.concatenate([inv21, inv22], axis=1)], axis=0)
    hi_ref[...], lo_ref[...] = split2(inverse)


def factor_call(first, second):
    rank = first.shape[1]
    out = jax.ShapeDtypeStruct((rank, rank), BF16)
    return pl.pallas_call(
        factor_kernel,
        in_specs=[WHOLE] * 2,
        out_specs=[WHOLE] * 2,
        out_shape=[out, out],
        compiler_params=pltpu.CompilerParams(vmem_limit_bytes=24 * MIB),
        cost_estimate=cost(1e6, 1e5),
        name="factor_inverse",
    )(first, second)


def basis_kernel(hi_ref, lo_ref, raw_ref, terms_ref, basis_ref):
    rank = hi_ref.shape[0]
    hi, lo = raw_ref[:rank, :], raw_ref[rank:, :]
    basis = dot(hi_ref[...], hi) + (dot(hi_ref[...], lo) + dot(lo_ref[...], hi))
    basis = basis.T
    basis_ref[...] = basis
    hi, lo = split2(basis)
    terms_ref[...] = jnp.concatenate([hi, lo, hi], axis=1)


def basis_call(inv, raw):
    rows = raw.shape[1]
    rank = inv[0].shape[0]
    tile = 256
    inv_spec = pl.BlockSpec((rank, rank), lambda i: (0, 0))
    return pl.pallas_call(
        basis_kernel,
        grid=(rows // tile,),
        in_specs=[inv_spec] * 2 + [pl.BlockSpec((2 * rank, tile), lambda i: (0, i))],
        out_specs=[
            pl.BlockSpec((tile, 3 * rank), lambda i: (i, 0)),
            pl.BlockSpec((tile, rank), lambda i: (i, 0)),
        ],
        out_shape=[
            jax.ShapeDtypeStruct((rows, 3 * rank), BF16),
            jax.ShapeDtypeStruct((rows, rank), F32),
        ],
        compiler_params=params(24),
        cost_estimate=cost(1e6, 1e5),
        name="left_basis",
    )(*inv, raw)


def rotate_kernel(pieces, hi_ref, lo_ref, *refs):
    parts, (turned_ref, terms_ref, squares_ref) = refs[:-3], refs[-3:]
    rank = hi_ref.shape[0]
    squares = jnp.zeros((rank, 1), F32)
    start = 0
    for piece in pieces:
        total = piece[0]
        total = parts[total][...]
        for other in piece[1:]:
            total = total + parts[other][...]
        stop = start + total.shape[1]
        hi, lo = split2(total)
        right = dot(hi_ref[...], hi) + (dot(hi_ref[...], lo) + dot(lo_ref[...], hi))
        turned_ref[start:stop, :] = right.T
        hi, lo = split2((1.0 - decay_mu) * right)
        terms_ref[:rank, start:stop] = hi
        terms_ref[rank : 2 * rank, start:stop] = hi
        terms_ref[2 * rank :, start:stop] = lo
        squares = squares + jnp.sum(right * right, axis=1, keepdims=True)
        start = stop
    squares_ref[...] = jnp.broadcast_to(squares, (rank, 128)).T[:8, :]


def rotate_call(inv, pieces):
    rank = inv[0].shape[0]
    cols = sum(piece[0].shape[1] for piece in pieces)
    flat, places = [], []
    for piece in pieces:
        places.append(tuple(range(len(flat), len(flat) + len(piece))))
        flat.extend(piece)
    return pl.pallas_call(
        functools.partial(rotate_kernel, tuple(places)),
        in_specs=[WHOLE] * (2 + len(flat)),
        out_specs=[WHOLE] * 3,
        out_shape=[
            jax.ShapeDtypeStruct((cols, rank), F32),
            jax.ShapeDtypeStruct((3 * rank, cols), BF16),
            jax.ShapeDtypeStruct((8, rank), F32),
        ],
        compiler_params=pltpu.CompilerParams(vmem_limit_bytes=24 * MIB),
        cost_estimate=cost(6 * cols * rank * rank, cols * rank * 16),
        name="right_rotate",
    )(*inv, *flat)


def momentum_kernel(first, shi_ref, slo_ref, left_ref, terms_ref, *refs):
    out_ref = refs[-1]
    tile = out_ref.shape[0]
    rows = pl.ds(pl.multiple_of((first + pl.program_id(0)) * tile, tile), tile)
    summed = shi_ref[rows, :].astype(F32) + slo_ref[rows, :].astype(F32)
    out_ref[...] = summed - dot(left_ref[rows, :], terms_ref[...])


def momentum_call(part, parts, shi, slo, left, terms, before=None):
    rows, cols = shi.shape
    rank = left.shape[1] // 3
    tile = 256
    count = max(rows // tile // parts, 1)
    first = part * count
    operands = [in_space(shi, pltpu.VMEM), in_space(slo, pltpu.VMEM), left, terms]
    specs = [WHOLE] * 4
    if before is not None:
        operands.append(before)
        specs.append(pl.BlockSpec(memory_space=pl.ANY))
    return pl.pallas_call(
        functools.partial(momentum_kernel, first),
        grid=(count,),
        in_specs=specs,
        out_specs=pl.BlockSpec((tile, cols), lambda i: (first + i, 0)),
        out_shape=jax.ShapeDtypeStruct((rows, cols), F32),
        input_output_aliases={} if before is None else {4: 0},
        compiler_params=params(24),
        cost_estimate=cost(6 * rows * cols * rank // parts, rows * cols * 4 // parts),
        name="momentum_update",
    )(*operands)


def update_kernel(factor, turned_ref, squares_ref, left_ref, terms_ref, update_ref, basis_ref):
    norms = jnp.sqrt(squares_ref[:1, :] + norm_epsilon)
    tile = update_ref.shape[0]
    step = pl.program_id(0)
    rows = pl.ds(pl.multiple_of(step * tile, tile), tile)
    hi, lo = split2(left_ref[rows, :] * (factor / norms))
    scaled = jnp.concatenate([hi, lo, hi], axis=1)
    update_ref[...] = dot(scaled, terms_ref[...]).astype(BF16)
    share = basis_ref.shape[0]
    part = pl.ds(pl.multiple_of(step * share, 8), share)
    basis_ref[...] = turned_ref[part, :] * (1.0 / norms)


def update_call(factor, turned, squares, left, terms):
    cols, rank = turned.shape
    rows = left.shape[0]
    tile = 256
    share = cols // (rows // tile)
    return pl.pallas_call(
        functools.partial(update_kernel, factor / (1.0 - decay_mu)),
        grid=(rows // tile,),
        in_specs=[WHOLE] * 4,
        out_specs=[
            pl.BlockSpec((tile, cols), lambda i: (i, 0)),
            pl.BlockSpec((share, rank), lambda i: (i, 0)),
        ],
        out_shape=[
            jax.ShapeDtypeStruct((rows, cols), BF16),
            jax.ShapeDtypeStruct((cols, rank), F32),
        ],
        compiler_params=params(24),
        cost_estimate=cost(6 * rows * cols * rank, rows * cols * 2),
        name="update_basis",
    )(turned, squares, left, terms)


def swap(x, axis, pairs):
    return lax.ppermute(x, axis, pairs)


def exchanges(wide):
    core, y, za, zb = 1, 2, 4, 12
    steps = ((core, core), (y, za), (za, y), (zb, zb))
    return [[(i, i ^ bits[i % 2]) for i in range(wide)] for bits in steps]


def add_kernel(a_ref, b_ref, *refs):
    refs[-1][...] = a_ref[...] + b_ref[...]


def add_call(a, b, held):
    return pl.pallas_call(
        add_kernel,
        in_specs=[WHOLE] * (2 + len(held)),
        out_specs=WHOLE,
        out_shape=jax.ShapeDtypeStruct(a.shape, a.dtype),
        compiler_params=pltpu.CompilerParams(vmem_limit_bytes=24 * MIB),
        cost_estimate=cost(a.size, 12 * a.size),
        name="add_pieces",
    )(a, b, *(in_space(x, pltpu.VMEM) for x in held))


def join_kernel(a_ref, b_ref, *refs):
    half = a_ref.shape[0]
    refs[-1][:half, :] = a_ref[...]
    refs[-1][half:, :] = b_ref[...]


def join_call(a, b, held):
    rows, cols = a.shape
    return pl.pallas_call(
        join_kernel,
        in_specs=[WHOLE] * (2 + len(held)),
        out_specs=WHOLE,
        out_shape=jax.ShapeDtypeStruct((2 * rows, cols), a.dtype),
        compiler_params=pltpu.CompilerParams(vmem_limit_bytes=24 * MIB),
        cost_estimate=cost(a.size, 16 * a.size),
        name="join_pieces",
    )(a, b, *(in_space(x, pltpu.VMEM) for x in held))


def wide_sum(steps, keep, send, held):
    core, first, second, third = steps
    got = swap(send, "wide", core)
    for pairs in (first, second):
        h = keep.shape[0] // 2
        total = add_call(keep, got, held)
        send, keep = total[h:], total[:h]
        got = swap(send, "wide", pairs)
    mine = add_call(keep, got, held)
    mine = add_call(mine, swap(mine, "wide", third), held)
    for pairs in (second, first):
        mine = join_call(mine, swap(mine, "wide", pairs), held)
    return mine, swap(mine, "wide", core)


def per_device(narrow, wide, whole_rows, whole_cols, momentum, gradient, right_basis, signs, select):
    rows, cols = momentum.shape
    rank = right_basis.shape[1]
    fast = is_fast(narrow, wide)
    index = lax.axis_index("wide")
    steps = exchanges(wide) if fast else None
    across = [(0, 1), (1, 0)]
    shi, slo, send, keep = left_call(fast, momentum, gradient, right_basis)
    sketch_rows = select.shape[0]
    scale = 1.0 / math.sqrt(sketch_rows)
    if fast:
        share = sketch_rows // wide
        mine = lax.dynamic_slice_in_dim(select, index * share, share)
        first, second = wide_sum(steps, keep, send, (shi, slo))
        left, sketch = sketch_call(fast, first, second, mine, signs, scale, (shi, slo))
        other = swap(sketch, "narrow", across)
        cut = cols * 2 // 7
        (right,) = right_call(left, shi, slo, 0, cut)
        pieces = [[right, swap(right, "narrow", across)]]
        right, sketch = right_call(left, shi, slo, cut, cols, sketch, other)
        pieces.append([right, swap(right, "narrow", across)])
        for pairs in reversed(steps[1:]):
            sketch = jnp.concatenate([sketch, swap(sketch, "wide", pairs)], axis=0)
        sketches = (sketch, swap(sketch, "wide", steps[0]))
    else:
        first, second = lax.psum((keep, send), "wide")
        left, sketch = sketch_call(fast, first, second, select, signs, scale, ())
        sketch = lax.psum(sketch, "narrow")
        sketches = (sketch[: sketch_rows // 2], sketch[sketch_rows // 2 :])
        (right,) = right_call(left, shi, slo, 0, cols)
        pieces = [[lax.psum(right, "narrow")]]
    inv = factor_call(*sketches)
    left_terms, basis = basis_call(inv, left)
    left_terms, pieces[-1][-1] = lax.optimization_barrier((left_terms, pieces[-1][-1]))
    turned, right_terms, squares = rotate_call(inv, pieces)
    if fast:
        momentum_out = None
        for part, pairs in enumerate(steps):
            squares = squares + swap(squares, "wide", pairs)
            momentum_out = momentum_call(
                part, len(steps), shi, slo, left_terms, right_terms, momentum_out
            )
    else:
        squares = lax.psum(squares, "wide")
        momentum_out = momentum_call(0, 1, shi, slo, left_terms, right_terms)
    factor = math.sqrt(whole_rows * whole_cols / rank)
    update, basis_out = update_call(factor, turned, squares, basis, right_terms)
    return momentum_out, basis_out, update


def solution(mesh):
    in_specs = (P("narrow", "wide"), P("narrow", "wide"), P("wide", None), P(), P())
    out_specs = (P("narrow", "wide"), P("wide", None), P("narrow", "wide"))
    narrow, wide = mesh.shape["narrow"], mesh.shape["wide"]

    def whole(momentum, *rest):
        body = functools.partial(per_device, narrow, wide, *momentum.shape)
        return jax.shard_map(
            body, mesh=mesh, in_specs=in_specs, out_specs=out_specs, check_vma=False
        )(momentum, *rest)

    return whole
```

time: 432 us -> 152 us (0.35); the launches traced: 426 us -> 152 us
  waiting for transfers between devices: 185 us -> 52.1 us
  matrix products: 120 us -> 0 us
  Pallas kernels: 0 us -> 61.3 us
  other arithmetic: 57.8 us -> 0.03 us
  blocking collectives: 39.3 us -> 0 us
  starting transfers between devices: 1.05 us -> 31.2 us
  between operations: 15.4 us -> 0.9 us
    psum x2 -> x0, waiting for transfers between devices: 125 us -> none  [the longest x1 100 us: per_device(): row_block = lax.psum(partial_left, 'wide')]
    dot_general x6 -> x0, matrix products: 113 us -> none  [the longest x1 29.2 us: per_device(): jnp.dot(left_full, right_full.T, precision=high, preferred_element_type=j...]
    pallas_call x0 -> x18, Pallas kernels: none -> 61.3 us  [the longest x1 15.6 us: left_call(): pl.pallas_call(functools.partial(left_kernel, fast), in_specs=[hbm] * 3,...]
    another operation x10 -> x0, other arithmetic: 54.3 us -> none  [the longest x7 34.6 us: orthonormal(): lower_factor = jnp.linalg.cholesky(gram)]
    ppermute x0 -> x18, waiting for transfers between devices: none -> 52.1 us  [swap(): return lax.ppermute(x, axis, pairs)]
    psum x1 -> x0, blocking collectives: 39.3 us -> none  [per_device(): norms = jnp.sqrt(lax.psum(squares, ('narrow', 'wide')) + norm_epsilon)]
    ppermute x0 -> x18, starting transfers between devices: none -> 31.2 us  [swap(): return lax.ppermute(x, axis, pairs)]
    all_gather x1 -> x0, waiting for transfers between devices: 31.1 us -> none  [per_device(): basis_out = lax.all_gather(normalized, 'narrow', axis=0, tiled=True)]
  transfers between devices with their start and end apart: 4 -> 18, of which waited for: 4 -> 13; matrix products, arithmetic and copies ran while one was open for 0% -> 0% of each run, Pallas kernels for 0% -> 20%
where the time goes in v2:
time: 152 us
  Pallas kernels  61.3 us (40%)
  waiting for transfers between devices  52.1 us (34%)
  starting transfers between devices  31.2 us (21%)
  local copies, waits for them, and re-layouts  6.54 us (4%)
    ppermute x18, waiting for transfers between devices, swap(): return lax.ppermute(x, axis, pairs)  52.1 us
    ppermute x18, starting transfers between devices, swap(): return lax.ppermute(x, axis, pairs)  31.2 us
    pallas_call x1, Pallas kernels, left_call(): pl.pallas_call(functools.partial(left_kernel, fast), in_specs=[hbm] * 3,...  15.6 us
    pallas_call x1, Pallas kernels, factor_call(): pl.pallas_call(factor_kernel, in_specs=[WHOLE] * 2, out_specs=[WHOLE] * 2...  13 us
    pallas_call x4, Pallas kernels, momentum_call(): pl.pallas_call(functools.partial(momentum_kernel, first), grid=(count,),...  12.3 us
    pallas_call x1, Pallas kernels, update_call(): pl.pallas_call(functools.partial(update_kernel, factor / (1.0 - decay_mu)...  8.24 us
    unnamed x25, local copies, waits for them, and re-layouts  6.24 us
    pallas_call x2, Pallas kernels, right_call(): pl.pallas_call(functools.partial(right_kernel, first), in_specs=[WHOLE] *...  6.16 us
  transfers between devices with their start and end apart: 18, of which 13 were waited for; matrix products, arithmetic and copies ran while one was open for 0% of the time, Pallas kernels for 20%

profile of v2, /device:TPU:0, one launch (start us, length us, event | category | flops | bytes accessed | tf_op | source)
XLA Modules:
  0.0 152.0 jit_solution(4847061464219772043)
XLA Ops:
  0.6 0.0 copy-start
  0.6 15.6 %left_factor.1 = (bf16[2048,1792]{1,0:T(8,128)(2,1)S(1)}, bf16[2048,1792]{1,0:T(8,128)(2,1)S(1)}, f32[128,2048]{1,0:T(8,128)S(1)}, f32[128,2048]{1,0:T(8,128)S(1)}) custom-call(f32[2048,1792]{1,0:T(8,128)} %m_hbm.1, bf16[2048,1792]{1,0:T(8,128)(2,1)} %g_hbm.1, f32[1792,256]{1,0:T(8,128)} %b_hbm.1), custom_call_target="tpu_custom_call" | custom-call | flops 5637144576 | bytes 22020096 | tf_op jit(solution)/shard_map/left_factor/pallas_call | solution.py:126
  16.2 0.0 copy-start.2
  16.2 0.0 copy-start.4
  16.2 0.5 collective-permute-start
  16.7 2.3 %collective-permute-done.b_ref = f32[128,2048]{1,0:T(8,128)S(1)} collective-permute-done((f32[128,2048]{1,0:T(8,128)S(1)}, f32[128,2048]{1,0:T(8,128)S(1)}, u32[]{:S(2)}, u32[]{:S(2)}) %collective-permute-start) | collective-permute-done | bytes 1048608 | tf_op jit(solution)/shard_map/ppermute | solution.py:459
  19.0 0.1 add_pieces.4
  19.1 0.1 fusion
  19.2 3.0 %collective-permute-start.1 = (f32[64,2048]{1,0:T(8,128)S(1)}, f32[64,2048]{1,0:T(8,128)S(1)}, u32[]{:S(2)}, u32[]{:S(2)}) collective-permute-start(f32[64,2048]{1,0:T(8,128)S(1)} %get-tuple-element.41), channel_id=1, source_target_pairs={{0,2},{1,5},{2,0},{3,7},{4,6},{5,1},{6,4},{7,3},{8,10},{9,13},{10,... | collective-permute-start | bytes 1572872 | tf_op jit(solution)/shard_map/ppermute | solution.py:459
  22.2 7.2 %collective-permute-done.1.b_ref = f32[64,2048]{1,0:T(8,128)S(1)} collective-permute-done((f32[64,2048]{1,0:T(8,128)S(1)}, f32[64,2048]{1,0:T(8,128)S(1)}, u32[]{:S(2)}, u32[]{:S(2)}) %collective-permute-start.1) | collective-permute-done | bytes 524320 | tf_op jit(solution)/shard_map/ppermute | solution.py:459
  29.4 0.1 add_pieces.5
  29.5 2.1 %collective-permute-start.2 = (f32[32,2048]{1,0:T(8,128)S(1)}, f32[32,2048]{1,0:T(8,128)S(1)}, u32[]{:S(2)}, u32[]{:S(2)}) collective-permute-start(f32[32,2048]{1,0:T(8,128)S(1)} %get-tuple-element.43), channel_id=1, source_target_pairs={{0,4},{1,3},{2,6},{3,1},{4,0},{5,7},{6,2},{7,5},{8,12},{9,11},{10,... | collective-permute-start | bytes 786440 | tf_op jit(solution)/shard_map/ppermute | solution.py:459
  31.6 4.4 %collective-permute-done.2.b_ref = f32[32,2048]{1,0:T(8,128)S(1)} collective-permute-done((f32[32,2048]{1,0:T(8,128)S(1)}, f32[32,2048]{1,0:T(8,128)S(1)}, u32[]{:S(2)}, u32[]{:S(2)}) %collective-permute-start.2) | collective-permute-done | bytes 262176 | tf_op jit(solution)/shard_map/ppermute | solution.py:459
  36.0 4.1 %collective-permute-start.3 = (f32[32,2048]{1,0:T(8,128)S(1)}, f32[32,2048]{1,0:T(8,128)S(1)}, u32[]{:S(2)}, u32[]{:S(2)}) collective-permute-start(f32[32,2048]{1,0:T(8,128)S(1)} %add_pieces.6.a_ref), channel_id=1, source_target_pairs={{0,12},{1,13},{2,14},{3,15},{4,8},{5,9},{6,10},{7,11},{8,4},{9,5},... | collective-permute-start | bytes 786440 | tf_op jit(solution)/shard_map/ppermute | solution.py:459
  40.1 5.0 %collective-permute-done.3.b_ref = f32[32,2048]{1,0:T(8,128)S(1)} collective-permute-done((f32[32,2048]{1,0:T(8,128)S(1)}, f32[32,2048]{1,0:T(8,128)S(1)}, u32[]{:S(2)}, u32[]{:S(2)}) %collective-permute-start.3) | collective-permute-done | bytes 262176 | tf_op jit(solution)/shard_map/ppermute | solution.py:459
  45.1 5.3 %collective-permute-start.4 = (f32[32,2048]{1,0:T(8,128)S(1)}, f32[32,2048]{1,0:T(8,128)S(1)}, u32[]{:S(2)}, u32[]{:S(2)}) collective-permute-start(f32[32,2048]{1,0:T(8,128)S(1)} %add_pieces.7.a_ref), channel_id=1, source_target_pairs={{0,4},{1,3},{2,6},{3,1},{4,0},{5,7},{6,2},{7,5},{8,12},{9,11},{10,... | collective-permute-start | bytes 786440 | tf_op jit(solution)/shard_map/ppermute | solution.py:459
  50.4 4.4 %collective-permute-done.4.b_ref = f32[32,2048]{1,0:T(8,128)S(1)} collective-permute-done((f32[32,2048]{1,0:T(8,128)S(1)}, f32[32,2048]{1,0:T(8,128)S(1)}, u32[]{:S(2)}, u32[]{:S(2)}) %collective-permute-start.4) | collective-permute-done | bytes 262176 | tf_op jit(solution)/shard_map/ppermute | solution.py:459
  54.8 0.0 copy-start.6
  54.8 1.6 %collective-permute-start.5 = (f32[64,2048]{1,0:T(8,128)S(1)}, f32[64,2048]{1,0:T(8,128)S(1)}, u32[]{:S(2)}, u32[]{:S(2)}) collective-permute-start(f32[64,2048]{1,0:T(8,128)S(1)} %join_pieces.2.a_ref), channel_id=1, source_target_pairs={{0,2},{1,5},{2,0},{3,7},{4,6},{5,1},{6,4},{7,3},{8,10},{9,13},{10,... | collective-permute-start | bytes 1572872 | tf_op jit(solution)/shard_map/ppermute | solution.py:459
  56.4 7.7 %collective-permute-done.5.b_ref = f32[64,2048]{1,0:T(8,128)S(1)} collective-permute-done((f32[64,2048]{1,0:T(8,128)S(1)}, f32[64,2048]{1,0:T(8,128)S(1)}, u32[]{:S(2)}, u32[]{:S(2)}) %collective-permute-start.5) | collective-permute-done | bytes 524320 | tf_op jit(solution)/shard_map/ppermute | solution.py:459
  64.1 0.1 join_pieces.3.a_ref
  64.2 0.1 collective-permute-start.6
  64.2 0.1 dynamic-slice_bitcast_fusion
  64.3 0.1 copy.11.select_ref
  64.4 2.5 %collective-permute-done.6.b_ref = f32[128,2048]{1,0:T(8,128)S(1)} collective-permute-done((f32[128,2048]{1,0:T(8,128)S(1)}, f32[128,2048]{1,0:T(8,128)S(1)}, u32[]{:S(2)}, u32[]{:S(2)}) %collective-permute-start.6) | collective-permute-done | bytes 1048608 | tf_op jit(solution)/shard_map/ppermute | solution.py:459
  66.9 3.1 %copy-done.3 = bf16[2048,1792]{1,0:T(8,128)(2,1)S(1)} copy-done((bf16[2048,1792]{1,0:T(8,128)(2,1)S(1)}, bf16[2048,1792]{1,0:T(8,128)(2,1)}, u32[]{:S(2)}) %copy-start.3) | copy-done | bytes 7340056
  70.0 3.1 %copy-done.5 = bf16[2048,1792]{1,0:T(8,128)(2,1)S(1)} copy-done((bf16[2048,1792]{1,0:T(8,128)(2,1)S(1)}, bf16[2048,1792]{1,0:T(8,128)(2,1)}, u32[]{:S(2)}) %copy-start.5) | copy-done | bytes 7340056
  73.1 1.2 sketch_rows.1
  74.2 1.5 %collective-permute-start.7 = (f32[24,256]{1,0:T(8,128)S(1)}, f32[24,256]{1,0:T(8,128)S(1)}, u32[]{:S(2)}, u32[]{:S(2)}) collective-permute-start(f32[24,256]{1,0:T(8,128)S(1)} %get-tuple-element.27.refs_0_), channel_id=1, source_target_pairs={{0,16},{16,0},{1,17},{17,1},{2,18},{18,2},{3,19},{19,3},{4,20},{20... | collective-permute-start | bytes 73736 | tf_op jit(solution)/shard_map/ppermute | solution.py:459
  75.8 2.3 %collective-permute-done.7.refs_1_ = f32[24,256]{1,0:T(8,128)S(1)} collective-permute-done((f32[24,256]{1,0:T(8,128)S(1)}, f32[24,256]{1,0:T(8,128)S(1)}, u32[]{:S(2)}, u32[]{:S(2)}) %collective-permute-start.7) | collective-permute-done | bytes 24608 | tf_op jit(solution)/shard_map/ppermute | solution.py:459
  78.1 4.4 %right_factor.2 = (f32[256,1280]{1,0:T(8,128)S(1)}, f32[24,256]{1,0:T(8,128)S(1)}) custom-call(bf16[512,2048]{1,0:T(8,128)(2,1)S(1)} %get-tuple-element.26.left_ref.raw_ref, bf16[2048,1792]{1,0:T(8,128)(2,1)S(1)} %copy-done.3, bf16[2048,1792]{1,0:T(8,128)(2,1)S(1)} %copy-done.5, f32[24,256]{1,0:T(8,128)S(1)} %get-tuple-element.27.refs_0_, ...), custom_call_target="tpu_custom_call" | custom-call | flops 4026531840 | bytes 10485760 | tf_op jit(solution)/shard_map/right_factor/pallas_call | solution.py:224
  82.5 0.0 slice-start
  82.5 0.0 slice-start.2
  82.5 0.0 slice-start.1
  82.5 0.0 slice-start.3
  82.5 1.6 %collective-permute-start.12 = (f32[256,1280]{1,0:T(8,128)S(1)}, f32[256,1280]{1,0:T(8,128)S(1)}, u32[]{:S(2)}, u32[]{:S(2)}) collective-permute-start(f32[256,1280]{1,0:T(8,128)S(1)} %get-tuple-element.32.refs_2_), channel_id=1, source_target_pairs={{0,16},{16,0},{1,17},{17,1},{2,18},{18,2},{3,19},{19,3},{4,20},{20... | collective-permute-start | bytes 3932168 | tf_op jit(solution)/shard_map/ppermute | solution.py:459
  84.1 1.8 %right_factor.3.refs_0_ = f32[256,512]{1,0:T(8,128)S(1)} custom-call(bf16[512,2048]{1,0:T(8,128)(2,1)S(1)} %get-tuple-element.26.left_ref.raw_ref, bf16[2048,1792]{1,0:T(8,128)(2,1)S(1)} %copy-done.3, bf16[2048,1792]{1,0:T(8,128)(2,1)S(1)} %copy-done.5), custom_call_target="tpu_custom_call" | custom-call | flops 1610612736 | bytes 4194304 | tf_op jit(solution)/shard_map/right_factor/pallas_call | solution.py:224
  85.9 0.6 collective-permute-start.13
  86.5 2.5 %collective-permute-start.8 = (f32[24,256]{1,0:T(8,128)S(1)}, f32[24,256]{1,0:T(8,128)S(1)}, u32[]{:S(2)}, u32[]{:S(2)}) collective-permute-start(f32[24,256]{1,0:T(8,128)S(1)} %get-tuple-element.28), channel_id=1, source_target_pairs={{0,12},{1,13},{2,14},{3,15},{4,8},{5,9},{6,10},{7,11},{8,4},{9,5},... | collective-permute-start | bytes 73736 | tf_op jit(solution)/shard_map/ppermute | solution.py:459
  89.0 3.1 %collective-permute-done.8 = f32[24,256]{1,0:T(8,128)S(1)} collective-permute-done((f32[24,256]{1,0:T(8,128)S(1)}, f32[24,256]{1,0:T(8,128)S(1)}, u32[]{:S(2)}, u32[]{:S(2)}) %collective-permute-start.8) | collective-permute-done | bytes 24608 | tf_op jit(solution)/shard_map/ppermute | solution.py:459
  92.1 0.2 collective-permute-start.9
  92.3 4.4 %collective-permute-done.9 = f32[48,256]{1,0:T(8,128)S(1)} collective-permute-done((f32[48,256]{1,0:T(8,128)S(1)}, f32[48,256]{1,0:T(8,128)S(1)}, u32[]{:S(2)}, u32[]{:S(2)}) %collective-permute-start.9) | collective-permute-done | bytes 49184 | tf_op jit(solution)/shard_map/ppermute | solution.py:459
  96.7 1.6 %collective-permute-start.10 = (f32[96,256]{1,0:T(8,128)S(1)}, f32[96,256]{1,0:T(8,128)S(1)}, u32[]{:S(2)}, u32[]{:S(2)}) collective-permute-start(f32[96,256]{1,0:T(8,128)S(1)} %pad_maximum_fusion), channel_id=1, source_target_pairs={{0,2},{1,5},{2,0},{3,7},{4,6},{5,1},{6,4},{7,3},{8,10},{9,13},{10,... | collective-permute-start | bytes 294920 | tf_op jit(solution)/shard_map/ppermute | solution.py:459
  98.3 3.1 %collective-permute-done.10 = f32[96,256]{1,0:T(8,128)S(1)} collective-permute-done((f32[96,256]{1,0:T(8,128)S(1)}, f32[96,256]{1,0:T(8,128)S(1)}, u32[]{:S(2)}, u32[]{:S(2)}) %collective-permute-start.10) | collective-permute-done | bytes 98336 | tf_op jit(solution)/shard_map/ppermute | solution.py:459
  101.4 0.1 collective-permute-start.11
  101.5 1.4 collective-permute-done.11.b_ref
  102.9 13.0 %factor_inverse.1 = (bf16[256,256]{1,0:T(8,128)(2,1)S(1)}, bf16[256,256]{1,0:T(8,128)(2,1)S(1)}) custom-call(f32[192,256]{1,0:T(8,128)S(1)} %constant_dynamic-update-slice_fusion.a_ref, f32[192,256]{1,0:T(8,128)S(1)} %collective-permute-done.11.b_ref), custom_call_target="tpu_custom_call" | custom-call | flops 1000000 | bytes 100000 | tf_op jit(solution)/shard_map/factor_inverse/pallas_call | solution.py:301
  115.9 3.1 %left_basis.1 = (bf16[2048,768]{1,0:T(8,128)(2,1)S(1)}, f32[2048,256]{1,0:T(8,128)S(1)}) custom-call(bf16[256,256]{1,0:T(8,128)(2,1)S(1)} %get-tuple-element.29.hi_ref, bf16[256,256]{1,0:T(8,128)(2,1)S(1)} %get-tuple-element.30.lo_ref, bf16[512,2048]{1,0:T(8,128)(2,1)S(1)} %get-tuple-element.26.left_ref.raw_ref), custom_call_target="tpu_custom_call" | custom-call | flops 1000000 | bytes 100000 | tf_op jit(solution)/shard_map/left_basis/pallas_call | solution.py:327
  119.1 0.0 collective-permute-done.12.refs_3_
  119.1 4.4 %collective-permute-done.13.refs_1_ = f32[256,512]{1,0:T(8,128)S(1)} collective-permute-done((f32[256,512]{1,0:T(8,128)S(1)}, f32[256,512]{1,0:T(8,128)S(1)}, u32[]{:S(2)}, u32[]{:S(2)}) %collective-permute-start.13) | collective-permute-done | bytes 524320 | tf_op jit(solution)/shard_map/ppermute | solution.py:459
  123.5 1.5 right_rotate.1
  125.0 0.0 collective-permute-start.14
  125.1 3.1 %momentum_update.4.refs_0_ = f32[2048,1792]{1,0:T(8,128)} custom-call(bf16[2048,1792]{1,0:T(8,128)(2,1)S(1)} %bitcast.4, bf16[2048,1792]{1,0:T(8,128)(2,1)S(1)} %bitcast.6, bf16[2048,768]{1,0:T(8,128)(2,1)S(1)} %get-tuple-element.33.left_ref, bf16[768,1792]{1,0:T(8,128)(2,1)S(1)} %get-tuple-element.35.terms_ref), custom_call_target="tpu_custom_call" | custom-call | flops 1409286144 | bytes 3670016 | tf_op jit(solution)/shard_map/momentum_update/pallas_call | solution.py:409
  128.2 0.0 collective-permute-done.14
  128.2 1.5 %collective-permute-start.15 = (f32[8,256]{1,0:T(8,128)S(1)}, f32[8,256]{1,0:T(8,128)S(1)}, u32[]{:S(2)}, u32[]{:S(2)}) collective-permute-start(f32[8,256]{1,0:T(8,128)S(1)} %add.16), channel_id=1, source_target_pairs={{0,2},{1,5},{2,0},{3,7},{4,6},{5,1},{6,4},{7,3},{8,10},{9,13},{10,... | collective-permute-start | bytes 24584 | tf_op jit(solution)/shard_map/ppermute | solution.py:459
  129.7 3.1 %momentum_update.5.refs_0_ = f32[2048,1792]{1,0:T(8,128)} custom-call(bf16[2048,1792]{1,0:T(8,128)(2,1)S(1)} %bitcast.4, bf16[2048,1792]{1,0:T(8,128)(2,1)S(1)} %bitcast.6, bf16[2048,768]{1,0:T(8,128)(2,1)S(1)} %get-tuple-element.33.left_ref, bf16[768,1792]{1,0:T(8,128)(2,1)S(1)} %get-tuple-element.35.terms_ref, ...), custom_call_target="tpu_custom_call", output_to_operand_aliasing={{}: (4, {})} | custom-call | flops 1409286144 | bytes 3670016 | tf_op jit(solution)/shard_map/momentum_update/pallas_call | solution.py:409
  132.8 0.0 collective-permute-done.15
  132.8 2.0 %collective-permute-start.16 = (f32[8,256]{1,0:T(8,128)S(1)}, f32[8,256]{1,0:T(8,128)S(1)}, u32[]{:S(2)}, u32[]{:S(2)}) collective-permute-start(f32[8,256]{1,0:T(8,128)S(1)} %add.17), channel_id=1, source_target_pairs={{0,4},{1,3},{2,6},{3,1},{4,0},{5,7},{6,2},{7,5},{8,12},{9,11},{10,... | collective-permute-start | bytes 24584 | tf_op jit(solution)/shard_map/ppermute | solution.py:459
  134.8 3.1 %momentum_update.6.refs_0_ = f32[2048,1792]{1,0:T(8,128)} custom-call(bf16[2048,1792]{1,0:T(8,128)(2,1)S(1)} %bitcast.4, bf16[2048,1792]{1,0:T(8,128)(2,1)S(1)} %bitcast.6, bf16[2048,768]{1,0:T(8,128)(2,1)S(1)} %get-tuple-element.33.left_ref, bf16[768,1792]{1,0:T(8,128)(2,1)S(1)} %get-tuple-element.35.terms_ref, ...), custom_call_target="tpu_custom_call", output_to_operand_aliasing={{}: (4, {})} | custom-call | flops 1409286144 | bytes 3670016 | tf_op jit(solution)/shard_map/momentum_update/pallas_call | solution.py:409
  137.9 0.0 collective-permute-done.16
  137.9 2.8 %collective-permute-start.17 = (f32[8,256]{1,0:T(8,128)S(1)}, f32[8,256]{1,0:T(8,128)S(1)}, u32[]{:S(2)}, u32[]{:S(2)}) collective-permute-start(f32[8,256]{1,0:T(8,128)S(1)} %add.18), channel_id=1, source_target_pairs={{0,12},{1,13},{2,14},{3,15},{4,8},{5,9},{6,10},{7,11},{8,4},{9,5},... | collective-permute-start | bytes 24584 | tf_op jit(solution)/shard_map/ppermute | solution.py:459
  140.7 3.1 %momentum_update.7 = f32[2048,1792]{1,0:T(8,128)} custom-call(bf16[2048,1792]{1,0:T(8,128)(2,1)S(1)} %bitcast.4, bf16[2048,1792]{1,0:T(8,128)(2,1)S(1)} %bitcast.6, bf16[2048,768]{1,0:T(8,128)(2,1)S(1)} %get-tuple-element.33.left_ref, bf16[768,1792]{1,0:T(8,128)(2,1)S(1)} %get-tuple-element.35.terms_ref, ...), custom_call_target="tpu_custom_call", output_to_operand_aliasing={{}: (4, {})} | custom-call | flops 1409286144 | bytes 3670016 | tf_op jit(solution)/shard_map/momentum_update/pallas_call | solution.py:409
  143.7 0.0 collective-permute-done.17
  143.7 8.2 %update_basis.1 = (bf16[2048,1792]{1,0:T(8,128)(2,1)}, f32[1792,256]{1,0:T(8,128)}) custom-call(f32[1792,256]{1,0:T(8,128)S(1)} %get-tuple-element.36.turned_ref, f32[8,256]{1,0:T(8,128)S(1)} %add.19.squares_ref, f32[2048,256]{1,0:T(8,128)S(1)} %get-tuple-element.38.left_ref, bf16[768,1792]{1,0:T(8,128)(2,1)S(1)} %get-tuple-element.35.terms_ref), custom_call_target="tpu_custom_call" | custom-call | flops 5637144576 | bytes 7340032 | tf_op jit(solution)/shard_map/update_basis/pallas_call | solution.py:440
  (28 shorter events, 0.2 us)
Async XLA Ops:
  0.6 63.6 %copy-start = (s32[384]{0:T(512)S(1)}, s32[384]{0:T(512)}, u32[]{:S(2)}) copy-start(s32[384]{0:T(512)} %param.9) | copy-start | bytes 4612
  16.2 47.9 %copy-start.2 = (bf16[2048,1792]{1,0:T(8,128)(2,1)}, bf16[2048,1792]{1,0:T(8,128)(2,1)S(1)}, u32[]{:S(2)}) copy-start(bf16[2048,1792]{1,0:T(8,128)(2,1)S(1)} %get-tuple-element.22.refs_0_.shi_ref) | copy-start | bytes 22020100
  16.2 47.9 %copy-start.4 = (bf16[2048,1792]{1,0:T(8,128)(2,1)}, bf16[2048,1792]{1,0:T(8,128)(2,1)S(1)}, u32[]{:S(2)}) copy-start(bf16[2048,1792]{1,0:T(8,128)(2,1)S(1)} %get-tuple-element.23.refs_1_.slo_ref) | copy-start | bytes 22020100
  16.2 2.8 %collective-permute-start = (f32[128,2048]{1,0:T(8,128)S(1)}, f32[128,2048]{1,0:T(8,128)S(1)}, u32[]{:S(2)}, u32[]{:S(2)}) collective-permute-start(f32[128,2048]{1,0:T(8,128)S(1)} %get-tuple-element.25), channel_id=1, source_target_pairs={{0,1},{1,0},{2,3},{3,2},{4,5},{5,4},{6,7},{7,6},{8,9},{9,8},{10,11... | collective-permute-start | bytes 3145736 | tf_op jit(solution)/shard_map/ppermute | solution.py:459
  19.2 10.1 %collective-permute-start.1 = (f32[64,2048]{1,0:T(8,128)S(1)}, f32[64,2048]{1,0:T(8,128)S(1)}, u32[]{:S(2)}, u32[]{:S(2)}) collective-permute-start(f32[64,2048]{1,0:T(8,128)S(1)} %get-tuple-element.41), channel_id=1, source_target_pairs={{0,2},{1,5},{2,0},{3,7},{4,6},{5,1},{6,4},{7,3},{8,10},{9,13},{10,... | collective-permute-start | bytes 1572872 | tf_op jit(solution)/shard_map/ppermute | solution.py:459
  29.5 6.5 %collective-permute-start.2 = (f32[32,2048]{1,0:T(8,128)S(1)}, f32[32,2048]{1,0:T(8,128)S(1)}, u32[]{:S(2)}, u32[]{:S(2)}) collective-permute-start(f32[32,2048]{1,0:T(8,128)S(1)} %get-tuple-element.43), channel_id=1, source_target_pairs={{0,4},{1,3},{2,6},{3,1},{4,0},{5,7},{6,2},{7,5},{8,12},{9,11},{10,... | collective-permute-start | bytes 786440 | tf_op jit(solution)/shard_map/ppermute | solution.py:459
  36.0 9.1 %collective-permute-start.3 = (f32[32,2048]{1,0:T(8,128)S(1)}, f32[32,2048]{1,0:T(8,128)S(1)}, u32[]{:S(2)}, u32[]{:S(2)}) collective-permute-start(f32[32,2048]{1,0:T(8,128)S(1)} %add_pieces.6.a_ref), channel_id=1, source_target_pairs={{0,12},{1,13},{2,14},{3,15},{4,8},{5,9},{6,10},{7,11},{8,4},{9,5},... | collective-permute-start | bytes 786440 | tf_op jit(solution)/shard_map/ppermute | solution.py:459
  45.1 9.6 %collective-permute-start.4 = (f32[32,2048]{1,0:T(8,128)S(1)}, f32[32,2048]{1,0:T(8,128)S(1)}, u32[]{:S(2)}, u32[]{:S(2)}) collective-permute-start(f32[32,2048]{1,0:T(8,128)S(1)} %add_pieces.7.a_ref), channel_id=1, source_target_pairs={{0,4},{1,3},{2,6},{3,1},{4,0},{5,7},{6,2},{7,5},{8,12},{9,11},{10,... | collective-permute-start | bytes 786440 | tf_op jit(solution)/shard_map/ppermute | solution.py:459
  54.8 12.1 %copy-start.6 = (s32[4096]{0:T(1024)S(1)}, s32[4096]{0:T(1024)}, u32[]{:S(2)}) copy-start(s32[4096]{0:T(1024)} %param.8) | copy-start | bytes 49156
  54.8 9.2 %collective-permute-start.5 = (f32[64,2048]{1,0:T(8,128)S(1)}, f32[64,2048]{1,0:T(8,128)S(1)}, u32[]{:S(2)}, u32[]{:S(2)}) collective-permute-start(f32[64,2048]{1,0:T(8,128)S(1)} %join_pieces.2.a_ref), channel_id=1, source_target_pairs={{0,2},{1,5},{2,0},{3,7},{4,6},{5,1},{6,4},{7,3},{8,10},{9,13},{10,... | collective-permute-start | bytes 1572872 | tf_op jit(solution)/shard_map/ppermute | solution.py:459
  64.2 2.7 %collective-permute-start.6 = (f32[128,2048]{1,0:T(8,128)S(1)}, f32[128,2048]{1,0:T(8,128)S(1)}, u32[]{:S(2)}, u32[]{:S(2)}) collective-permute-start(f32[128,2048]{1,0:T(8,128)S(1)} %join_pieces.3.a_ref), channel_id=1, source_target_pairs={{0,1},{1,0},{2,3},{3,2},{4,5},{5,4},{6,7},{7,6},{8,9},{9,8},{10,11... | collective-permute-start | bytes 3145736 | tf_op jit(solution)/shard_map/ppermute | solution.py:459
  66.9 3.1 %copy-start.3 = (bf16[2048,1792]{1,0:T(8,128)(2,1)S(1)}, bf16[2048,1792]{1,0:T(8,128)(2,1)}, u32[]{:S(2)}) copy-start(bf16[2048,1792]{1,0:T(8,128)(2,1)} %copy-done.2) | copy-start | bytes 22020100
  70.0 3.1 %copy-start.5 = (bf16[2048,1792]{1,0:T(8,128)(2,1)S(1)}, bf16[2048,1792]{1,0:T(8,128)(2,1)}, u32[]{:S(2)}) copy-start(bf16[2048,1792]{1,0:T(8,128)(2,1)} %copy-done.4) | copy-start | bytes 22020100
  74.2 3.9 %collective-permute-start.7 = (f32[24,256]{1,0:T(8,128)S(1)}, f32[24,256]{1,0:T(8,128)S(1)}, u32[]{:S(2)}, u32[]{:S(2)}) collective-permute-start(f32[24,256]{1,0:T(8,128)S(1)} %get-tuple-element.27.refs_0_), channel_id=1, source_target_pairs={{0,16},{16,0},{1,17},{17,1},{2,18},{18,2},{3,19},{19,3},{4,20},{20... | collective-permute-start | bytes 73736 | tf_op jit(solution)/shard_map/ppermute | solution.py:459
  82.5 42.5 %slice-start = ((s8[7340032]{0:T(1024)(128)(4,1)}), s8[4194304]{0:T(1024)(128)(4,1)S(1)}, s32[]{:S(2)}) async-start(s8[7340032]{0:T(1024)(128)(4,1)} %bitcast.3), calls=%async_computation | async-start | bytes 8388608
  82.5 42.5 %slice-start.2 = ((s8[7340032]{0:T(1024)(128)(4,1)}), s8[4194304]{0:T(1024)(128)(4,1)S(1)}, s32[]{:S(2)}) async-start(s8[7340032]{0:T(1024)(128)(4,1)} %bitcast.5), calls=%async_computation.2 | async-start | bytes 8388608
  82.5 42.5 %slice-start.1 = ((s8[7340032]{0:T(1024)(128)(4,1)}), s8[3145728]{0:T(1024)(128)(4,1)S(1)}, s32[]{:S(2)}) async-start(s8[7340032]{0:T(1024)(128)(4,1)} %bitcast.3), calls=%async_computation.1 | async-start | bytes 6291456
  82.5 42.5 %slice-start.3 = ((s8[7340032]{0:T(1024)(128)(4,1)}), s8[3145728]{0:T(1024)(128)(4,1)S(1)}, s32[]{:S(2)}) async-start(s8[7340032]{0:T(1024)(128)(4,1)} %bitcast.5), calls=%async_computation.3 | async-start | bytes 6291456
  82.5 36.5 %collective-permute-start.12 = (f32[256,1280]{1,0:T(8,128)S(1)}, f32[256,1280]{1,0:T(8,128)S(1)}, u32[]{:S(2)}, u32[]{:S(2)}) collective-permute-start(f32[256,1280]{1,0:T(8,128)S(1)} %get-tuple-element.32.refs_2_), channel_id=1, source_target_pairs={{0,16},{16,0},{1,17},{17,1},{2,18},{18,2},{3,19},{19,3},{4,20},{20... | collective-permute-start | bytes 3932168 | tf_op jit(solution)/shard_map/ppermute | solution.py:459
  85.9 37.6 %collective-permute-start.13 = (f32[256,512]{1,0:T(8,128)S(1)}, f32[256,512]{1,0:T(8,128)S(1)}, u32[]{:S(2)}, u32[]{:S(2)}) collective-permute-start(f32[256,512]{1,0:T(8,128)S(1)} %right_factor.3.refs_0_), channel_id=1, source_target_pairs={{0,16},{16,0},{1,17},{17,1},{2,18},{18,2},{3,19},{19,3},{4,20},{20... | collective-permute-start | bytes 1572872 | tf_op jit(solution)/shard_map/ppermute | solution.py:459
  86.5 5.6 %collective-permute-start.8 = (f32[24,256]{1,0:T(8,128)S(1)}, f32[24,256]{1,0:T(8,128)S(1)}, u32[]{:S(2)}, u32[]{:S(2)}) collective-permute-start(f32[24,256]{1,0:T(8,128)S(1)} %get-tuple-element.28), channel_id=1, source_target_pairs={{0,12},{1,13},{2,14},{3,15},{4,8},{5,9},{6,10},{7,11},{8,4},{9,5},... | collective-permute-start | bytes 73736 | tf_op jit(solution)/shard_map/ppermute | solution.py:459
  92.1 4.6 %collective-permute-start.9 = (f32[48,256]{1,0:T(8,128)S(1)}, f32[48,256]{1,0:T(8,128)S(1)}, u32[]{:S(2)}, u32[]{:S(2)}) collective-permute-start(f32[48,256]{1,0:T(8,128)S(1)} %pad_maximum_fusion.1), channel_id=1, source_target_pairs={{0,4},{1,3},{2,6},{3,1},{4,0},{5,7},{6,2},{7,5},{8,12},{9,11},{10,... | collective-permute-start | bytes 147464 | tf_op jit(solution)/shard_map/ppermute | solution.py:459
  96.7 4.7 %collective-permute-start.10 = (f32[96,256]{1,0:T(8,128)S(1)}, f32[96,256]{1,0:T(8,128)S(1)}, u32[]{:S(2)}, u32[]{:S(2)}) collective-permute-start(f32[96,256]{1,0:T(8,128)S(1)} %pad_maximum_fusion), channel_id=1, source_target_pairs={{0,2},{1,5},{2,0},{3,7},{4,6},{5,1},{6,4},{7,3},{8,10},{9,13},{10,... | collective-permute-start | bytes 294920 | tf_op jit(solution)/shard_map/ppermute | solution.py:459
  101.4 1.5 collective-permute-start.11
  125.0 3.2 %collective-permute-start.14 = (f32[8,256]{1,0:T(8,128)S(1)}, f32[8,256]{1,0:T(8,128)S(1)}, u32[]{:S(2)}, u32[]{:S(2)}) collective-permute-start(f32[8,256]{1,0:T(8,128)S(1)} %get-tuple-element.37), channel_id=1, source_target_pairs={{0,1},{1,0},{2,3},{3,2},{4,5},{5,4},{6,7},{7,6},{8,9},{9,8},{10,11... | collective-permute-start | bytes 24584 | tf_op jit(solution)/shard_map/ppermute | solution.py:459
  128.2 4.6 %collective-permute-start.15 = (f32[8,256]{1,0:T(8,128)S(1)}, f32[8,256]{1,0:T(8,128)S(1)}, u32[]{:S(2)}, u32[]{:S(2)}) collective-permute-start(f32[8,256]{1,0:T(8,128)S(1)} %add.16), channel_id=1, source_target_pairs={{0,2},{1,5},{2,0},{3,7},{4,6},{5,1},{6,4},{7,3},{8,10},{9,13},{10,... | collective-permute-start | bytes 24584 | tf_op jit(solution)/shard_map/ppermute | solution.py:459
  132.8 5.1 %collective-permute-start.16 = (f32[8,256]{1,0:T(8,128)S(1)}, f32[8,256]{1,0:T(8,128)S(1)}, u32[]{:S(2)}, u32[]{:S(2)}) collective-permute-start(f32[8,256]{1,0:T(8,128)S(1)} %add.17), channel_id=1, source_target_pairs={{0,4},{1,3},{2,6},{3,1},{4,0},{5,7},{6,2},{7,5},{8,12},{9,11},{10,... | collective-permute-start | bytes 24584 | tf_op jit(solution)/shard_map/ppermute | solution.py:459
  137.9 5.9 %collective-permute-start.17 = (f32[8,256]{1,0:T(8,128)S(1)}, f32[8,256]{1,0:T(8,128)S(1)}, u32[]{:S(2)}, u32[]{:S(2)}) collective-permute-start(f32[8,256]{1,0:T(8,128)S(1)} %add.18), channel_id=1, source_target_pairs={{0,12},{1,13},{2,14},{3,15},{4,8},{5,9},{6,10},{7,11},{8,4},{9,5},... | collective-permute-start | bytes 24584 | tf_op jit(solution)/shard_map/ppermute | solution.py:459
  143.7 8.2 %copy-start.1 = (s32[384]{0:T(512)S(1)}, s32[384]{0:T(512)}, u32[]{:S(2)}) copy-start(s32[384]{0:T(512)} %param.9) | copy-start | bytes 4612

commit v3 on v2

--- a/solution.py
+++ b/solution.py
@@ -149,7 +149,44 @@
     )(*(in_space(x, pltpu.HBM) for x in (momentum, gradient, right_basis)))
 
 
-def sketch_kernel(fast, scale, a_ref, b_ref, select_ref, signs_ref, *refs):
+def entries_kernel(fast, select_ref, signs_ref, *refs):
+    entries_ref, column_ref = refs[-2:]
+    share, rows = entries_ref.shape
+    column_ref[...] = jnp.broadcast_to(
+        select_ref[...].astype(F32), (column_ref.shape[1], select_ref.shape[1])
+    ).T
+    start = pl.multiple_of(lax.axis_index("wide") * share, 8) if fast else 0
+    select = column_ref[pl.ds(start, share), :1].astype(jnp.int32)
+    first = pl.multiple_of(lax.axis_index("narrow") * rows, rows)
+    column = first + lax.broadcasted_iota(jnp.int32, (1, rows), 1)
+    bits = jnp.bitwise_and(select, column)
+    for shift in (8, 4, 2, 1):
+        bits = jnp.bitwise_xor(bits, jnp.right_shift(bits, shift))
+    entries = (1 - 2 * jnp.bitwise_and(bits, 1)) * signs_ref[:, pl.ds(first, rows)]
+    entries_ref[...] = entries.astype(F32).astype(BF16)
+
+
+def entries_call(fast, select, share, signs, rows, after, held):
+    return pl.pallas_call(
+        functools.partial(entries_kernel, fast),
+        in_specs=[WHOLE] * 2
+        + [pl.BlockSpec(memory_space=pl.ANY)] * len(after)
+        + [WHOLE] * len(held),
+        out_specs=WHOLE,
+        out_shape=jax.ShapeDtypeStruct((share, rows), BF16),
+        scratch_shapes=[pltpu.VMEM((select.shape[0], 128), F32)],
+        compiler_params=pltpu.CompilerParams(vmem_limit_bytes=24 * MIB),
+        cost_estimate=cost(20 * share * rows, 2 * share * rows),
+        name="hadamard_signs",
+    )(
+        select[None, :],
+        signs[None, :],
+        *after,
+        *(in_space(x, pltpu.VMEM) for x in held),
+    )
+
+
+def sketch_kernel(fast, scale, a_ref, b_ref, entries_ref, *refs):
     left_ref, sketch_ref = refs[-2:]
     half, rows = a_ref.shape
     rank = 2 * half
@@ -161,14 +198,8 @@
             hi, lo = split2(ref[block * q : block * q + block, :])
             left_ref[pl.ds(start, block), :] = hi
             left_ref[pl.ds(pl.multiple_of(rank + start, block), block), :] = lo
-    first = pl.multiple_of(lax.axis_index("narrow") * rows, rows)
-    column = first + lax.broadcasted_iota(jnp.int32, (1, rows), 1)
-    bits = jnp.bitwise_and(select_ref[...], column)
-    for shift in (8, 4, 2, 1):
-        bits = jnp.bitwise_xor(bits, jnp.right_shift(bits, shift))
-    entries = (1 - 2 * jnp.bitwise_and(bits, 1)) * signs_ref[:, pl.ds(first, rows)]
     both = lax.dot_general(
-        entries.astype(F32).astype(BF16),
+        entries_ref[...],
         left_ref[...],
         (((1,), (1,)), ((), ())),
         preferred_element_type=F32,
@@ -176,27 +207,22 @@
     sketch_ref[...] = (both[:, :rank] + both[:, rank:]) * scale
 
 
-def sketch_call(fast, first, second, select, signs, scale, held):
+def sketch_call(fast, first, second, entries, scale, held):
     half, rows = first.shape
     rank = 2 * half
+    share = entries.shape[0]
     return pl.pallas_call(
         functools.partial(sketch_kernel, fast, scale),
-        in_specs=[WHOLE] * (4 + len(held)),
+        in_specs=[WHOLE] * (3 + len(held)),
         out_specs=[WHOLE] * 2,
         out_shape=[
             jax.ShapeDtypeStruct((2 * rank, rows), BF16),
-            jax.ShapeDtypeStruct((select.shape[0], rank), F32),
-        ],
-        compiler_params=pltpu.CompilerParams(vmem_limit_bytes=24 * MIB),
-        cost_estimate=cost(4 * select.shape[0] * rank * rows, rows * rank * 8),
+            jax.ShapeDtypeStruct((share, rank), F32),
+        ],
+        compiler_params=pltpu.CompilerParams(vmem_limit_bytes=24 * MIB),
+        cost_estimate=cost(4 * share * rank * rows, rows * rank * 8),
         name="sketch_rows",
-    )(
-        first,
-        second,
-        select[:, None],
-        signs[None, :],
-        *(in_space(x, pltpu.VMEM) for x in held),
-    )
+    )(first, second, entries, *(in_space(x, pltpu.VMEM) for x in held))
 
 
 def right_kernel(first, left_ref, shi_ref, slo_ref, *refs):
@@ -519,7 +545,6 @@
     rows, cols = momentum.shape
     rank = right_basis.shape[1]
     fast = is_fast(narrow, wide)
-    index = lax.axis_index("wide")
     steps = exchanges(wide) if fast else None
     across = [(0, 1), (1, 0)]
     shi, slo, send, keep = left_call(fast, momentum, gradient, right_basis)
@@ -527,21 +552,22 @@
     scale = 1.0 / math.sqrt(sketch_rows)
     if fast:
         share = sketch_rows // wide
-        mine = lax.dynamic_slice_in_dim(select, index * share, share)
         first, second = wide_sum(steps, keep, send, (shi, slo))
-        left, sketch = sketch_call(fast, first, second, mine, signs, scale, (shi, slo))
+        entries = entries_call(fast, select, share, signs, rows, (first,), (shi, slo))
+        left, sketch = sketch_call(fast, first, second, entries, scale, (shi, slo))
         other = swap(sketch, "narrow", across)
-        cut = cols * 2 // 7
+        cut = cols // 256 * 128
         (right,) = right_call(left, shi, slo, 0, cut)
         pieces = [[right, swap(right, "narrow", across)]]
         right, sketch = right_call(left, shi, slo, cut, cols, sketch, other)
         pieces.append([right, swap(right, "narrow", across)])
         for pairs in reversed(steps[1:]):
-            sketch = jnp.concatenate([sketch, swap(sketch, "wide", pairs)], axis=0)
+            sketch = join_call(sketch, swap(sketch, "wide", pairs), ())
         sketches = (sketch, swap(sketch, "wide", steps[0]))
     else:
         first, second = lax.psum((keep, send), "wide")
-        left, sketch = sketch_call(fast, first, second, select, signs, scale, ())
+        entries = entries_call(fast, select, sketch_rows, signs, rows, (), ())
+        left, sketch = sketch_call(fast, first, second, entries, scale, ())
         sketch = lax.psum(sketch, "narrow")
         sketches = (sketch[: sketch_rows // 2], sketch[sketch_rows // 2 :])
         (right,) = right_call(left, shi, slo, 0, cols)
@@ -553,7 +579,7 @@
     if fast:
         momentum_out = None
         for part, pairs in enumerate(steps):
-            squares = squares + swap(squares, "wide", pairs)
+            squares = add_call(squares, swap(squares, "wide", pairs), ())
             momentum_out = momentum_call(
                 part, len(steps), shi, slo, left_terms, right_terms, momentum_out
             )

time: 152 us -> 145 us (0.954)
  local copies, waits for them, and re-layouts: 6.54 us -> 0.14 us
  waiting for transfers between devices: 52.1 us -> 50.2 us
  Pallas kernels: 61.3 us -> 63.1 us
    unnamed x25 -> x4, local copies, waits for them, and re-layouts: 6.24 us -> 0.01 us
    ppermute x18, waiting for transfers between devices: 52.1 us -> 50.2 us  [swap(): return lax.ppermute(x, axis, pairs)]
  transfers between devices with their start and end apart: 18 -> 18, of which waited for: 13 -> 13; matrix products, arithmetic and copies ran while one was open for 0% -> 0% of each run, Pallas kernels for 20% -> 22%
where the time goes in v3:
time: 145 us
  Pallas kernels  63.1 us (44%)
  waiting for transfers between devices  50.2 us (35%)
  starting transfers between devices  31.1 us (21%)
    ppermute x18, waiting for transfers between devices, swap(): return lax.ppermute(x, axis, pairs)  50.2 us
    ppermute x18, starting transfers between devices, swap(): return lax.ppermute(x, axis, pairs)  31.1 us
    pallas_call x1, Pallas kernels, left_call(): pl.pallas_call(functools.partial(left_kernel, fast), in_specs=[hbm] * 3,...  15.5 us
    pallas_call x1, Pallas kernels, factor_call(): pl.pallas_call(factor_kernel, in_specs=[WHOLE] * 2, out_specs=[WHOLE] * 2...  13 us
    pallas_call x4, Pallas kernels, momentum_call(): pl.pallas_call(functools.partial(momentum_kernel, first), grid=(count,),...  12.5 us
    pallas_call x1, Pallas kernels, update_call(): pl.pallas_call(functools.partial(update_kernel, factor / (1.0 - decay_mu)...  8.25 us
    pallas_call x2, Pallas kernels, right_call(): pl.pallas_call(functools.partial(right_kernel, first), in_specs=[WHOLE] *...  7.16 us
    pallas_call x1, Pallas kernels, basis_call(): pl.pallas_call(basis_kernel, grid=(rows // tile,), in_specs=[inv_spec] *...  3.14 us
  transfers between devices with their start and end apart: 18, of which 13 were waited for; matrix products, arithmetic and copies ran while one was open for 0% of the time, Pallas kernels for 22%

profile of v3, /device:TPU:0, one launch (start us, length us, event | category | flops | bytes accessed | tf_op | source)
XLA Modules:
  0.0 145.3 jit_solution(4826769950585932772)
XLA Ops:
  0.6 15.5 %left_factor.1 = (bf16[2048,1792]{1,0:T(8,128)(2,1)S(1)}, bf16[2048,1792]{1,0:T(8,128)(2,1)S(1)}, f32[128,2048]{1,0:T(8,128)S(1)}, f32[128,2048]{1,0:T(8,128)S(1)}) custom-call(f32[2048,1792]{1,0:T(8,128)} %m_hbm.1, bf16[2048,1792]{1,0:T(8,128)(2,1)} %g_hbm.1, f32[1792,256]{1,0:T(8,128)} %b_hbm.1), custom_call_target="tpu_custom_call" | custom-call | flops 5637144576 | bytes 22020096 | tf_op jit(solution)/shard_map/left_factor/pallas_call | solution.py:126
  16.2 0.5 collective-permute-start
  16.7 2.3 %collective-permute-done.b_ref = f32[128,2048]{1,0:T(8,128)S(1)} collective-permute-done((f32[128,2048]{1,0:T(8,128)S(1)}, f32[128,2048]{1,0:T(8,128)S(1)}, u32[]{:S(2)}, u32[]{:S(2)}) %collective-permute-start) | collective-permute-done | bytes 1048608 | tf_op jit(solution)/shard_map/ppermute | solution.py:485
  19.0 0.1 add_pieces.8
  19.1 0.1 fusion
  19.2 3.0 %collective-permute-start.1 = (f32[64,2048]{1,0:T(8,128)S(1)}, f32[64,2048]{1,0:T(8,128)S(1)}, u32[]{:S(2)}, u32[]{:S(2)}) collective-permute-start(f32[64,2048]{1,0:T(8,128)S(1)} %get-tuple-element.41), channel_id=1, source_target_pairs={{0,2},{1,5},{2,0},{3,7},{4,6},{5,1},{6,4},{7,3},{8,10},{9,13},{10,... | collective-permute-start | bytes 1572872 | tf_op jit(solution)/shard_map/ppermute | solution.py:485
  22.2 7.2 %collective-permute-done.1.b_ref = f32[64,2048]{1,0:T(8,128)S(1)} collective-permute-done((f32[64,2048]{1,0:T(8,128)S(1)}, f32[64,2048]{1,0:T(8,128)S(1)}, u32[]{:S(2)}, u32[]{:S(2)}) %collective-permute-start.1) | collective-permute-done | bytes 524320 | tf_op jit(solution)/shard_map/ppermute | solution.py:485
  29.3 0.1 add_pieces.9
  29.4 2.1 %collective-permute-start.2 = (f32[32,2048]{1,0:T(8,128)S(1)}, f32[32,2048]{1,0:T(8,128)S(1)}, u32[]{:S(2)}, u32[]{:S(2)}) collective-permute-start(f32[32,2048]{1,0:T(8,128)S(1)} %get-tuple-element.43), channel_id=1, source_target_pairs={{0,4},{1,3},{2,6},{3,1},{4,0},{5,7},{6,2},{7,5},{8,12},{9,11},{10,... | collective-permute-start | bytes 786440 | tf_op jit(solution)/shard_map/ppermute | solution.py:485
  31.6 4.4 %collective-permute-done.2.b_ref = f32[32,2048]{1,0:T(8,128)S(1)} collective-permute-done((f32[32,2048]{1,0:T(8,128)S(1)}, f32[32,2048]{1,0:T(8,128)S(1)}, u32[]{:S(2)}, u32[]{:S(2)}) %collective-permute-start.2) | collective-permute-done | bytes 262176 | tf_op jit(solution)/shard_map/ppermute | solution.py:485
  35.9 4.1 %collective-permute-start.3 = (f32[32,2048]{1,0:T(8,128)S(1)}, f32[32,2048]{1,0:T(8,128)S(1)}, u32[]{:S(2)}, u32[]{:S(2)}) collective-permute-start(f32[32,2048]{1,0:T(8,128)S(1)} %add_pieces.10.a_ref), channel_id=1, source_target_pairs={{0,12},{1,13},{2,14},{3,15},{4,8},{5,9},{6,10},{7,11},{8,4},{9,5},... | collective-permute-start | bytes 786440 | tf_op jit(solution)/shard_map/ppermute | solution.py:485
  40.1 5.0 %collective-permute-done.3.b_ref = f32[32,2048]{1,0:T(8,128)S(1)} collective-permute-done((f32[32,2048]{1,0:T(8,128)S(1)}, f32[32,2048]{1,0:T(8,128)S(1)}, u32[]{:S(2)}, u32[]{:S(2)}) %collective-permute-start.3) | collective-permute-done | bytes 262176 | tf_op jit(solution)/shard_map/ppermute | solution.py:485
  45.1 5.3 %collective-permute-start.4 = (f32[32,2048]{1,0:T(8,128)S(1)}, f32[32,2048]{1,0:T(8,128)S(1)}, u32[]{:S(2)}, u32[]{:S(2)}) collective-permute-start(f32[32,2048]{1,0:T(8,128)S(1)} %add_pieces.11.a_ref), channel_id=1, source_target_pairs={{0,4},{1,3},{2,6},{3,1},{4,0},{5,7},{6,2},{7,5},{8,12},{9,11},{10,... | collective-permute-start | bytes 786440 | tf_op jit(solution)/shard_map/ppermute | solution.py:485
  50.4 4.4 %collective-permute-done.4.b_ref = f32[32,2048]{1,0:T(8,128)S(1)} collective-permute-done((f32[32,2048]{1,0:T(8,128)S(1)}, f32[32,2048]{1,0:T(8,128)S(1)}, u32[]{:S(2)}, u32[]{:S(2)}) %collective-permute-start.4) | collective-permute-done | bytes 262176 | tf_op jit(solution)/shard_map/ppermute | solution.py:485
  54.8 0.0 copy-start.1
  54.8 0.0 copy-start
  54.8 1.6 %collective-permute-start.5 = (f32[64,2048]{1,0:T(8,128)S(1)}, f32[64,2048]{1,0:T(8,128)S(1)}, u32[]{:S(2)}, u32[]{:S(2)}) collective-permute-start(f32[64,2048]{1,0:T(8,128)S(1)} %join_pieces.5.a_ref), channel_id=1, source_target_pairs={{0,2},{1,5},{2,0},{3,7},{4,6},{5,1},{6,4},{7,3},{8,10},{9,13},{10,... | collective-permute-start | bytes 1572872 | tf_op jit(solution)/shard_map/ppermute | solution.py:485
  56.4 7.7 %collective-permute-done.5.b_ref = f32[64,2048]{1,0:T(8,128)S(1)} collective-permute-done((f32[64,2048]{1,0:T(8,128)S(1)}, f32[64,2048]{1,0:T(8,128)S(1)}, u32[]{:S(2)}, u32[]{:S(2)}) %collective-permute-start.5) | collective-permute-done | bytes 524320 | tf_op jit(solution)/shard_map/ppermute | solution.py:485
  64.0 0.1 join_pieces.6.refs_0_.a_ref
  64.1 0.1 collective-permute-start.6
  64.2 0.0 copy-done.1
  64.2 0.0 copy-done
  64.2 0.3 hadamard_signs.1.entries_ref
  64.5 2.3 %collective-permute-done.6.b_ref = f32[128,2048]{1,0:T(8,128)S(1)} collective-permute-done((f32[128,2048]{1,0:T(8,128)S(1)}, f32[128,2048]{1,0:T(8,128)S(1)}, u32[]{:S(2)}, u32[]{:S(2)}) %collective-permute-start.6) | collective-permute-done | bytes 1048608 | tf_op jit(solution)/shard_map/ppermute | solution.py:485
  66.8 1.2 sketch_rows.1
  68.0 1.5 %collective-permute-start.7 = (f32[24,256]{1,0:T(8,128)S(1)}, f32[24,256]{1,0:T(8,128)S(1)}, u32[]{:S(2)}, u32[]{:S(2)}) collective-permute-start(f32[24,256]{1,0:T(8,128)S(1)} %get-tuple-element.27.refs_0_), channel_id=1, source_target_pairs={{0,16},{16,0},{1,17},{17,1},{2,18},{18,2},{3,19},{19,3},{4,20},{20... | collective-permute-start | bytes 73736 | tf_op jit(solution)/shard_map/ppermute | solution.py:485
  69.5 2.3 %collective-permute-done.7.refs_1_ = f32[24,256]{1,0:T(8,128)S(1)} collective-permute-done((f32[24,256]{1,0:T(8,128)S(1)}, f32[24,256]{1,0:T(8,128)S(1)}, u32[]{:S(2)}, u32[]{:S(2)}) %collective-permute-start.7) | collective-permute-done | bytes 24608 | tf_op jit(solution)/shard_map/ppermute | solution.py:485
  71.9 3.7 %right_factor.2 = (f32[256,896]{1,0:T(8,128)S(1)}, f32[24,256]{1,0:T(8,128)S(1)}) custom-call(bf16[512,2048]{1,0:T(8,128)(2,1)S(1)} %get-tuple-element.26.left_ref.raw_ref, bf16[2048,1792]{1,0:T(8,128)(2,1)S(1)} %get-tuple-element.22.refs_0_.refs_1_.shi_ref, bf16[2048,1792]{1,0:T(8,128)(2,1)S(1)} %get-tuple-element.23.refs_1_.refs_2_.slo_ref, ...), custom_call_target="tpu_custom_call" | custom-call | flops 2818572288 | bytes 7340032 | tf_op jit(solution)/shard_map/right_factor/pallas_call | solution.py:250
  75.6 1.6 %collective-permute-start.12 = (f32[256,896]{1,0:T(8,128)S(1)}, f32[256,896]{1,0:T(8,128)S(1)}, u32[]{:S(2)}, u32[]{:S(2)}) collective-permute-start(f32[256,896]{1,0:T(8,128)S(1)} %get-tuple-element.32.refs_2_), channel_id=1, source_target_pairs={{0,16},{16,0},{1,17},{17,1},{2,18},{18,2},{3,19},{19,3},{4,20},{20... | collective-permute-start | bytes 2752520 | tf_op jit(solution)/shard_map/ppermute | solution.py:485
  77.1 3.5 %right_factor.3.refs_0_ = f32[256,896]{1,0:T(8,128)S(1)} custom-call(bf16[512,2048]{1,0:T(8,128)(2,1)S(1)} %get-tuple-element.26.left_ref.raw_ref, bf16[2048,1792]{1,0:T(8,128)(2,1)S(1)} %get-tuple-element.22.refs_0_.refs_1_.shi_ref, bf16[2048,1792]{1,0:T(8,128)(2,1)S(1)} %get-tuple-element.23.refs_1_.refs_2_.slo_ref), custom_call_target="tpu_custom_call" | custom-call | flops 2818572288 | bytes 7340032 | tf_op jit(solution)/shard_map/right_factor/pallas_call | solution.py:250
  80.6 0.6 collective-permute-start.13
  81.2 2.5 %collective-permute-start.8 = (f32[24,256]{1,0:T(8,128)S(1)}, f32[24,256]{1,0:T(8,128)S(1)}, u32[]{:S(2)}, u32[]{:S(2)}) collective-permute-start(f32[24,256]{1,0:T(8,128)S(1)} %get-tuple-element.28.a_ref), channel_id=1, source_target_pairs={{0,12},{1,13},{2,14},{3,15},{4,8},{5,9},{6,10},{7,11},{8,4},{9,5},... | collective-permute-start | bytes 73736 | tf_op jit(solution)/shard_map/ppermute | solution.py:485
  83.7 3.1 %collective-permute-done.8.b_ref = f32[24,256]{1,0:T(8,128)S(1)} collective-permute-done((f32[24,256]{1,0:T(8,128)S(1)}, f32[24,256]{1,0:T(8,128)S(1)}, u32[]{:S(2)}, u32[]{:S(2)}) %collective-permute-start.8) | collective-permute-done | bytes 24608 | tf_op jit(solution)/shard_map/ppermute | solution.py:485
  86.8 0.2 collective-permute-start.9
  87.1 4.4 %collective-permute-done.9.b_ref = f32[48,256]{1,0:T(8,128)S(1)} collective-permute-done((f32[48,256]{1,0:T(8,128)S(1)}, f32[48,256]{1,0:T(8,128)S(1)}, u32[]{:S(2)}, u32[]{:S(2)}) %collective-permute-start.9) | collective-permute-done | bytes 49184 | tf_op jit(solution)/shard_map/ppermute | solution.py:485
  91.5 1.6 %collective-permute-start.10 = (f32[96,256]{1,0:T(8,128)S(1)}, f32[96,256]{1,0:T(8,128)S(1)}, u32[]{:S(2)}, u32[]{:S(2)}) collective-permute-start(f32[96,256]{1,0:T(8,128)S(1)} %join_pieces.8.a_ref), channel_id=1, source_target_pairs={{0,2},{1,5},{2,0},{3,7},{4,6},{5,1},{6,4},{7,3},{8,10},{9,13},{10,... | collective-permute-start | bytes 294920 | tf_op jit(solution)/shard_map/ppermute | solution.py:485
  93.1 3.1 %collective-permute-done.10.b_ref = f32[96,256]{1,0:T(8,128)S(1)} collective-permute-done((f32[96,256]{1,0:T(8,128)S(1)}, f32[96,256]{1,0:T(8,128)S(1)}, u32[]{:S(2)}, u32[]{:S(2)}) %collective-permute-start.10) | collective-permute-done | bytes 98336 | tf_op jit(solution)/shard_map/ppermute | solution.py:485
  96.2 0.1 collective-permute-start.11
  96.2 1.4 collective-permute-done.11.b_ref
  97.7 13.0 %factor_inverse.1 = (bf16[256,256]{1,0:T(8,128)(2,1)S(1)}, bf16[256,256]{1,0:T(8,128)(2,1)S(1)}) custom-call(f32[192,256]{1,0:T(8,128)S(1)} %join_pieces.9.a_ref, f32[192,256]{1,0:T(8,128)S(1)} %collective-permute-done.11.b_ref), custom_call_target="tpu_custom_call" | custom-call | flops 1000000 | bytes 100000 | tf_op jit(solution)/shard_map/factor_inverse/pallas_call | solution.py:327
  110.7 3.1 %left_basis.1 = (bf16[2048,768]{1,0:T(8,128)(2,1)S(1)}, f32[2048,256]{1,0:T(8,128)S(1)}) custom-call(bf16[256,256]{1,0:T(8,128)(2,1)S(1)} %get-tuple-element.29.hi_ref, bf16[256,256]{1,0:T(8,128)(2,1)S(1)} %get-tuple-element.30.lo_ref, bf16[512,2048]{1,0:T(8,128)(2,1)S(1)} %get-tuple-element.26.left_ref.raw_ref), custom_call_target="tpu_custom_call" | custom-call | flops 1000000 | bytes 100000 | tf_op jit(solution)/shard_map/left_basis/pallas_call | solution.py:353
  113.8 0.0 collective-permute-done.12.refs_3_
  113.8 2.7 %collective-permute-done.13.refs_1_ = f32[256,896]{1,0:T(8,128)S(1)} collective-permute-done((f32[256,896]{1,0:T(8,128)S(1)}, f32[256,896]{1,0:T(8,128)S(1)}, u32[]{:S(2)}, u32[]{:S(2)}) %collective-permute-start.13) | collective-permute-done | bytes 917536 | tf_op jit(solution)/shard_map/ppermute | solution.py:485
  116.5 1.7 %right_rotate.1 = (f32[1792,256]{1,0:T(8,128)S(1)}, bf16[768,1792]{1,0:T(8,128)(2,1)S(1)}, f32[8,256]{1,0:T(8,128)S(1)}) custom-call(bf16[256,256]{1,0:T(8,128)(2,1)S(1)} %get-tuple-element.29.hi_ref, bf16[256,256]{1,0:T(8,128)(2,1)S(1)} %get-tuple-element.30.lo_ref, f32[256,896]{1,0:T(8,128)S(1)} %right_factor.3.refs_0_, ...), custom_call_target="tpu_custom_call" | custom-call | flops 704643072 | bytes 7340032 | tf_op jit(solution)/shard_map/right_rotate/pallas_call | solution.py:401
  118.2 0.0 collective-permute-start.14
  118.2 3.1 %momentum_update.4.refs_0_ = f32[2048,1792]{1,0:T(8,128)} custom-call(bf16[2048,1792]{1,0:T(8,128)(2,1)S(1)} %get-tuple-element.22.refs_0_.refs_1_.shi_ref, bf16[2048,1792]{1,0:T(8,128)(2,1)S(1)} %get-tuple-element.23.refs_1_.refs_2_.slo_ref, bf16[2048,768]{1,0:T(8,128)(2,1)S(1)} %get-tuple-element.33.left_ref, bf16[768,1792]{1,0:T(8,128)(2,1)S(1)} %get-tuple-element.35.terms_ref), custom_call_target="tpu_custom_call" | custom-call | flops 1409286144 | bytes 3670016 | tf_op jit(solution)/shard_map/momentum_update/pallas_call | solution.py:435
  121.4 0.0 collective-permute-done.14.b_ref
  121.4 1.5 %collective-permute-start.15 = (f32[8,256]{1,0:T(8,128)S(1)}, f32[8,256]{1,0:T(8,128)S(1)}, u32[]{:S(2)}, u32[]{:S(2)}) collective-permute-start(f32[8,256]{1,0:T(8,128)S(1)} %add_pieces.12.a_ref), channel_id=1, source_target_pairs={{0,2},{1,5},{2,0},{3,7},{4,6},{5,1},{6,4},{7,3},{8,10},{9,13},{10,... | collective-permute-start | bytes 24584 | tf_op jit(solution)/shard_map/ppermute | solution.py:485
  122.9 3.1 %momentum_update.5.refs_0_ = f32[2048,1792]{1,0:T(8,128)} custom-call(bf16[2048,1792]{1,0:T(8,128)(2,1)S(1)} %get-tuple-element.22.refs_0_.refs_1_.shi_ref, bf16[2048,1792]{1,0:T(8,128)(2,1)S(1)} %get-tuple-element.23.refs_1_.refs_2_.slo_ref, bf16[2048,768]{1,0:T(8,128)(2,1)S(1)} %get-tuple-element.33.left_ref, ...), custom_call_target="tpu_custom_call", output_to_operand_aliasing={{}: (4, {})} | custom-call | flops 1409286144 | bytes 3670016 | tf_op jit(solution)/shard_map/momentum_update/pallas_call | solution.py:435
  126.0 0.0 collective-permute-done.15.b_ref
  126.0 2.0 %collective-permute-start.16 = (f32[8,256]{1,0:T(8,128)S(1)}, f32[8,256]{1,0:T(8,128)S(1)}, u32[]{:S(2)}, u32[]{:S(2)}) collective-permute-start(f32[8,256]{1,0:T(8,128)S(1)} %add_pieces.13.a_ref), channel_id=1, source_target_pairs={{0,4},{1,3},{2,6},{3,1},{4,0},{5,7},{6,2},{7,5},{8,12},{9,11},{10,... | collective-permute-start | bytes 24584 | tf_op jit(solution)/shard_map/ppermute | solution.py:485
  128.0 3.1 %momentum_update.6.refs_0_ = f32[2048,1792]{1,0:T(8,128)} custom-call(bf16[2048,1792]{1,0:T(8,128)(2,1)S(1)} %get-tuple-element.22.refs_0_.refs_1_.shi_ref, bf16[2048,1792]{1,0:T(8,128)(2,1)S(1)} %get-tuple-element.23.refs_1_.refs_2_.slo_ref, bf16[2048,768]{1,0:T(8,128)(2,1)S(1)} %get-tuple-element.33.left_ref, ...), custom_call_target="tpu_custom_call", output_to_operand_aliasing={{}: (4, {})} | custom-call | flops 1409286144 | bytes 3670016 | tf_op jit(solution)/shard_map/momentum_update/pallas_call | solution.py:435
  131.2 0.0 collective-permute-done.16.b_ref
  131.2 2.8 %collective-permute-start.17 = (f32[8,256]{1,0:T(8,128)S(1)}, f32[8,256]{1,0:T(8,128)S(1)}, u32[]{:S(2)}, u32[]{:S(2)}) collective-permute-start(f32[8,256]{1,0:T(8,128)S(1)} %add_pieces.14.a_ref), channel_id=1, source_target_pairs={{0,12},{1,13},{2,14},{3,15},{4,8},{5,9},{6,10},{7,11},{8,4},{9,5},... | collective-permute-start | bytes 24584 | tf_op jit(solution)/shard_map/ppermute | solution.py:485
  134.0 3.1 %momentum_update.7 = f32[2048,1792]{1,0:T(8,128)} custom-call(bf16[2048,1792]{1,0:T(8,128)(2,1)S(1)} %get-tuple-element.22.refs_0_.refs_1_.shi_ref, bf16[2048,1792]{1,0:T(8,128)(2,1)S(1)} %get-tuple-element.23.refs_1_.refs_2_.slo_ref, bf16[2048,768]{1,0:T(8,128)(2,1)S(1)} %get-tuple-element.33.left_ref, ...), custom_call_target="tpu_custom_call", output_to_operand_aliasing={{}: (4, {})} | custom-call | flops 1409286144 | bytes 3670016 | tf_op jit(solution)/shard_map/momentum_update/pallas_call | solution.py:435
  137.1 0.0 collective-permute-done.17.b_ref
  137.1 8.3 %update_basis.1 = (bf16[2048,1792]{1,0:T(8,128)(2,1)}, f32[1792,256]{1,0:T(8,128)}) custom-call(f32[1792,256]{1,0:T(8,128)S(1)} %get-tuple-element.36.turned_ref, f32[8,256]{1,0:T(8,128)S(1)} %add_pieces.15.squares_ref, f32[2048,256]{1,0:T(8,128)S(1)} %get-tuple-element.38.left_ref, bf16[768,1792]{1,0:T(8,128)(2,1)S(1)} %get-tuple-element.35.terms_ref), custom_call_target="tpu_custom_call" | custom-call | flops 5637144576 | bytes 7340032 | tf_op jit(solution)/shard_map/update_basis/pallas_call | solution.py:466
  (12 shorter events, 0.2 us)
Async XLA Ops:
  16.2 2.8 %collective-permute-start = (f32[128,2048]{1,0:T(8,128)S(1)}, f32[128,2048]{1,0:T(8,128)S(1)}, u32[]{:S(2)}, u32[]{:S(2)}) collective-permute-start(f32[128,2048]{1,0:T(8,128)S(1)} %get-tuple-element.25), channel_id=1, source_target_pairs={{0,1},{1,0},{2,3},{3,2},{4,5},{5,4},{6,7},{7,6},{8,9},{9,8},{10,11... | collective-permute-start | bytes 3145736 | tf_op jit(solution)/shard_map/ppermute | solution.py:485
  19.2 10.1 %collective-permute-start.1 = (f32[64,2048]{1,0:T(8,128)S(1)}, f32[64,2048]{1,0:T(8,128)S(1)}, u32[]{:S(2)}, u32[]{:S(2)}) collective-permute-start(f32[64,2048]{1,0:T(8,128)S(1)} %get-tuple-element.41), channel_id=1, source_target_pairs={{0,2},{1,5},{2,0},{3,7},{4,6},{5,1},{6,4},{7,3},{8,10},{9,13},{10,... | collective-permute-start | bytes 1572872 | tf_op jit(solution)/shard_map/ppermute | solution.py:485
  29.4 6.5 %collective-permute-start.2 = (f32[32,2048]{1,0:T(8,128)S(1)}, f32[32,2048]{1,0:T(8,128)S(1)}, u32[]{:S(2)}, u32[]{:S(2)}) collective-permute-start(f32[32,2048]{1,0:T(8,128)S(1)} %get-tuple-element.43), channel_id=1, source_target_pairs={{0,4},{1,3},{2,6},{3,1},{4,0},{5,7},{6,2},{7,5},{8,12},{9,11},{10,... | collective-permute-start | bytes 786440 | tf_op jit(solution)/shard_map/ppermute | solution.py:485
  35.9 9.1 %collective-permute-start.3 = (f32[32,2048]{1,0:T(8,128)S(1)}, f32[32,2048]{1,0:T(8,128)S(1)}, u32[]{:S(2)}, u32[]{:S(2)}) collective-permute-start(f32[32,2048]{1,0:T(8,128)S(1)} %add_pieces.10.a_ref), channel_id=1, source_target_pairs={{0,12},{1,13},{2,14},{3,15},{4,8},{5,9},{6,10},{7,11},{8,4},{9,5},... | collective-permute-start | bytes 786440 | tf_op jit(solution)/shard_map/ppermute | solution.py:485
  45.1 9.6 %collective-permute-start.4 = (f32[32,2048]{1,0:T(8,128)S(1)}, f32[32,2048]{1,0:T(8,128)S(1)}, u32[]{:S(2)}, u32[]{:S(2)}) collective-permute-start(f32[32,2048]{1,0:T(8,128)S(1)} %add_pieces.11.a_ref), channel_id=1, source_target_pairs={{0,4},{1,3},{2,6},{3,1},{4,0},{5,7},{6,2},{7,5},{8,12},{9,11},{10,... | collective-permute-start | bytes 786440 | tf_op jit(solution)/shard_map/ppermute | solution.py:485
  54.8 9.4 %copy-start.1 = (s32[384]{0:T(512)S(1)}, s32[384]{0:T(512)}, u32[]{:S(2)}) copy-start(s32[384]{0:T(512)} %param.9) | copy-start | bytes 4612
  54.8 9.4 %copy-start = (s32[4096]{0:T(1024)S(1)}, s32[4096]{0:T(1024)}, u32[]{:S(2)}) copy-start(s32[4096]{0:T(1024)} %param.8) | copy-start | bytes 49156
  54.8 9.2 %collective-permute-start.5 = (f32[64,2048]{1,0:T(8,128)S(1)}, f32[64,2048]{1,0:T(8,128)S(1)}, u32[]{:S(2)}, u32[]{:S(2)}) collective-permute-start(f32[64,2048]{1,0:T(8,128)S(1)} %join_pieces.5.a_ref), channel_id=1, source_target_pairs={{0,2},{1,5},{2,0},{3,7},{4,6},{5,1},{6,4},{7,3},{8,10},{9,13},{10,... | collective-permute-start | bytes 1572872 | tf_op jit(solution)/shard_map/ppermute | solution.py:485
  64.1 2.7 %collective-permute-start.6 = (f32[128,2048]{1,0:T(8,128)S(1)}, f32[128,2048]{1,0:T(8,128)S(1)}, u32[]{:S(2)}, u32[]{:S(2)}) collective-permute-start(f32[128,2048]{1,0:T(8,128)S(1)} %join_pieces.6.refs_0_.a_ref), channel_id=1, source_target_pairs={{0,1},{1,0},{2,3},{3,2},{4,5},{5,4},{6,7},{7,6},{8,9},{9,8},{10,11... | collective-permute-start | bytes 3145736 | tf_op jit(solution)/shard_map/ppermute | solution.py:485
  68.0 3.9 %collective-permute-start.7 = (f32[24,256]{1,0:T(8,128)S(1)}, f32[24,256]{1,0:T(8,128)S(1)}, u32[]{:S(2)}, u32[]{:S(2)}) collective-permute-start(f32[24,256]{1,0:T(8,128)S(1)} %get-tuple-element.27.refs_0_), channel_id=1, source_target_pairs={{0,16},{16,0},{1,17},{17,1},{2,18},{18,2},{3,19},{19,3},{4,20},{20... | collective-permute-start | bytes 73736 | tf_op jit(solution)/shard_map/ppermute | solution.py:485
  75.6 38.3 %collective-permute-start.12 = (f32[256,896]{1,0:T(8,128)S(1)}, f32[256,896]{1,0:T(8,128)S(1)}, u32[]{:S(2)}, u32[]{:S(2)}) collective-permute-start(f32[256,896]{1,0:T(8,128)S(1)} %get-tuple-element.32.refs_2_), channel_id=1, source_target_pairs={{0,16},{16,0},{1,17},{17,1},{2,18},{18,2},{3,19},{19,3},{4,20},{20... | collective-permute-start | bytes 2752520 | tf_op jit(solution)/shard_map/ppermute | solution.py:485
  80.6 35.9 %collective-permute-start.13 = (f32[256,896]{1,0:T(8,128)S(1)}, f32[256,896]{1,0:T(8,128)S(1)}, u32[]{:S(2)}, u32[]{:S(2)}) collective-permute-start(f32[256,896]{1,0:T(8,128)S(1)} %right_factor.3.refs_0_), channel_id=1, source_target_pairs={{0,16},{16,0},{1,17},{17,1},{2,18},{18,2},{3,19},{19,3},{4,20},{20... | collective-permute-start | bytes 2752520 | tf_op jit(solution)/shard_map/ppermute | solution.py:485
  81.2 5.6 %collective-permute-start.8 = (f32[24,256]{1,0:T(8,128)S(1)}, f32[24,256]{1,0:T(8,128)S(1)}, u32[]{:S(2)}, u32[]{:S(2)}) collective-permute-start(f32[24,256]{1,0:T(8,128)S(1)} %get-tuple-element.28.a_ref), channel_id=1, source_target_pairs={{0,12},{1,13},{2,14},{3,15},{4,8},{5,9},{6,10},{7,11},{8,4},{9,5},... | collective-permute-start | bytes 73736 | tf_op jit(solution)/shard_map/ppermute | solution.py:485
  86.8 4.6 %collective-permute-start.9 = (f32[48,256]{1,0:T(8,128)S(1)}, f32[48,256]{1,0:T(8,128)S(1)}, u32[]{:S(2)}, u32[]{:S(2)}) collective-permute-start(f32[48,256]{1,0:T(8,128)S(1)} %join_pieces.7.a_ref), channel_id=1, source_target_pairs={{0,4},{1,3},{2,6},{3,1},{4,0},{5,7},{6,2},{7,5},{8,12},{9,11},{10,... | collective-permute-start | bytes 147464 | tf_op jit(solution)/shard_map/ppermute | solution.py:485
  91.5 4.7 %collective-permute-start.10 = (f32[96,256]{1,0:T(8,128)S(1)}, f32[96,256]{1,0:T(8,128)S(1)}, u32[]{:S(2)}, u32[]{:S(2)}) collective-permute-start(f32[96,256]{1,0:T(8,128)S(1)} %join_pieces.8.a_ref), channel_id=1, source_target_pairs={{0,2},{1,5},{2,0},{3,7},{4,6},{5,1},{6,4},{7,3},{8,10},{9,13},{10,... | collective-permute-start | bytes 294920 | tf_op jit(solution)/shard_map/ppermute | solution.py:485
  96.2 1.5 %collective-permute-start.11 = (f32[192,256]{1,0:T(8,128)S(1)}, f32[192,256]{1,0:T(8,128)S(1)}, u32[]{:S(2)}, u32[]{:S(2)}) collective-permute-start(f32[192,256]{1,0:T(8,128)S(1)} %join_pieces.9.a_ref), channel_id=1, source_target_pairs={{0,1},{1,0},{2,3},{3,2},{4,5},{5,4},{6,7},{7,6},{8,9},{9,8},{10,11... | collective-permute-start | bytes 589832 | tf_op jit(solution)/shard_map/ppermute | solution.py:485
  118.2 3.2 %collective-permute-start.14 = (f32[8,256]{1,0:T(8,128)S(1)}, f32[8,256]{1,0:T(8,128)S(1)}, u32[]{:S(2)}, u32[]{:S(2)}) collective-permute-start(f32[8,256]{1,0:T(8,128)S(1)} %get-tuple-element.37.a_ref), channel_id=1, source_target_pairs={{0,1},{1,0},{2,3},{3,2},{4,5},{5,4},{6,7},{7,6},{8,9},{9,8},{10,11... | collective-permute-start | bytes 24584 | tf_op jit(solution)/shard_map/ppermute | solution.py:485
  121.4 4.6 %collective-permute-start.15 = (f32[8,256]{1,0:T(8,128)S(1)}, f32[8,256]{1,0:T(8,128)S(1)}, u32[]{:S(2)}, u32[]{:S(2)}) collective-permute-start(f32[8,256]{1,0:T(8,128)S(1)} %add_pieces.12.a_ref), channel_id=1, source_target_pairs={{0,2},{1,5},{2,0},{3,7},{4,6},{5,1},{6,4},{7,3},{8,10},{9,13},{10,... | collective-permute-start | bytes 24584 | tf_op jit(solution)/shard_map/ppermute | solution.py:485
  126.0 5.1 %collective-permute-start.16 = (f32[8,256]{1,0:T(8,128)S(1)}, f32[8,256]{1,0:T(8,128)S(1)}, u32[]{:S(2)}, u32[]{:S(2)}) collective-permute-start(f32[8,256]{1,0:T(8,128)S(1)} %add_pieces.13.a_ref), channel_id=1, source_target_pairs={{0,4},{1,3},{2,6},{3,1},{4,0},{5,7},{6,2},{7,5},{8,12},{9,11},{10,... | collective-permute-start | bytes 24584 | tf_op jit(solution)/shard_map/ppermute | solution.py:485
  131.2 5.9 %collective-permute-start.17 = (f32[8,256]{1,0:T(8,128)S(1)}, f32[8,256]{1,0:T(8,128)S(1)}, u32[]{:S(2)}, u32[]{:S(2)}) collective-permute-start(f32[8,256]{1,0:T(8,128)S(1)} %add_pieces.14.a_ref), channel_id=1, source_target_pairs={{0,12},{1,13},{2,14},{3,15},{4,8},{5,9},{6,10},{7,11},{8,4},{9,5},... | collective-permute-start | bytes 24584 | tf_op jit(solution)/shard_map/ppermute | solution.py:485

commit v4 on v3

--- a/solution.py
+++ b/solution.py
@@ -110,7 +110,8 @@
         hi, lo = split2(m_ref[slot, :] + g_ref[slot, :].astype(F32))
         shi_ref[part, :] = hi
         slo_ref[part, :] = lo
-        left = dot(hi, bhi[...]) + (dot(lo, bhi[...]) + dot(hi, blo[...]))
+        both = dot(jnp.concatenate([hi, lo], axis=0), bhi[...])
+        left = (both[:TILE] + both[TILE:]) + dot(hi, blo[...])
         lt[...] = left.T
         for side, ref in enumerate((keep_ref, send_ref)):
             for q in range(4):
@@ -461,7 +462,7 @@
 def update_call(factor, turned, squares, left, terms):
     cols, rank = turned.shape
     rows = left.shape[0]
-    tile = 256
+    tile = min(rows, 512)
     share = cols // (rows // tile)
     return pl.pallas_call(
         functools.partial(update_kernel, factor / (1.0 - decay_mu)),

time: 145 us -> 145 us (level)
  no operation moved by 1% of the time
where the time goes in v4:
time: 145 us
  Pallas kernels  62.6 us (43%)
  waiting for transfers between devices  50.2 us (35%)
  starting transfers between devices  31.1 us (21%)
    ppermute x18, waiting for transfers between devices, swap(): return lax.ppermute(x, axis, pairs)  50.2 us
    ppermute x18, starting transfers between devices, swap(): return lax.ppermute(x, axis, pairs)  31.1 us
    pallas_call x1, Pallas kernels, left_call(): pl.pallas_call(functools.partial(left_kernel, fast), in_specs=[hbm] * 3,...  15.5 us
    pallas_call x1, Pallas kernels, factor_call(): pl.pallas_call(factor_kernel, in_specs=[WHOLE] * 2, out_specs=[WHOLE] * 2...  13 us
    pallas_call x4, Pallas kernels, momentum_call(): pl.pallas_call(functools.partial(momentum_kernel, first), grid=(count,),...  12.5 us
    pallas_call x1, Pallas kernels, update_call(): pl.pallas_call(functools.partial(update_kernel, factor / (1.0 - decay_mu)...  7.86 us
    pallas_call x2, Pallas kernels, right_call(): pl.pallas_call(functools.partial(right_kernel, first), in_specs=[WHOLE] *...  7.16 us
    pallas_call x1, Pallas kernels, basis_call(): pl.pallas_call(basis_kernel, grid=(rows // tile,), in_specs=[inv_spec] *...  3.14 us
  transfers between devices with their start and end apart: 18, of which 13 were waited for; matrix products, arithmetic and copies ran while one was open for 0% of the time, Pallas kernels for 22%

profile of v4, /device:TPU:0, one launch (start us, length us, event | category | flops | bytes accessed | tf_op | source)
XLA Modules:
  0.0 144.9 jit_solution(10571618521936133517)
XLA Ops:
  0.6 15.5 %left_factor.1 = (bf16[2048,1792]{1,0:T(8,128)(2,1)S(1)}, bf16[2048,1792]{1,0:T(8,128)(2,1)S(1)}, f32[128,2048]{1,0:T(8,128)S(1)}, f32[128,2048]{1,0:T(8,128)S(1)}) custom-call(f32[2048,1792]{1,0:T(8,128)} %m_hbm.1, bf16[2048,1792]{1,0:T(8,128)(2,1)} %g_hbm.1, f32[1792,256]{1,0:T(8,128)} %b_hbm.1), custom_call_target="tpu_custom_call" | custom-call | flops 5637144576 | bytes 22020096 | tf_op jit(solution)/shard_map/left_factor/pallas_call | solution.py:127
  16.2 0.5 collective-permute-start
  16.7 2.3 %collective-permute-done.b_ref = f32[128,2048]{1,0:T(8,128)S(1)} collective-permute-done((f32[128,2048]{1,0:T(8,128)S(1)}, f32[128,2048]{1,0:T(8,128)S(1)}, u32[]{:S(2)}, u32[]{:S(2)}) %collective-permute-start) | collective-permute-done | bytes 1048608 | tf_op jit(solution)/shard_map/ppermute | solution.py:486
  19.0 0.1 add_pieces.8
  19.1 0.1 fusion
  19.2 3.0 %collective-permute-start.1 = (f32[64,2048]{1,0:T(8,128)S(1)}, f32[64,2048]{1,0:T(8,128)S(1)}, u32[]{:S(2)}, u32[]{:S(2)}) collective-permute-start(f32[64,2048]{1,0:T(8,128)S(1)} %get-tuple-element.41), channel_id=1, source_target_pairs={{0,2},{1,5},{2,0},{3,7},{4,6},{5,1},{6,4},{7,3},{8,10},{9,13},{10,... | collective-permute-start | bytes 1572872 | tf_op jit(solution)/shard_map/ppermute | solution.py:486
  22.1 7.2 %collective-permute-done.1.b_ref = f32[64,2048]{1,0:T(8,128)S(1)} collective-permute-done((f32[64,2048]{1,0:T(8,128)S(1)}, f32[64,2048]{1,0:T(8,128)S(1)}, u32[]{:S(2)}, u32[]{:S(2)}) %collective-permute-start.1) | collective-permute-done | bytes 524320 | tf_op jit(solution)/shard_map/ppermute | solution.py:486
  29.3 0.1 add_pieces.9
  29.4 2.1 %collective-permute-start.2 = (f32[32,2048]{1,0:T(8,128)S(1)}, f32[32,2048]{1,0:T(8,128)S(1)}, u32[]{:S(2)}, u32[]{:S(2)}) collective-permute-start(f32[32,2048]{1,0:T(8,128)S(1)} %get-tuple-element.43), channel_id=1, source_target_pairs={{0,4},{1,3},{2,6},{3,1},{4,0},{5,7},{6,2},{7,5},{8,12},{9,11},{10,... | collective-permute-start | bytes 786440 | tf_op jit(solution)/shard_map/ppermute | solution.py:486
  31.6 4.4 %collective-permute-done.2.b_ref = f32[32,2048]{1,0:T(8,128)S(1)} collective-permute-done((f32[32,2048]{1,0:T(8,128)S(1)}, f32[32,2048]{1,0:T(8,128)S(1)}, u32[]{:S(2)}, u32[]{:S(2)}) %collective-permute-start.2) | collective-permute-done | bytes 262176 | tf_op jit(solution)/shard_map/ppermute | solution.py:486
  35.9 4.1 %collective-permute-start.3 = (f32[32,2048]{1,0:T(8,128)S(1)}, f32[32,2048]{1,0:T(8,128)S(1)}, u32[]{:S(2)}, u32[]{:S(2)}) collective-permute-start(f32[32,2048]{1,0:T(8,128)S(1)} %add_pieces.10.a_ref), channel_id=1, source_target_pairs={{0,12},{1,13},{2,14},{3,15},{4,8},{5,9},{6,10},{7,11},{8,4},{9,5},... | collective-permute-start | bytes 786440 | tf_op jit(solution)/shard_map/ppermute | solution.py:486
  40.0 5.0 %collective-permute-done.3.b_ref = f32[32,2048]{1,0:T(8,128)S(1)} collective-permute-done((f32[32,2048]{1,0:T(8,128)S(1)}, f32[32,2048]{1,0:T(8,128)S(1)}, u32[]{:S(2)}, u32[]{:S(2)}) %collective-permute-start.3) | collective-permute-done | bytes 262176 | tf_op jit(solution)/shard_map/ppermute | solution.py:486
  45.1 5.3 %collective-permute-start.4 = (f32[32,2048]{1,0:T(8,128)S(1)}, f32[32,2048]{1,0:T(8,128)S(1)}, u32[]{:S(2)}, u32[]{:S(2)}) collective-permute-start(f32[32,2048]{1,0:T(8,128)S(1)} %add_pieces.11.a_ref), channel_id=1, source_target_pairs={{0,4},{1,3},{2,6},{3,1},{4,0},{5,7},{6,2},{7,5},{8,12},{9,11},{10,... | collective-permute-start | bytes 786440 | tf_op jit(solution)/shard_map/ppermute | solution.py:486
  50.4 4.4 %collective-permute-done.4.b_ref = f32[32,2048]{1,0:T(8,128)S(1)} collective-permute-done((f32[32,2048]{1,0:T(8,128)S(1)}, f32[32,2048]{1,0:T(8,128)S(1)}, u32[]{:S(2)}, u32[]{:S(2)}) %collective-permute-start.4) | collective-permute-done | bytes 262176 | tf_op jit(solution)/shard_map/ppermute | solution.py:486
  54.8 0.0 copy-start.1
  54.8 0.0 copy-start
  54.8 1.6 %collective-permute-start.5 = (f32[64,2048]{1,0:T(8,128)S(1)}, f32[64,2048]{1,0:T(8,128)S(1)}, u32[]{:S(2)}, u32[]{:S(2)}) collective-permute-start(f32[64,2048]{1,0:T(8,128)S(1)} %join_pieces.5.a_ref), channel_id=1, source_target_pairs={{0,2},{1,5},{2,0},{3,7},{4,6},{5,1},{6,4},{7,3},{8,10},{9,13},{10,... | collective-permute-start | bytes 1572872 | tf_op jit(solution)/shard_map/ppermute | solution.py:486
  56.4 7.7 %collective-permute-done.5.b_ref = f32[64,2048]{1,0:T(8,128)S(1)} collective-permute-done((f32[64,2048]{1,0:T(8,128)S(1)}, f32[64,2048]{1,0:T(8,128)S(1)}, u32[]{:S(2)}, u32[]{:S(2)}) %collective-permute-start.5) | collective-permute-done | bytes 524320 | tf_op jit(solution)/shard_map/ppermute | solution.py:486
  64.0 0.1 join_pieces.6.refs_0_.a_ref
  64.1 0.1 collective-permute-start.6
  64.2 0.0 copy-done.1
  64.2 0.0 copy-done
  64.2 0.3 hadamard_signs.1.entries_ref
  64.5 2.3 %collective-permute-done.6.b_ref = f32[128,2048]{1,0:T(8,128)S(1)} collective-permute-done((f32[128,2048]{1,0:T(8,128)S(1)}, f32[128,2048]{1,0:T(8,128)S(1)}, u32[]{:S(2)}, u32[]{:S(2)}) %collective-permute-start.6) | collective-permute-done | bytes 1048608 | tf_op jit(solution)/shard_map/ppermute | solution.py:486
  66.8 1.2 sketch_rows.1
  68.0 1.5 %collective-permute-start.7 = (f32[24,256]{1,0:T(8,128)S(1)}, f32[24,256]{1,0:T(8,128)S(1)}, u32[]{:S(2)}, u32[]{:S(2)}) collective-permute-start(f32[24,256]{1,0:T(8,128)S(1)} %get-tuple-element.27.refs_0_), channel_id=1, source_target_pairs={{0,16},{16,0},{1,17},{17,1},{2,18},{18,2},{3,19},{19,3},{4,20},{20... | collective-permute-start | bytes 73736 | tf_op jit(solution)/shard_map/ppermute | solution.py:486
  69.5 2.3 %collective-permute-done.7.refs_1_ = f32[24,256]{1,0:T(8,128)S(1)} collective-permute-done((f32[24,256]{1,0:T(8,128)S(1)}, f32[24,256]{1,0:T(8,128)S(1)}, u32[]{:S(2)}, u32[]{:S(2)}) %collective-permute-start.7) | collective-permute-done | bytes 24608 | tf_op jit(solution)/shard_map/ppermute | solution.py:486
  71.9 3.7 %right_factor.2 = (f32[256,896]{1,0:T(8,128)S(1)}, f32[24,256]{1,0:T(8,128)S(1)}) custom-call(bf16[512,2048]{1,0:T(8,128)(2,1)S(1)} %get-tuple-element.26.left_ref.raw_ref, bf16[2048,1792]{1,0:T(8,128)(2,1)S(1)} %get-tuple-element.22.refs_0_.refs_1_.shi_ref, bf16[2048,1792]{1,0:T(8,128)(2,1)S(1)} %get-tuple-element.23.refs_1_.refs_2_.slo_ref, ...), custom_call_target="tpu_custom_call" | custom-call | flops 2818572288 | bytes 7340032 | tf_op jit(solution)/shard_map/right_factor/pallas_call | solution.py:251
  75.5 1.6 %collective-permute-start.12 = (f32[256,896]{1,0:T(8,128)S(1)}, f32[256,896]{1,0:T(8,128)S(1)}, u32[]{:S(2)}, u32[]{:S(2)}) collective-permute-start(f32[256,896]{1,0:T(8,128)S(1)} %get-tuple-element.32.refs_2_), channel_id=1, source_target_pairs={{0,16},{16,0},{1,17},{17,1},{2,18},{18,2},{3,19},{19,3},{4,20},{20... | collective-permute-start | bytes 2752520 | tf_op jit(solution)/shard_map/ppermute | solution.py:486
  77.1 3.5 %right_factor.3.refs_0_ = f32[256,896]{1,0:T(8,128)S(1)} custom-call(bf16[512,2048]{1,0:T(8,128)(2,1)S(1)} %get-tuple-element.26.left_ref.raw_ref, bf16[2048,1792]{1,0:T(8,128)(2,1)S(1)} %get-tuple-element.22.refs_0_.refs_1_.shi_ref, bf16[2048,1792]{1,0:T(8,128)(2,1)S(1)} %get-tuple-element.23.refs_1_.refs_2_.slo_ref), custom_call_target="tpu_custom_call" | custom-call | flops 2818572288 | bytes 7340032 | tf_op jit(solution)/shard_map/right_factor/pallas_call | solution.py:251
  80.6 0.6 collective-permute-start.13
  81.2 2.5 %collective-permute-start.8 = (f32[24,256]{1,0:T(8,128)S(1)}, f32[24,256]{1,0:T(8,128)S(1)}, u32[]{:S(2)}, u32[]{:S(2)}) collective-permute-start(f32[24,256]{1,0:T(8,128)S(1)} %get-tuple-element.28.a_ref), channel_id=1, source_target_pairs={{0,12},{1,13},{2,14},{3,15},{4,8},{5,9},{6,10},{7,11},{8,4},{9,5},... | collective-permute-start | bytes 73736 | tf_op jit(solution)/shard_map/ppermute | solution.py:486
  83.7 3.1 %collective-permute-done.8.b_ref = f32[24,256]{1,0:T(8,128)S(1)} collective-permute-done((f32[24,256]{1,0:T(8,128)S(1)}, f32[24,256]{1,0:T(8,128)S(1)}, u32[]{:S(2)}, u32[]{:S(2)}) %collective-permute-start.8) | collective-permute-done | bytes 24608 | tf_op jit(solution)/shard_map/ppermute | solution.py:486
  86.8 0.2 collective-permute-start.9
  87.1 4.4 %collective-permute-done.9.b_ref = f32[48,256]{1,0:T(8,128)S(1)} collective-permute-done((f32[48,256]{1,0:T(8,128)S(1)}, f32[48,256]{1,0:T(8,128)S(1)}, u32[]{:S(2)}, u32[]{:S(2)}) %collective-permute-start.9) | collective-permute-done | bytes 49184 | tf_op jit(solution)/shard_map/ppermute | solution.py:486
  91.5 1.6 %collective-permute-start.10 = (f32[96,256]{1,0:T(8,128)S(1)}, f32[96,256]{1,0:T(8,128)S(1)}, u32[]{:S(2)}, u32[]{:S(2)}) collective-permute-start(f32[96,256]{1,0:T(8,128)S(1)} %join_pieces.8.a_ref), channel_id=1, source_target_pairs={{0,2},{1,5},{2,0},{3,7},{4,6},{5,1},{6,4},{7,3},{8,10},{9,13},{10,... | collective-permute-start | bytes 294920 | tf_op jit(solution)/shard_map/ppermute | solution.py:486
  93.0 3.1 %collective-permute-done.10.b_ref = f32[96,256]{1,0:T(8,128)S(1)} collective-permute-done((f32[96,256]{1,0:T(8,128)S(1)}, f32[96,256]{1,0:T(8,128)S(1)}, u32[]{:S(2)}, u32[]{:S(2)}) %collective-permute-start.10) | collective-permute-done | bytes 98336 | tf_op jit(solution)/shard_map/ppermute | solution.py:486
  96.2 0.1 collective-permute-start.11
  96.2 1.4 collective-permute-done.11.b_ref
  97.7 13.0 %factor_inverse.1 = (bf16[256,256]{1,0:T(8,128)(2,1)S(1)}, bf16[256,256]{1,0:T(8,128)(2,1)S(1)}) custom-call(f32[192,256]{1,0:T(8,128)S(1)} %join_pieces.9.a_ref, f32[192,256]{1,0:T(8,128)S(1)} %collective-permute-done.11.b_ref), custom_call_target="tpu_custom_call" | custom-call | flops 1000000 | bytes 100000 | tf_op jit(solution)/shard_map/factor_inverse/pallas_call | solution.py:328
  110.6 3.1 %left_basis.1 = (bf16[2048,768]{1,0:T(8,128)(2,1)S(1)}, f32[2048,256]{1,0:T(8,128)S(1)}) custom-call(bf16[256,256]{1,0:T(8,128)(2,1)S(1)} %get-tuple-element.29.hi_ref, bf16[256,256]{1,0:T(8,128)(2,1)S(1)} %get-tuple-element.30.lo_ref, bf16[512,2048]{1,0:T(8,128)(2,1)S(1)} %get-tuple-element.26.left_ref.raw_ref), custom_call_target="tpu_custom_call" | custom-call | flops 1000000 | bytes 100000 | tf_op jit(solution)/shard_map/left_basis/pallas_call | solution.py:354
  113.8 0.0 collective-permute-done.12.refs_3_
  113.8 2.7 %collective-permute-done.13.refs_1_ = f32[256,896]{1,0:T(8,128)S(1)} collective-permute-done((f32[256,896]{1,0:T(8,128)S(1)}, f32[256,896]{1,0:T(8,128)S(1)}, u32[]{:S(2)}, u32[]{:S(2)}) %collective-permute-start.13) | collective-permute-done | bytes 917536 | tf_op jit(solution)/shard_map/ppermute | solution.py:486
  116.5 1.7 %right_rotate.1 = (f32[1792,256]{1,0:T(8,128)S(1)}, bf16[768,1792]{1,0:T(8,128)(2,1)S(1)}, f32[8,256]{1,0:T(8,128)S(1)}) custom-call(bf16[256,256]{1,0:T(8,128)(2,1)S(1)} %get-tuple-element.29.hi_ref, bf16[256,256]{1,0:T(8,128)(2,1)S(1)} %get-tuple-element.30.lo_ref, f32[256,896]{1,0:T(8,128)S(1)} %right_factor.3.refs_0_, ...), custom_call_target="tpu_custom_call" | custom-call | flops 704643072 | bytes 7340032 | tf_op jit(solution)/shard_map/right_rotate/pallas_call | solution.py:402
  118.2 0.0 collective-permute-start.14
  118.2 3.1 %momentum_update.4.refs_0_ = f32[2048,1792]{1,0:T(8,128)} custom-call(bf16[2048,1792]{1,0:T(8,128)(2,1)S(1)} %get-tuple-element.22.refs_0_.refs_1_.shi_ref, bf16[2048,1792]{1,0:T(8,128)(2,1)S(1)} %get-tuple-element.23.refs_1_.refs_2_.slo_ref, bf16[2048,768]{1,0:T(8,128)(2,1)S(1)} %get-tuple-element.33.left_ref, bf16[768,1792]{1,0:T(8,128)(2,1)S(1)} %get-tuple-element.35.terms_ref), custom_call_target="tpu_custom_call" | custom-call | flops 1409286144 | bytes 3670016 | tf_op jit(solution)/shard_map/momentum_update/pallas_call | solution.py:436
  121.4 0.0 collective-permute-done.14.b_ref
  121.4 1.5 %collective-permute-start.15 = (f32[8,256]{1,0:T(8,128)S(1)}, f32[8,256]{1,0:T(8,128)S(1)}, u32[]{:S(2)}, u32[]{:S(2)}) collective-permute-start(f32[8,256]{1,0:T(8,128)S(1)} %add_pieces.12.a_ref), channel_id=1, source_target_pairs={{0,2},{1,5},{2,0},{3,7},{4,6},{5,1},{6,4},{7,3},{8,10},{9,13},{10,... | collective-permute-start | bytes 24584 | tf_op jit(solution)/shard_map/ppermute | solution.py:486
  122.9 3.1 %momentum_update.5.refs_0_ = f32[2048,1792]{1,0:T(8,128)} custom-call(bf16[2048,1792]{1,0:T(8,128)(2,1)S(1)} %get-tuple-element.22.refs_0_.refs_1_.shi_ref, bf16[2048,1792]{1,0:T(8,128)(2,1)S(1)} %get-tuple-element.23.refs_1_.refs_2_.slo_ref, bf16[2048,768]{1,0:T(8,128)(2,1)S(1)} %get-tuple-element.33.left_ref, ...), custom_call_target="tpu_custom_call", output_to_operand_aliasing={{}: (4, {})} | custom-call | flops 1409286144 | bytes 3670016 | tf_op jit(solution)/shard_map/momentum_update/pallas_call | solution.py:436
  126.0 0.0 collective-permute-done.15.b_ref
  126.0 2.0 %collective-permute-start.16 = (f32[8,256]{1,0:T(8,128)S(1)}, f32[8,256]{1,0:T(8,128)S(1)}, u32[]{:S(2)}, u32[]{:S(2)}) collective-permute-start(f32[8,256]{1,0:T(8,128)S(1)} %add_pieces.13.a_ref), channel_id=1, source_target_pairs={{0,4},{1,3},{2,6},{3,1},{4,0},{5,7},{6,2},{7,5},{8,12},{9,11},{10,... | collective-permute-start | bytes 24584 | tf_op jit(solution)/shard_map/ppermute | solution.py:486
  128.0 3.1 %momentum_update.6.refs_0_ = f32[2048,1792]{1,0:T(8,128)} custom-call(bf16[2048,1792]{1,0:T(8,128)(2,1)S(1)} %get-tuple-element.22.refs_0_.refs_1_.shi_ref, bf16[2048,1792]{1,0:T(8,128)(2,1)S(1)} %get-tuple-element.23.refs_1_.refs_2_.slo_ref, bf16[2048,768]{1,0:T(8,128)(2,1)S(1)} %get-tuple-element.33.left_ref, ...), custom_call_target="tpu_custom_call", output_to_operand_aliasing={{}: (4, {})} | custom-call | flops 1409286144 | bytes 3670016 | tf_op jit(solution)/shard_map/momentum_update/pallas_call | solution.py:436
  131.1 0.0 collective-permute-done.16.b_ref
  131.2 2.8 %collective-permute-start.17 = (f32[8,256]{1,0:T(8,128)S(1)}, f32[8,256]{1,0:T(8,128)S(1)}, u32[]{:S(2)}, u32[]{:S(2)}) collective-permute-start(f32[8,256]{1,0:T(8,128)S(1)} %add_pieces.14.a_ref), channel_id=1, source_target_pairs={{0,12},{1,13},{2,14},{3,15},{4,8},{5,9},{6,10},{7,11},{8,4},{9,5},... | collective-permute-start | bytes 24584 | tf_op jit(solution)/shard_map/ppermute | solution.py:486
  134.0 3.1 %momentum_update.7 = f32[2048,1792]{1,0:T(8,128)} custom-call(bf16[2048,1792]{1,0:T(8,128)(2,1)S(1)} %get-tuple-element.22.refs_0_.refs_1_.shi_ref, bf16[2048,1792]{1,0:T(8,128)(2,1)S(1)} %get-tuple-element.23.refs_1_.refs_2_.slo_ref, bf16[2048,768]{1,0:T(8,128)(2,1)S(1)} %get-tuple-element.33.left_ref, ...), custom_call_target="tpu_custom_call", output_to_operand_aliasing={{}: (4, {})} | custom-call | flops 1409286144 | bytes 3670016 | tf_op jit(solution)/shard_map/momentum_update/pallas_call | solution.py:436
  137.1 0.0 collective-permute-done.17.b_ref
  137.1 7.9 %update_basis.1 = (bf16[2048,1792]{1,0:T(8,128)(2,1)}, f32[1792,256]{1,0:T(8,128)}) custom-call(f32[1792,256]{1,0:T(8,128)S(1)} %get-tuple-element.36.turned_ref, f32[8,256]{1,0:T(8,128)S(1)} %add_pieces.15.squares_ref, f32[2048,256]{1,0:T(8,128)S(1)} %get-tuple-element.38.left_ref, bf16[768,1792]{1,0:T(8,128)(2,1)S(1)} %get-tuple-element.35.terms_ref), custom_call_target="tpu_custom_call" | custom-call | flops 5637144576 | bytes 7340032 | tf_op jit(solution)/shard_map/update_basis/pallas_call | solution.py:467
  (12 shorter events, 0.2 us)
Async XLA Ops:
  16.2 2.8 %collective-permute-start = (f32[128,2048]{1,0:T(8,128)S(1)}, f32[128,2048]{1,0:T(8,128)S(1)}, u32[]{:S(2)}, u32[]{:S(2)}) collective-permute-start(f32[128,2048]{1,0:T(8,128)S(1)} %get-tuple-element.25), channel_id=1, source_target_pairs={{0,1},{1,0},{2,3},{3,2},{4,5},{5,4},{6,7},{7,6},{8,9},{9,8},{10,11... | collective-permute-start | bytes 3145736 | tf_op jit(solution)/shard_map/ppermute | solution.py:486
  19.2 10.1 %collective-permute-start.1 = (f32[64,2048]{1,0:T(8,128)S(1)}, f32[64,2048]{1,0:T(8,128)S(1)}, u32[]{:S(2)}, u32[]{:S(2)}) collective-permute-start(f32[64,2048]{1,0:T(8,128)S(1)} %get-tuple-element.41), channel_id=1, source_target_pairs={{0,2},{1,5},{2,0},{3,7},{4,6},{5,1},{6,4},{7,3},{8,10},{9,13},{10,... | collective-permute-start | bytes 1572872 | tf_op jit(solution)/shard_map/ppermute | solution.py:486
  29.4 6.5 %collective-permute-start.2 = (f32[32,2048]{1,0:T(8,128)S(1)}, f32[32,2048]{1,0:T(8,128)S(1)}, u32[]{:S(2)}, u32[]{:S(2)}) collective-permute-start(f32[32,2048]{1,0:T(8,128)S(1)} %get-tuple-element.43), channel_id=1, source_target_pairs={{0,4},{1,3},{2,6},{3,1},{4,0},{5,7},{6,2},{7,5},{8,12},{9,11},{10,... | collective-permute-start | bytes 786440 | tf_op jit(solution)/shard_map/ppermute | solution.py:486
  35.9 9.1 %collective-permute-start.3 = (f32[32,2048]{1,0:T(8,128)S(1)}, f32[32,2048]{1,0:T(8,128)S(1)}, u32[]{:S(2)}, u32[]{:S(2)}) collective-permute-start(f32[32,2048]{1,0:T(8,128)S(1)} %add_pieces.10.a_ref), channel_id=1, source_target_pairs={{0,12},{1,13},{2,14},{3,15},{4,8},{5,9},{6,10},{7,11},{8,4},{9,5},... | collective-permute-start | bytes 786440 | tf_op jit(solution)/shard_map/ppermute | solution.py:486
  45.1 9.6 %collective-permute-start.4 = (f32[32,2048]{1,0:T(8,128)S(1)}, f32[32,2048]{1,0:T(8,128)S(1)}, u32[]{:S(2)}, u32[]{:S(2)}) collective-permute-start(f32[32,2048]{1,0:T(8,128)S(1)} %add_pieces.11.a_ref), channel_id=1, source_target_pairs={{0,4},{1,3},{2,6},{3,1},{4,0},{5,7},{6,2},{7,5},{8,12},{9,11},{10,... | collective-permute-start | bytes 786440 | tf_op jit(solution)/shard_map/ppermute | solution.py:486
  54.8 9.4 %copy-start.1 = (s32[384]{0:T(512)S(1)}, s32[384]{0:T(512)}, u32[]{:S(2)}) copy-start(s32[384]{0:T(512)} %param.9) | copy-start | bytes 4612
  54.8 9.4 %copy-start = (s32[4096]{0:T(1024)S(1)}, s32[4096]{0:T(1024)}, u32[]{:S(2)}) copy-start(s32[4096]{0:T(1024)} %param.8) | copy-start | bytes 49156
  54.8 9.2 %collective-permute-start.5 = (f32[64,2048]{1,0:T(8,128)S(1)}, f32[64,2048]{1,0:T(8,128)S(1)}, u32[]{:S(2)}, u32[]{:S(2)}) collective-permute-start(f32[64,2048]{1,0:T(8,128)S(1)} %join_pieces.5.a_ref), channel_id=1, source_target_pairs={{0,2},{1,5},{2,0},{3,7},{4,6},{5,1},{6,4},{7,3},{8,10},{9,13},{10,... | collective-permute-start | bytes 1572872 | tf_op jit(solution)/shard_map/ppermute | solution.py:486
  64.1 2.7 %collective-permute-start.6 = (f32[128,2048]{1,0:T(8,128)S(1)}, f32[128,2048]{1,0:T(8,128)S(1)}, u32[]{:S(2)}, u32[]{:S(2)}) collective-permute-start(f32[128,2048]{1,0:T(8,128)S(1)} %join_pieces.6.refs_0_.a_ref), channel_id=1, source_target_pairs={{0,1},{1,0},{2,3},{3,2},{4,5},{5,4},{6,7},{7,6},{8,9},{9,8},{10,11... | collective-permute-start | bytes 3145736 | tf_op jit(solution)/shard_map/ppermute | solution.py:486
  68.0 3.9 %collective-permute-start.7 = (f32[24,256]{1,0:T(8,128)S(1)}, f32[24,256]{1,0:T(8,128)S(1)}, u32[]{:S(2)}, u32[]{:S(2)}) collective-permute-start(f32[24,256]{1,0:T(8,128)S(1)} %get-tuple-element.27.refs_0_), channel_id=1, source_target_pairs={{0,16},{16,0},{1,17},{17,1},{2,18},{18,2},{3,19},{19,3},{4,20},{20... | collective-permute-start | bytes 73736 | tf_op jit(solution)/shard_map/ppermute | solution.py:486
  75.5 38.2 %collective-permute-start.12 = (f32[256,896]{1,0:T(8,128)S(1)}, f32[256,896]{1,0:T(8,128)S(1)}, u32[]{:S(2)}, u32[]{:S(2)}) collective-permute-start(f32[256,896]{1,0:T(8,128)S(1)} %get-tuple-element.32.refs_2_), channel_id=1, source_target_pairs={{0,16},{16,0},{1,17},{17,1},{2,18},{18,2},{3,19},{19,3},{4,20},{20... | collective-permute-start | bytes 2752520 | tf_op jit(solution)/shard_map/ppermute | solution.py:486
  80.6 35.9 %collective-permute-start.13 = (f32[256,896]{1,0:T(8,128)S(1)}, f32[256,896]{1,0:T(8,128)S(1)}, u32[]{:S(2)}, u32[]{:S(2)}) collective-permute-start(f32[256,896]{1,0:T(8,128)S(1)} %right_factor.3.refs_0_), channel_id=1, source_target_pairs={{0,16},{16,0},{1,17},{17,1},{2,18},{18,2},{3,19},{19,3},{4,20},{20... | collective-permute-start | bytes 2752520 | tf_op jit(solution)/shard_map/ppermute | solution.py:486
  81.2 5.6 %collective-permute-start.8 = (f32[24,256]{1,0:T(8,128)S(1)}, f32[24,256]{1,0:T(8,128)S(1)}, u32[]{:S(2)}, u32[]{:S(2)}) collective-permute-start(f32[24,256]{1,0:T(8,128)S(1)} %get-tuple-element.28.a_ref), channel_id=1, source_target_pairs={{0,12},{1,13},{2,14},{3,15},{4,8},{5,9},{6,10},{7,11},{8,4},{9,5},... | collective-permute-start | bytes 73736 | tf_op jit(solution)/shard_map/ppermute | solution.py:486
  86.8 4.6 %collective-permute-start.9 = (f32[48,256]{1,0:T(8,128)S(1)}, f32[48,256]{1,0:T(8,128)S(1)}, u32[]{:S(2)}, u32[]{:S(2)}) collective-permute-start(f32[48,256]{1,0:T(8,128)S(1)} %join_pieces.7.a_ref), channel_id=1, source_target_pairs={{0,4},{1,3},{2,6},{3,1},{4,0},{5,7},{6,2},{7,5},{8,12},{9,11},{10,... | collective-permute-start | bytes 147464 | tf_op jit(solution)/shard_map/ppermute | solution.py:486
  91.5 4.7 %collective-permute-start.10 = (f32[96,256]{1,0:T(8,128)S(1)}, f32[96,256]{1,0:T(8,128)S(1)}, u32[]{:S(2)}, u32[]{:S(2)}) collective-permute-start(f32[96,256]{1,0:T(8,128)S(1)} %join_pieces.8.a_ref), channel_id=1, source_target_pairs={{0,2},{1,5},{2,0},{3,7},{4,6},{5,1},{6,4},{7,3},{8,10},{9,13},{10,... | collective-permute-start | bytes 294920 | tf_op jit(solution)/shard_map/ppermute | solution.py:486
  96.2 1.5 %collective-permute-start.11 = (f32[192,256]{1,0:T(8,128)S(1)}, f32[192,256]{1,0:T(8,128)S(1)}, u32[]{:S(2)}, u32[]{:S(2)}) collective-permute-start(f32[192,256]{1,0:T(8,128)S(1)} %join_pieces.9.a_ref), channel_id=1, source_target_pairs={{0,1},{1,0},{2,3},{3,2},{4,5},{5,4},{6,7},{7,6},{8,9},{9,8},{10,11... | collective-permute-start | bytes 589832 | tf_op jit(solution)/shard_map/ppermute | solution.py:486
  118.2 3.2 %collective-permute-start.14 = (f32[8,256]{1,0:T(8,128)S(1)}, f32[8,256]{1,0:T(8,128)S(1)}, u32[]{:S(2)}, u32[]{:S(2)}) collective-permute-start(f32[8,256]{1,0:T(8,128)S(1)} %get-tuple-element.37.a_ref), channel_id=1, source_target_pairs={{0,1},{1,0},{2,3},{3,2},{4,5},{5,4},{6,7},{7,6},{8,9},{9,8},{10,11... | collective-permute-start | bytes 24584 | tf_op jit(solution)/shard_map/ppermute | solution.py:486
  121.4 4.6 %collective-permute-start.15 = (f32[8,256]{1,0:T(8,128)S(1)}, f32[8,256]{1,0:T(8,128)S(1)}, u32[]{:S(2)}, u32[]{:S(2)}) collective-permute-start(f32[8,256]{1,0:T(8,128)S(1)} %add_pieces.12.a_ref), channel_id=1, source_target_pairs={{0,2},{1,5},{2,0},{3,7},{4,6},{5,1},{6,4},{7,3},{8,10},{9,13},{10,... | collective-permute-start | bytes 24584 | tf_op jit(solution)/shard_map/ppermute | solution.py:486
  126.0 5.1 %collective-permute-start.16 = (f32[8,256]{1,0:T(8,128)S(1)}, f32[8,256]{1,0:T(8,128)S(1)}, u32[]{:S(2)}, u32[]{:S(2)}) collective-permute-start(f32[8,256]{1,0:T(8,128)S(1)} %add_pieces.13.a_ref), channel_id=1, source_target_pairs={{0,4},{1,3},{2,6},{3,1},{4,0},{5,7},{6,2},{7,5},{8,12},{9,11},{10,... | collective-permute-start | bytes 24584 | tf_op jit(solution)/shard_map/ppermute | solution.py:486
  131.2 5.9 %collective-permute-start.17 = (f32[8,256]{1,0:T(8,128)S(1)}, f32[8,256]{1,0:T(8,128)S(1)}, u32[]{:S(2)}, u32[]{:S(2)}) collective-permute-start(f32[8,256]{1,0:T(8,128)S(1)} %add_pieces.14.a_ref), channel_id=1, source_target_pairs={{0,12},{1,13},{2,14},{3,15},{4,8},{5,9},{6,10},{7,11},{8,4},{9,5},... | collective-permute-start | bytes 24584 | tf_op jit(solution)/shard_map/ppermute | solution.py:486

commit v5 on v4

--- a/solution.py
+++ b/solution.py
@@ -508,6 +508,26 @@
     )(a, b, *(in_space(x, pltpu.VMEM) for x in held))
 
 
+def halves_kernel(a_ref, b_ref, *refs):
+    send_ref, keep_ref = refs[-2:]
+    h = send_ref.shape[0]
+    send_ref[...] = a_ref[h:, :] + b_ref[h:, :]
+    keep_ref[...] = a_ref[:h, :] + b_ref[:h, :]
+
+
+def halves_call(a, b, held):
+    half = jax.ShapeDtypeStruct((a.shape[0] // 2, a.shape[1]), a.dtype)
+    return pl.pallas_call(
+        halves_kernel,
+        in_specs=[WHOLE] * (2 + len(held)),
+        out_specs=[WHOLE] * 2,
+        out_shape=[half, half],
+        compiler_params=pltpu.CompilerParams(vmem_limit_bytes=24 * MIB),
+        cost_estimate=cost(a.size, 12 * a.size),
+        name="add_halves",
+    )(a, b, *(in_space(x, pltpu.VMEM) for x in held))
+
+
 def join_kernel(a_ref, b_ref, *refs):
     half = a_ref.shape[0]
     refs[-1][:half, :] = a_ref[...]
@@ -531,9 +551,7 @@
     core, first, second, third = steps
     got = swap(send, "wide", core)
     for pairs in (first, second):
-        h = keep.shape[0] // 2
-        total = add_call(keep, got, held)
-        send, keep = total[h:], total[:h]
+        send, keep = halves_call(keep, got, held)
         got = swap(send, "wide", pairs)
     mine = add_call(keep, got, held)
     mine = add_call(mine, swap(mine, "wide", third), held)

time: 145 us -> 145 us (level)
  no operation moved by 1% of the time
where the time goes in v5:
time: 145 us
  Pallas kernels  62.7 us (43%)
  waiting for transfers between devices  50.2 us (35%)
  starting transfers between devices  31.1 us (21%)
    ppermute x18, waiting for transfers between devices, swap(): return lax.ppermute(x, axis, pairs)  50.2 us
    ppermute x18, starting transfers between devices, swap(): return lax.ppermute(x, axis, pairs)  31.1 us
    pallas_call x1, Pallas kernels, left_call(): pl.pallas_call(functools.partial(left_kernel, fast), in_specs=[hbm] * 3,...  15.5 us
    pallas_call x1, Pallas kernels, factor_call(): pl.pallas_call(factor_kernel, in_specs=[WHOLE] * 2, out_specs=[WHOLE] * 2...  13 us
    pallas_call x4, Pallas kernels, momentum_call(): pl.pallas_call(functools.partial(momentum_kernel, first), grid=(count,),...  12.5 us
    pallas_call x1, Pallas kernels, update_call(): pl.pallas_call(functools.partial(update_kernel, factor / (1.0 - decay_mu)...  7.86 us
    pallas_call x2, Pallas kernels, right_call(): pl.pallas_call(functools.partial(right_kernel, first), in_specs=[WHOLE] *...  7.18 us
    pallas_call x1, Pallas kernels, basis_call(): pl.pallas_call(basis_kernel, grid=(rows // tile,), in_specs=[inv_spec] *...  3.13 us
  transfers between devices with their start and end apart: 18, of which 13 were waited for; matrix products, arithmetic and copies ran while one was open for 0% of the time, Pallas kernels for 22%

profile of v5, /device:TPU:0, one launch (start us, length us, event | category | flops | bytes accessed | tf_op | source)
XLA Modules:
  0.0 144.8 jit_solution(14710569879425658299)
XLA Ops:
  0.6 15.5 %left_factor.1 = (bf16[2048,1792]{1,0:T(8,128)(2,1)S(1)}, bf16[2048,1792]{1,0:T(8,128)(2,1)S(1)}, f32[128,2048]{1,0:T(8,128)S(1)}, f32[128,2048]{1,0:T(8,128)S(1)}) custom-call(f32[2048,1792]{1,0:T(8,128)} %m_hbm.1, bf16[2048,1792]{1,0:T(8,128)(2,1)} %g_hbm.1, f32[1792,256]{1,0:T(8,128)} %b_hbm.1), custom_call_target="tpu_custom_call" | custom-call | flops 5637144576 | bytes 22020096 | tf_op jit(solution)/shard_map/left_factor/pallas_call | solution.py:127
  16.2 0.5 collective-permute-start
  16.7 2.3 %collective-permute-done.b_ref = f32[128,2048]{1,0:T(8,128)S(1)} collective-permute-done((f32[128,2048]{1,0:T(8,128)S(1)}, f32[128,2048]{1,0:T(8,128)S(1)}, u32[]{:S(2)}, u32[]{:S(2)}) %collective-permute-start) | collective-permute-done | bytes 1048608 | tf_op jit(solution)/shard_map/ppermute | solution.py:486
  19.0 0.1 add_halves.2
  19.1 3.0 %collective-permute-start.1 = (f32[64,2048]{1,0:T(8,128)S(1)}, f32[64,2048]{1,0:T(8,128)S(1)}, u32[]{:S(2)}, u32[]{:S(2)}) collective-permute-start(f32[64,2048]{1,0:T(8,128)S(1)} %get-tuple-element.31), channel_id=1, source_target_pairs={{0,2},{1,5},{2,0},{3,7},{4,6},{5,1},{6,4},{7,3},{8,10},{9,13},{10,... | collective-permute-start | bytes 1572872 | tf_op jit(solution)/shard_map/ppermute | solution.py:486
  22.0 7.2 %collective-permute-done.1.b_ref = f32[64,2048]{1,0:T(8,128)S(1)} collective-permute-done((f32[64,2048]{1,0:T(8,128)S(1)}, f32[64,2048]{1,0:T(8,128)S(1)}, u32[]{:S(2)}, u32[]{:S(2)}) %collective-permute-start.1) | collective-permute-done | bytes 524320 | tf_op jit(solution)/shard_map/ppermute | solution.py:486
  29.2 0.1 add_halves.3
  29.3 2.1 %collective-permute-start.2 = (f32[32,2048]{1,0:T(8,128)S(1)}, f32[32,2048]{1,0:T(8,128)S(1)}, u32[]{:S(2)}, u32[]{:S(2)}) collective-permute-start(f32[32,2048]{1,0:T(8,128)S(1)} %get-tuple-element.33), channel_id=1, source_target_pairs={{0,4},{1,3},{2,6},{3,1},{4,0},{5,7},{6,2},{7,5},{8,12},{9,11},{10,... | collective-permute-start | bytes 786440 | tf_op jit(solution)/shard_map/ppermute | solution.py:486
  31.4 4.4 %collective-permute-done.2.b_ref = f32[32,2048]{1,0:T(8,128)S(1)} collective-permute-done((f32[32,2048]{1,0:T(8,128)S(1)}, f32[32,2048]{1,0:T(8,128)S(1)}, u32[]{:S(2)}, u32[]{:S(2)}) %collective-permute-start.2) | collective-permute-done | bytes 262176 | tf_op jit(solution)/shard_map/ppermute | solution.py:486
  35.8 4.1 %collective-permute-start.3 = (f32[32,2048]{1,0:T(8,128)S(1)}, f32[32,2048]{1,0:T(8,128)S(1)}, u32[]{:S(2)}, u32[]{:S(2)}) collective-permute-start(f32[32,2048]{1,0:T(8,128)S(1)} %add_pieces.6.a_ref), channel_id=1, source_target_pairs={{0,12},{1,13},{2,14},{3,15},{4,8},{5,9},{6,10},{7,11},{8,4},{9,5},... | collective-permute-start | bytes 786440 | tf_op jit(solution)/shard_map/ppermute | solution.py:486
  39.9 5.0 %collective-permute-done.3.b_ref = f32[32,2048]{1,0:T(8,128)S(1)} collective-permute-done((f32[32,2048]{1,0:T(8,128)S(1)}, f32[32,2048]{1,0:T(8,128)S(1)}, u32[]{:S(2)}, u32[]{:S(2)}) %collective-permute-start.3) | collective-permute-done | bytes 262176 | tf_op jit(solution)/shard_map/ppermute | solution.py:486
  44.9 5.3 %collective-permute-start.4 = (f32[32,2048]{1,0:T(8,128)S(1)}, f32[32,2048]{1,0:T(8,128)S(1)}, u32[]{:S(2)}, u32[]{:S(2)}) collective-permute-start(f32[32,2048]{1,0:T(8,128)S(1)} %add_pieces.7.a_ref), channel_id=1, source_target_pairs={{0,4},{1,3},{2,6},{3,1},{4,0},{5,7},{6,2},{7,5},{8,12},{9,11},{10,... | collective-permute-start | bytes 786440 | tf_op jit(solution)/shard_map/ppermute | solution.py:486
  50.2 4.4 %collective-permute-done.4.b_ref = f32[32,2048]{1,0:T(8,128)S(1)} collective-permute-done((f32[32,2048]{1,0:T(8,128)S(1)}, f32[32,2048]{1,0:T(8,128)S(1)}, u32[]{:S(2)}, u32[]{:S(2)}) %collective-permute-start.4) | collective-permute-done | bytes 262176 | tf_op jit(solution)/shard_map/ppermute | solution.py:486
  54.6 0.0 copy-start.1
  54.6 0.0 copy-start
  54.6 1.6 %collective-permute-start.5 = (f32[64,2048]{1,0:T(8,128)S(1)}, f32[64,2048]{1,0:T(8,128)S(1)}, u32[]{:S(2)}, u32[]{:S(2)}) collective-permute-start(f32[64,2048]{1,0:T(8,128)S(1)} %join_pieces.5.a_ref), channel_id=1, source_target_pairs={{0,2},{1,5},{2,0},{3,7},{4,6},{5,1},{6,4},{7,3},{8,10},{9,13},{10,... | collective-permute-start | bytes 1572872 | tf_op jit(solution)/shard_map/ppermute | solution.py:486
  56.2 7.7 %collective-permute-done.5.b_ref = f32[64,2048]{1,0:T(8,128)S(1)} collective-permute-done((f32[64,2048]{1,0:T(8,128)S(1)}, f32[64,2048]{1,0:T(8,128)S(1)}, u32[]{:S(2)}, u32[]{:S(2)}) %collective-permute-start.5) | collective-permute-done | bytes 524320 | tf_op jit(solution)/shard_map/ppermute | solution.py:486
  63.9 0.1 join_pieces.6.refs_0_.a_ref
  64.0 0.1 collective-permute-start.6
  64.0 0.0 copy-done.1
  64.1 0.0 copy-done
  64.1 0.3 hadamard_signs.1.entries_ref
  64.4 2.3 %collective-permute-done.6.b_ref = f32[128,2048]{1,0:T(8,128)S(1)} collective-permute-done((f32[128,2048]{1,0:T(8,128)S(1)}, f32[128,2048]{1,0:T(8,128)S(1)}, u32[]{:S(2)}, u32[]{:S(2)}) %collective-permute-start.6) | collective-permute-done | bytes 1048608 | tf_op jit(solution)/shard_map/ppermute | solution.py:486
  66.7 1.2 sketch_rows.1
  67.9 1.5 %collective-permute-start.7 = (f32[24,256]{1,0:T(8,128)S(1)}, f32[24,256]{1,0:T(8,128)S(1)}, u32[]{:S(2)}, u32[]{:S(2)}) collective-permute-start(f32[24,256]{1,0:T(8,128)S(1)} %get-tuple-element.35.refs_0_), channel_id=1, source_target_pairs={{0,16},{16,0},{1,17},{17,1},{2,18},{18,2},{3,19},{19,3},{4,20},{20... | collective-permute-start | bytes 73736 | tf_op jit(solution)/shard_map/ppermute | solution.py:486
  69.4 2.3 %collective-permute-done.7.refs_1_ = f32[24,256]{1,0:T(8,128)S(1)} collective-permute-done((f32[24,256]{1,0:T(8,128)S(1)}, f32[24,256]{1,0:T(8,128)S(1)}, u32[]{:S(2)}, u32[]{:S(2)}) %collective-permute-start.7) | collective-permute-done | bytes 24608 | tf_op jit(solution)/shard_map/ppermute | solution.py:486
  71.7 3.7 %right_factor.2 = (f32[256,896]{1,0:T(8,128)S(1)}, f32[24,256]{1,0:T(8,128)S(1)}) custom-call(bf16[512,2048]{1,0:T(8,128)(2,1)S(1)} %get-tuple-element.34.left_ref.raw_ref, bf16[2048,1792]{1,0:T(8,128)(2,1)S(1)} %get-tuple-element.26.refs_0_.refs_1_.shi_ref, bf16[2048,1792]{1,0:T(8,128)(2,1)S(1)} %get-tuple-element.27.refs_1_.refs_2_.slo_ref, ...), custom_call_target="tpu_custom_call" | custom-call | flops 2818572288 | bytes 7340032 | tf_op jit(solution)/shard_map/right_factor/pallas_call | solution.py:251
  75.4 1.6 %collective-permute-start.12 = (f32[256,896]{1,0:T(8,128)S(1)}, f32[256,896]{1,0:T(8,128)S(1)}, u32[]{:S(2)}, u32[]{:S(2)}) collective-permute-start(f32[256,896]{1,0:T(8,128)S(1)} %get-tuple-element.40.refs_2_), channel_id=1, source_target_pairs={{0,16},{16,0},{1,17},{17,1},{2,18},{18,2},{3,19},{19,3},{4,20},{20... | collective-permute-start | bytes 2752520 | tf_op jit(solution)/shard_map/ppermute | solution.py:486
  77.0 3.5 %right_factor.3.refs_0_ = f32[256,896]{1,0:T(8,128)S(1)} custom-call(bf16[512,2048]{1,0:T(8,128)(2,1)S(1)} %get-tuple-element.34.left_ref.raw_ref, bf16[2048,1792]{1,0:T(8,128)(2,1)S(1)} %get-tuple-element.26.refs_0_.refs_1_.shi_ref, bf16[2048,1792]{1,0:T(8,128)(2,1)S(1)} %get-tuple-element.27.refs_1_.refs_2_.slo_ref), custom_call_target="tpu_custom_call" | custom-call | flops 2818572288 | bytes 7340032 | tf_op jit(solution)/shard_map/right_factor/pallas_call | solution.py:251
  80.5 0.6 collective-permute-start.13
  81.1 2.5 %collective-permute-start.8 = (f32[24,256]{1,0:T(8,128)S(1)}, f32[24,256]{1,0:T(8,128)S(1)}, u32[]{:S(2)}, u32[]{:S(2)}) collective-permute-start(f32[24,256]{1,0:T(8,128)S(1)} %get-tuple-element.36.a_ref), channel_id=1, source_target_pairs={{0,12},{1,13},{2,14},{3,15},{4,8},{5,9},{6,10},{7,11},{8,4},{9,5},... | collective-permute-start | bytes 73736 | tf_op jit(solution)/shard_map/ppermute | solution.py:486
  83.6 3.1 %collective-permute-done.8.b_ref = f32[24,256]{1,0:T(8,128)S(1)} collective-permute-done((f32[24,256]{1,0:T(8,128)S(1)}, f32[24,256]{1,0:T(8,128)S(1)}, u32[]{:S(2)}, u32[]{:S(2)}) %collective-permute-start.8) | collective-permute-done | bytes 24608 | tf_op jit(solution)/shard_map/ppermute | solution.py:486
  86.7 0.2 collective-permute-start.9
  86.9 4.4 %collective-permute-done.9.b_ref = f32[48,256]{1,0:T(8,128)S(1)} collective-permute-done((f32[48,256]{1,0:T(8,128)S(1)}, f32[48,256]{1,0:T(8,128)S(1)}, u32[]{:S(2)}, u32[]{:S(2)}) %collective-permute-start.9) | collective-permute-done | bytes 49184 | tf_op jit(solution)/shard_map/ppermute | solution.py:486
  91.3 1.6 %collective-permute-start.10 = (f32[96,256]{1,0:T(8,128)S(1)}, f32[96,256]{1,0:T(8,128)S(1)}, u32[]{:S(2)}, u32[]{:S(2)}) collective-permute-start(f32[96,256]{1,0:T(8,128)S(1)} %join_pieces.8.a_ref), channel_id=1, source_target_pairs={{0,2},{1,5},{2,0},{3,7},{4,6},{5,1},{6,4},{7,3},{8,10},{9,13},{10,... | collective-permute-start | bytes 294920 | tf_op jit(solution)/shard_map/ppermute | solution.py:486
  92.9 3.1 %collective-permute-done.10.b_ref = f32[96,256]{1,0:T(8,128)S(1)} collective-permute-done((f32[96,256]{1,0:T(8,128)S(1)}, f32[96,256]{1,0:T(8,128)S(1)}, u32[]{:S(2)}, u32[]{:S(2)}) %collective-permute-start.10) | collective-permute-done | bytes 98336 | tf_op jit(solution)/shard_map/ppermute | solution.py:486
  96.0 0.1 collective-permute-start.11
  96.1 1.4 collective-permute-done.11.b_ref
  97.5 13.0 %factor_inverse.1 = (bf16[256,256]{1,0:T(8,128)(2,1)S(1)}, bf16[256,256]{1,0:T(8,128)(2,1)S(1)}) custom-call(f32[192,256]{1,0:T(8,128)S(1)} %join_pieces.9.a_ref, f32[192,256]{1,0:T(8,128)S(1)} %collective-permute-done.11.b_ref), custom_call_target="tpu_custom_call" | custom-call | flops 1000000 | bytes 100000 | tf_op jit(solution)/shard_map/factor_inverse/pallas_call | solution.py:328
  110.5 3.1 %left_basis.1 = (bf16[2048,768]{1,0:T(8,128)(2,1)S(1)}, f32[2048,256]{1,0:T(8,128)S(1)}) custom-call(bf16[256,256]{1,0:T(8,128)(2,1)S(1)} %get-tuple-element.37.hi_ref, bf16[256,256]{1,0:T(8,128)(2,1)S(1)} %get-tuple-element.38.lo_ref, bf16[512,2048]{1,0:T(8,128)(2,1)S(1)} %get-tuple-element.34.left_ref.raw_ref), custom_call_target="tpu_custom_call" | custom-call | flops 1000000 | bytes 100000 | tf_op jit(solution)/shard_map/left_basis/pallas_call | solution.py:354
  113.7 0.0 collective-permute-done.12.refs_3_
  113.7 2.7 %collective-permute-done.13.refs_1_ = f32[256,896]{1,0:T(8,128)S(1)} collective-permute-done((f32[256,896]{1,0:T(8,128)S(1)}, f32[256,896]{1,0:T(8,128)S(1)}, u32[]{:S(2)}, u32[]{:S(2)}) %collective-permute-start.13) | collective-permute-done | bytes 917536 | tf_op jit(solution)/shard_map/ppermute | solution.py:486
  116.4 1.7 %right_rotate.1 = (f32[1792,256]{1,0:T(8,128)S(1)}, bf16[768,1792]{1,0:T(8,128)(2,1)S(1)}, f32[8,256]{1,0:T(8,128)S(1)}) custom-call(bf16[256,256]{1,0:T(8,128)(2,1)S(1)} %get-tuple-element.37.hi_ref, bf16[256,256]{1,0:T(8,128)(2,1)S(1)} %get-tuple-element.38.lo_ref, f32[256,896]{1,0:T(8,128)S(1)} %right_factor.3.refs_0_, ...), custom_call_target="tpu_custom_call" | custom-call | flops 704643072 | bytes 7340032 | tf_op jit(solution)/shard_map/right_rotate/pallas_call | solution.py:402
  118.1 0.0 collective-permute-start.14
  118.1 3.1 %momentum_update.4.refs_0_ = f32[2048,1792]{1,0:T(8,128)} custom-call(bf16[2048,1792]{1,0:T(8,128)(2,1)S(1)} %get-tuple-element.26.refs_0_.refs_1_.shi_ref, bf16[2048,1792]{1,0:T(8,128)(2,1)S(1)} %get-tuple-element.27.refs_1_.refs_2_.slo_ref, bf16[2048,768]{1,0:T(8,128)(2,1)S(1)} %get-tuple-element.41.left_ref, bf16[768,1792]{1,0:T(8,128)(2,1)S(1)} %get-tuple-element.43.terms_ref), custom_call_target="tpu_custom_call" | custom-call | flops 1409286144 | bytes 3670016 | tf_op jit(solution)/shard_map/momentum_update/pallas_call | solution.py:436
  121.2 0.0 collective-permute-done.14.b_ref
  121.3 1.5 %collective-permute-start.15 = (f32[8,256]{1,0:T(8,128)S(1)}, f32[8,256]{1,0:T(8,128)S(1)}, u32[]{:S(2)}, u32[]{:S(2)}) collective-permute-start(f32[8,256]{1,0:T(8,128)S(1)} %add_pieces.8.a_ref), channel_id=1, source_target_pairs={{0,2},{1,5},{2,0},{3,7},{4,6},{5,1},{6,4},{7,3},{8,10},{9,13},{10,... | collective-permute-start | bytes 24584 | tf_op jit(solution)/shard_map/ppermute | solution.py:486
  122.8 3.1 %momentum_update.5.refs_0_ = f32[2048,1792]{1,0:T(8,128)} custom-call(bf16[2048,1792]{1,0:T(8,128)(2,1)S(1)} %get-tuple-element.26.refs_0_.refs_1_.shi_ref, bf16[2048,1792]{1,0:T(8,128)(2,1)S(1)} %get-tuple-element.27.refs_1_.refs_2_.slo_ref, bf16[2048,768]{1,0:T(8,128)(2,1)S(1)} %get-tuple-element.41.left_ref, ...), custom_call_target="tpu_custom_call", output_to_operand_aliasing={{}: (4, {})} | custom-call | flops 1409286144 | bytes 3670016 | tf_op jit(solution)/shard_map/momentum_update/pallas_call | solution.py:436
  125.9 0.0 collective-permute-done.15.b_ref
  125.9 2.0 %collective-permute-start.16 = (f32[8,256]{1,0:T(8,128)S(1)}, f32[8,256]{1,0:T(8,128)S(1)}, u32[]{:S(2)}, u32[]{:S(2)}) collective-permute-start(f32[8,256]{1,0:T(8,128)S(1)} %add_pieces.9.a_ref), channel_id=1, source_target_pairs={{0,4},{1,3},{2,6},{3,1},{4,0},{5,7},{6,2},{7,5},{8,12},{9,11},{10,... | collective-permute-start | bytes 24584 | tf_op jit(solution)/shard_map/ppermute | solution.py:486
  127.9 3.1 %momentum_update.6.refs_0_ = f32[2048,1792]{1,0:T(8,128)} custom-call(bf16[2048,1792]{1,0:T(8,128)(2,1)S(1)} %get-tuple-element.26.refs_0_.refs_1_.shi_ref, bf16[2048,1792]{1,0:T(8,128)(2,1)S(1)} %get-tuple-element.27.refs_1_.refs_2_.slo_ref, bf16[2048,768]{1,0:T(8,128)(2,1)S(1)} %get-tuple-element.41.left_ref, ...), custom_call_target="tpu_custom_call", output_to_operand_aliasing={{}: (4, {})} | custom-call | flops 1409286144 | bytes 3670016 | tf_op jit(solution)/shard_map/momentum_update/pallas_call | solution.py:436
  131.0 0.0 collective-permute-done.16.b_ref
  131.0 2.8 %collective-permute-start.17 = (f32[8,256]{1,0:T(8,128)S(1)}, f32[8,256]{1,0:T(8,128)S(1)}, u32[]{:S(2)}, u32[]{:S(2)}) collective-permute-start(f32[8,256]{1,0:T(8,128)S(1)} %add_pieces.10.a_ref), channel_id=1, source_target_pairs={{0,12},{1,13},{2,14},{3,15},{4,8},{5,9},{6,10},{7,11},{8,4},{9,5},... | collective-permute-start | bytes 24584 | tf_op jit(solution)/shard_map/ppermute | solution.py:486
  133.8 3.1 %momentum_update.7 = f32[2048,1792]{1,0:T(8,128)} custom-call(bf16[2048,1792]{1,0:T(8,128)(2,1)S(1)} %get-tuple-element.26.refs_0_.refs_1_.shi_ref, bf16[2048,1792]{1,0:T(8,128)(2,1)S(1)} %get-tuple-element.27.refs_1_.refs_2_.slo_ref, bf16[2048,768]{1,0:T(8,128)(2,1)S(1)} %get-tuple-element.41.left_ref, ...), custom_call_target="tpu_custom_call", output_to_operand_aliasing={{}: (4, {})} | custom-call | flops 1409286144 | bytes 3670016 | tf_op jit(solution)/shard_map/momentum_update/pallas_call | solution.py:436
  137.0 0.0 collective-permute-done.17.b_ref
  137.0 7.9 %update_basis.1 = (bf16[2048,1792]{1,0:T(8,128)(2,1)}, f32[1792,256]{1,0:T(8,128)}) custom-call(f32[1792,256]{1,0:T(8,128)S(1)} %get-tuple-element.44.turned_ref, f32[8,256]{1,0:T(8,128)S(1)} %add_pieces.11.squares_ref, f32[2048,256]{1,0:T(8,128)S(1)} %get-tuple-element.46.left_ref, bf16[768,1792]{1,0:T(8,128)(2,1)S(1)} %get-tuple-element.43.terms_ref), custom_call_target="tpu_custom_call" | custom-call | flops 5637144576 | bytes 7340032 | tf_op jit(solution)/shard_map/update_basis/pallas_call | solution.py:467
  (11 shorter events, 0.1 us)
Async XLA Ops:
  16.2 2.8 %collective-permute-start = (f32[128,2048]{1,0:T(8,128)S(1)}, f32[128,2048]{1,0:T(8,128)S(1)}, u32[]{:S(2)}, u32[]{:S(2)}) collective-permute-start(f32[128,2048]{1,0:T(8,128)S(1)} %get-tuple-element.29), channel_id=1, source_target_pairs={{0,1},{1,0},{2,3},{3,2},{4,5},{5,4},{6,7},{7,6},{8,9},{9,8},{10,11... | collective-permute-start | bytes 3145736 | tf_op jit(solution)/shard_map/ppermute | solution.py:486
  19.1 10.1 %collective-permute-start.1 = (f32[64,2048]{1,0:T(8,128)S(1)}, f32[64,2048]{1,0:T(8,128)S(1)}, u32[]{:S(2)}, u32[]{:S(2)}) collective-permute-start(f32[64,2048]{1,0:T(8,128)S(1)} %get-tuple-element.31), channel_id=1, source_target_pairs={{0,2},{1,5},{2,0},{3,7},{4,6},{5,1},{6,4},{7,3},{8,10},{9,13},{10,... | collective-permute-start | bytes 1572872 | tf_op jit(solution)/shard_map/ppermute | solution.py:486
  29.3 6.5 %collective-permute-start.2 = (f32[32,2048]{1,0:T(8,128)S(1)}, f32[32,2048]{1,0:T(8,128)S(1)}, u32[]{:S(2)}, u32[]{:S(2)}) collective-permute-start(f32[32,2048]{1,0:T(8,128)S(1)} %get-tuple-element.33), channel_id=1, source_target_pairs={{0,4},{1,3},{2,6},{3,1},{4,0},{5,7},{6,2},{7,5},{8,12},{9,11},{10,... | collective-permute-start | bytes 786440 | tf_op jit(solution)/shard_map/ppermute | solution.py:486
  35.8 9.1 %collective-permute-start.3 = (f32[32,2048]{1,0:T(8,128)S(1)}, f32[32,2048]{1,0:T(8,128)S(1)}, u32[]{:S(2)}, u32[]{:S(2)}) collective-permute-start(f32[32,2048]{1,0:T(8,128)S(1)} %add_pieces.6.a_ref), channel_id=1, source_target_pairs={{0,12},{1,13},{2,14},{3,15},{4,8},{5,9},{6,10},{7,11},{8,4},{9,5},... | collective-permute-start | bytes 786440 | tf_op jit(solution)/shard_map/ppermute | solution.py:486
  44.9 9.6 %collective-permute-start.4 = (f32[32,2048]{1,0:T(8,128)S(1)}, f32[32,2048]{1,0:T(8,128)S(1)}, u32[]{:S(2)}, u32[]{:S(2)}) collective-permute-start(f32[32,2048]{1,0:T(8,128)S(1)} %add_pieces.7.a_ref), channel_id=1, source_target_pairs={{0,4},{1,3},{2,6},{3,1},{4,0},{5,7},{6,2},{7,5},{8,12},{9,11},{10,... | collective-permute-start | bytes 786440 | tf_op jit(solution)/shard_map/ppermute | solution.py:486
  54.6 9.4 %copy-start.1 = (s32[384]{0:T(512)S(1)}, s32[384]{0:T(512)}, u32[]{:S(2)}) copy-start(s32[384]{0:T(512)} %param.9) | copy-start | bytes 4612
  54.6 9.4 %copy-start = (s32[4096]{0:T(1024)S(1)}, s32[4096]{0:T(1024)}, u32[]{:S(2)}) copy-start(s32[4096]{0:T(1024)} %param.8) | copy-start | bytes 49156
  54.6 9.2 %collective-permute-start.5 = (f32[64,2048]{1,0:T(8,128)S(1)}, f32[64,2048]{1,0:T(8,128)S(1)}, u32[]{:S(2)}, u32[]{:S(2)}) collective-permute-start(f32[64,2048]{1,0:T(8,128)S(1)} %join_pieces.5.a_ref), channel_id=1, source_target_pairs={{0,2},{1,5},{2,0},{3,7},{4,6},{5,1},{6,4},{7,3},{8,10},{9,13},{10,... | collective-permute-start | bytes 1572872 | tf_op jit(solution)/shard_map/ppermute | solution.py:486
  64.0 2.7 %collective-permute-start.6 = (f32[128,2048]{1,0:T(8,128)S(1)}, f32[128,2048]{1,0:T(8,128)S(1)}, u32[]{:S(2)}, u32[]{:S(2)}) collective-permute-start(f32[128,2048]{1,0:T(8,128)S(1)} %join_pieces.6.refs_0_.a_ref), channel_id=1, source_target_pairs={{0,1},{1,0},{2,3},{3,2},{4,5},{5,4},{6,7},{7,6},{8,9},{9,8},{10,11... | collective-permute-start | bytes 3145736 | tf_op jit(solution)/shard_map/ppermute | solution.py:486
  67.9 3.9 %collective-permute-start.7 = (f32[24,256]{1,0:T(8,128)S(1)}, f32[24,256]{1,0:T(8,128)S(1)}, u32[]{:S(2)}, u32[]{:S(2)}) collective-permute-start(f32[24,256]{1,0:T(8,128)S(1)} %get-tuple-element.35.refs_0_), channel_id=1, source_target_pairs={{0,16},{16,0},{1,17},{17,1},{2,18},{18,2},{3,19},{19,3},{4,20},{20... | collective-permute-start | bytes 73736 | tf_op jit(solution)/shard_map/ppermute | solution.py:486
  75.4 38.2 %collective-permute-start.12 = (f32[256,896]{1,0:T(8,128)S(1)}, f32[256,896]{1,0:T(8,128)S(1)}, u32[]{:S(2)}, u32[]{:S(2)}) collective-permute-start(f32[256,896]{1,0:T(8,128)S(1)} %get-tuple-element.40.refs_2_), channel_id=1, source_target_pairs={{0,16},{16,0},{1,17},{17,1},{2,18},{18,2},{3,19},{19,3},{4,20},{20... | collective-permute-start | bytes 2752520 | tf_op jit(solution)/shard_map/ppermute | solution.py:486
  80.5 35.9 %collective-permute-start.13 = (f32[256,896]{1,0:T(8,128)S(1)}, f32[256,896]{1,0:T(8,128)S(1)}, u32[]{:S(2)}, u32[]{:S(2)}) collective-permute-start(f32[256,896]{1,0:T(8,128)S(1)} %right_factor.3.refs_0_), channel_id=1, source_target_pairs={{0,16},{16,0},{1,17},{17,1},{2,18},{18,2},{3,19},{19,3},{4,20},{20... | collective-permute-start | bytes 2752520 | tf_op jit(solution)/shard_map/ppermute | solution.py:486
  81.1 5.6 %collective-permute-start.8 = (f32[24,256]{1,0:T(8,128)S(1)}, f32[24,256]{1,0:T(8,128)S(1)}, u32[]{:S(2)}, u32[]{:S(2)}) collective-permute-start(f32[24,256]{1,0:T(8,128)S(1)} %get-tuple-element.36.a_ref), channel_id=1, source_target_pairs={{0,12},{1,13},{2,14},{3,15},{4,8},{5,9},{6,10},{7,11},{8,4},{9,5},... | collective-permute-start | bytes 73736 | tf_op jit(solution)/shard_map/ppermute | solution.py:486
  86.7 4.6 %collective-permute-start.9 = (f32[48,256]{1,0:T(8,128)S(1)}, f32[48,256]{1,0:T(8,128)S(1)}, u32[]{:S(2)}, u32[]{:S(2)}) collective-permute-start(f32[48,256]{1,0:T(8,128)S(1)} %join_pieces.7.a_ref), channel_id=1, source_target_pairs={{0,4},{1,3},{2,6},{3,1},{4,0},{5,7},{6,2},{7,5},{8,12},{9,11},{10,... | collective-permute-start | bytes 147464 | tf_op jit(solution)/shard_map/ppermute | solution.py:486
  91.3 4.7 %collective-permute-start.10 = (f32[96,256]{1,0:T(8,128)S(1)}, f32[96,256]{1,0:T(8,128)S(1)}, u32[]{:S(2)}, u32[]{:S(2)}) collective-permute-start(f32[96,256]{1,0:T(8,128)S(1)} %join_pieces.8.a_ref), channel_id=1, source_target_pairs={{0,2},{1,5},{2,0},{3,7},{4,6},{5,1},{6,4},{7,3},{8,10},{9,13},{10,... | collective-permute-start | bytes 294920 | tf_op jit(solution)/shard_map/ppermute | solution.py:486
  96.0 1.5 %collective-permute-start.11 = (f32[192,256]{1,0:T(8,128)S(1)}, f32[192,256]{1,0:T(8,128)S(1)}, u32[]{:S(2)}, u32[]{:S(2)}) collective-permute-start(f32[192,256]{1,0:T(8,128)S(1)} %join_pieces.9.a_ref), channel_id=1, source_target_pairs={{0,1},{1,0},{2,3},{3,2},{4,5},{5,4},{6,7},{7,6},{8,9},{9,8},{10,11... | collective-permute-start | bytes 589832 | tf_op jit(solution)/shard_map/ppermute | solution.py:486
  118.1 3.2 %collective-permute-start.14 = (f32[8,256]{1,0:T(8,128)S(1)}, f32[8,256]{1,0:T(8,128)S(1)}, u32[]{:S(2)}, u32[]{:S(2)}) collective-permute-start(f32[8,256]{1,0:T(8,128)S(1)} %get-tuple-element.45.a_ref), channel_id=1, source_target_pairs={{0,1},{1,0},{2,3},{3,2},{4,5},{5,4},{6,7},{7,6},{8,9},{9,8},{10,11... | collective-permute-start | bytes 24584 | tf_op jit(solution)/shard_map/ppermute | solution.py:486
  121.3 4.6 %collective-permute-start.15 = (f32[8,256]{1,0:T(8,128)S(1)}, f32[8,256]{1,0:T(8,128)S(1)}, u32[]{:S(2)}, u32[]{:S(2)}) collective-permute-start(f32[8,256]{1,0:T(8,128)S(1)} %add_pieces.8.a_ref), channel_id=1, source_target_pairs={{0,2},{1,5},{2,0},{3,7},{4,6},{5,1},{6,4},{7,3},{8,10},{9,13},{10,... | collective-permute-start | bytes 24584 | tf_op jit(solution)/shard_map/ppermute | solution.py:486
  125.9 5.1 %collective-permute-start.16 = (f32[8,256]{1,0:T(8,128)S(1)}, f32[8,256]{1,0:T(8,128)S(1)}, u32[]{:S(2)}, u32[]{:S(2)}) collective-permute-start(f32[8,256]{1,0:T(8,128)S(1)} %add_pieces.9.a_ref), channel_id=1, source_target_pairs={{0,4},{1,3},{2,6},{3,1},{4,0},{5,7},{6,2},{7,5},{8,12},{9,11},{10,... | collective-permute-start | bytes 24584 | tf_op jit(solution)/shard_map/ppermute | solution.py:486
  131.0 5.9 %collective-permute-start.17 = (f32[8,256]{1,0:T(8,128)S(1)}, f32[8,256]{1,0:T(8,128)S(1)}, u32[]{:S(2)}, u32[]{:S(2)}) collective-permute-start(f32[8,256]{1,0:T(8,128)S(1)} %add_pieces.10.a_ref), channel_id=1, source_target_pairs={{0,12},{1,13},{2,14},{3,15},{4,8},{5,9},{6,10},{7,11},{8,4},{9,5},... | collective-permute-start | bytes 24584 | tf_op jit(solution)/shard_map/ppermute | solution.py:486
